TPU v7x, 32 devices: a whole 2x2x4 slice. The times are simulated.
32 devices in a mesh: mp: 4 (over x, core), ctx: 8 (over z, y).
Axes of the slice: x: 2, y: 2, z: 4, core: 2. Of those that a mesh axis runs over, the one named last changes fastest.
Arguments:
- queries: bfloat16 [32768, 1024], P(('mp', 'ctx')), parts along dimension 0, may hold values from -6 to 6
- key_rows: bfloat16 [32768, 1024], P(('mp', 'ctx')), parts along dimension 0, may hold values from -6 to 6
- value_rows: bfloat16 [32768, 1024], P(('mp', 'ctx')), parts along dimension 0, may hold values from -6 to 6
- conv_weight: float32 [12, 4, 1024], P('mp'), parts along dimension 0, may hold values from -3 to 3
- head_gain: float32 [4096], P('mp'), parts along dimension 0, may hold values from 0.1 to 1.9
Outputs:
- attended: bfloat16 [32768, 1024], P(('mp', 'ctx')), parts along dimension 0
There are 4 independent parts, one for each index of `mp`. A program takes and returns all parts, laid end to end along the dimension named above; each array names one. Nothing has to cross between parts.
All inputs are finite; a program needn't handle non-finite values.
Results may differ from a plain program's by a relative error of at most 0.006.
Values may be sent and summed in bfloat16 or wider, within the bound.
No kernel may reach another device: no remote copies, remote signals or barrier semaphores. Data moves between devices by JAX's collectives and lax.ppermute only.
A program may use at most 128 MiB of HBM per device.

v0:
```python
import jax
import jax.numpy as jnp
from jax import lax
from jax.sharding import PartitionSpec as P

HDIM = 128
CONV = 4


def passed_along(value, axis, steps):
    count = lax.axis_size(axis)
    initial, last = (max(0, -steps), min(count, count - steps))
    return lax.ppermute(value, axis, [(source, source + steps) for source in range(initial, last)])


def causal_conv(rows, earlier, taps):
    tokens_here = rows.shape[0]
    padded = jnp.concatenate([earlier.astype(jnp.float32), rows.astype(jnp.float32)], axis=0)
    total = jnp.zeros((tokens_here, rows.shape[1]), jnp.float32)
    for tap in range(CONV):
        total = total + taps[tap][None, :] * padded[tap : tap + tokens_here]
    return total


def body(queries, key_rows, value_rows, conv_weight, head_gain):
    tokens_here = queries.shape[0]
    heads_n = head_gain.shape[0] // HDIM
    tails = jnp.stack(
        [
            queries[tokens_here - CONV + 1 :],
            key_rows[tokens_here - CONV + 1 :],
            value_rows[tokens_here - CONV + 1 :],
        ]
    )
    earlier = passed_along(tails, "ctx", 1)
    query_f = (
        jax.nn.silu(causal_conv(queries, earlier[0], conv_weight[0])) * HDIM ** (-0.5)
    ).astype(jnp.bfloat16)
    key_f = jax.nn.silu(causal_conv(key_rows, earlier[1], conv_weight[1])).astype(jnp.bfloat16)
    value_f = causal_conv(value_rows, earlier[2], conv_weight[2]).astype(jnp.bfloat16)
    query_h = query_f.reshape(tokens_here, heads_n, HDIM)
    key_h = key_f.reshape(tokens_here, heads_n, HDIM)
    value_h = value_f.reshape(tokens_here, heads_n, HDIM)
    local = jnp.einsum("shd,she->hde", key_h, value_h, preferred_element_type=jnp.float32)
    zeros_state = jnp.zeros_like(local)

    def relay_turn(turn_index, carry):
        incoming = passed_along(carry[1], "ctx", 1)
        return (incoming, incoming + local)

    prefix_sum, passed_on = lax.fori_loop(
        0, lax.axis_size("ctx") - 1, relay_turn, (zeros_state, local)
    )
    causal = jnp.arange(tokens_here)[:, None] >= jnp.arange(tokens_here)[None, :]
    scores = jnp.einsum("thd,shd->hts", query_h, key_h, preferred_element_type=jnp.float32)
    scores = jnp.where(causal[None], scores, 0.0).astype(jnp.bfloat16)
    inner = jnp.einsum("hts,she->the", scores, value_h, preferred_element_type=jnp.float32)
    cross = jnp.einsum(
        "thd,hde->the", query_h, prefix_sum.astype(jnp.bfloat16), preferred_element_type=jnp.float32
    )
    outputs = inner + cross
    scale_inv = lax.rsqrt(jnp.mean(outputs * outputs, axis=2, keepdims=True) + 1e-06)
    normed = outputs * scale_inv * head_gain.reshape(heads_n, HDIM)[None]
    return normed.reshape(tokens_here, heads_n * HDIM).astype(jnp.bfloat16)


def solution(mesh):
    return jax.shard_map(
        body,
        mesh=mesh,
        in_specs=(
            P(("mp", "ctx"), None),
            P(("mp", "ctx"), None),
            P(("mp", "ctx"), None),
            P("mp", None, None),
            P("mp"),
        ),
        out_specs=P(("mp", "ctx"), None),
        check_vma=False,
    )
```

profile of v0, /device:TPU:0, one launch (start us, length us, event | category | flops | bytes accessed | tf_op | source)
XLA Modules:
  0.0 161.8 jit_solution(9788405244350440410)
XLA Ops:
  1.7 4.9 %collective-permute-start.1 = (bf16[3,3,1024]{2,1,0:T(4,128)(2,1)S(1)}, bf16[3,3,1024]{2,1,0:T(4,128)(2,1)S(1)}, u32[]{:S(2)}, u32[]{:S(2)}) collective-permute-start(bf16[3,3,1024]{2,1,0:T(4,128)(2,1)S(1)} %pad_maximum_fusion.3), channel_id=1, source_target_pairs={{0,1},{1,2},{2,3},{3,4},{4,5},{5,6},{6,7},{8,9},{9,10},{10,11},{11... | collective-permute-start | bytes 55304 | tf_op jit(solution)/shard_map/ppermute | solution.py:13
  6.5 1.0 fusion.51
  7.5 1.4 iota_compare_fusion
  8.9 4.0 %convert_element_type.58 = f32[1024,1024]{1,0:T(8,128)} convert(bf16[1024,1024]{1,0:T(8,128)(2,1)} %param.8) | non-fusion elementwise | flops 1048576 | bytes 6291456 | tf_op jit(solution)/shard_map/convert_element_type | solution.py:18
  12.9 2.4 %convert_element_type.54 = f32[1024,1024]{1,0:T(8,128)} convert(bf16[1024,1024]{1,0:T(8,128)(2,1)S(1)} %copy-done.2) | non-fusion elementwise | flops 1048576 | bytes 6291456 | tf_op jit(solution)/shard_map/convert_element_type | solution.py:18
  15.4 2.4 %convert_element_type.50 = f32[1024,1024]{1,0:T(8,128)} convert(bf16[1024,1024]{1,0:T(8,128)(2,1)S(1)} %copy-done.3) | non-fusion elementwise | flops 1048576 | bytes 6291456 | tf_op jit(solution)/shard_map/convert_element_type | solution.py:18
  17.8 7.5 %multiply_convert_fusion = bf16[1024,1024]{1,0:T(8,128)(2,1)S(1)} fusion(f32[1024,1024]{1,0:T(8,128)} %convert_element_type.58, f32[3,1024]{1,0:T(4,128)S(1)} %get-tuple-element.48, f32[1024]{0:T(1024)S(1)} %bitcast.77, f32[1024]{0:T(1024)S(1)} %bitcast.78, f32[1024]{0:T(1024)S(1)} %bitcast.75, f32[1024]{0:T(1024)S(1)} %bitcast.76), kind=kLoop, calls=%fused_computation.44 | loop fusion | flops 15728640 | bytes 6320128 | tf_op jit(solution)/shard_map/convert_element_type | solution.py:39
  25.3 2.6 %copy.13 = bf16[1024,1024]{0,1:T(8,128)(2,1)} copy(bf16[1024,1024]{1,0:T(8,128)(2,1)S(1)} %multiply_convert_fusion) | data formatting | bytes 4194304 | tf_op jit(solution)/shard_map/reshape | solution.py:42
  27.9 7.5 %fusion.39 = bf16[128,8,8,128]{3,2,1,0:T(8,128)(2,1)S(1)} fusion(f32[1024,1024]{1,0:T(8,128)} %convert_element_type.50, f32[1024]{0:T(1024)S(1)} %bitcast.72, f32[3,1024]{1,0:T(4,128)S(1)} %get-tuple-element.47, f32[1024]{0:T(1024)S(1)} %bitcast.73, f32[1024]{0:T(1024)S(1)} %bitcast.74, f32[1024]{0:T(1024)S(1)} %bitcast.71), kind=kLoop, calls=%fused_computation.53 | loop fusion | flops 11534336 | bytes 6320128
  37.0 1.5 copy-done.1
  38.6 2.8 %fusion.40 = bf16[128,8,8,128]{3,2,1,0:T(8,128)(2,1)S(1)} fusion(f32[1024,1024]{1,0:T(8,128)S(1)} %copy-done.1, f32[1024]{0:T(1024)S(1)} %bitcast.67, f32[3,1024]{1,0:T(4,128)S(1)} %get-tuple-element.49, f32[1024]{0:T(1024)S(1)} %bitcast.68, f32[1024]{0:T(1024)S(1)} %bitcast.69, f32[1024]{0:T(1024)S(1)} %bitcast.70), kind=kLoop, calls=%fused_computation.54 | loop fusion | flops 16777216 | bytes 6320128
  41.4 13.4 %fusion = f32[8,128,1024]{2,1,0:T(8,128)} fusion(pred[1024,1024]{1,0:T(8,128)(4,1)} %iota_compare_fusion, bf16[1024,8,128]{0,2,1:T(8,128)(2,1)} %bitcast.65, bf16[128,8,8,128]{3,2,1,0:T(8,128)(2,1)S(1)} %fusion.40, bf16[128,8,8,128]{3,2,1,0:T(8,128)(2,1)} %copy-done.4), kind=kOutput, calls=%fused_computation.1 | convolution fusion | flops 4311744512 | bytes 11534336 | tf_op jit(solution)/shard_map/hts,she->the/dot_general | solution.py:57
  54.8 100.6 %while.12 = (s32[]{:T(128)}, f32[8,128,128]{2,1,0:T(8,128)}, f32[8,128,128]{2,1,0:T(8,128)}, f32[8,128,128]{2,1,0:T(8,128)S(1)}, s32[]{:T(128)}) while((s32[]{:T(128)}, f32[8,128,128]{2,1,0:T(8,128)}, f32[8,128,128]{2,1,0:T(8,128)}, f32[8,128,128]{2,1,0:T(8,128)S(1)}, s32[]{:T(128)}) %tuple.33), condition=%wide.region_1.2_spmd, body=%wide.region_0.1_spmd.sunk | while | flops 131074 | bytes 5767297 | solution.py:51
  54.8 3.5 %collective-permute-start = (f32[8,128,128]{2,1,0:T(8,128)}, f32[8,128,128]{2,1,0:T(8,128)S(1)}, u32[]{:S(2)}, u32[]{:S(2)}) collective-permute-start(f32[8,128,128]{2,1,0:T(8,128)} %get-tuple-element.84), channel_id=1, source_target_pairs={{0,1},{1,2},{2,3},{3,4},{4,5},{5,6},{6,7},{8,9},{9,10},{10,11},{11... | collective-permute-start | bytes 1572872 | tf_op jit(solution)/shard_map/while/body/eval_jaxpr/ppermute | solution.py:13
  58.2 11.2 %collective-permute-done = f32[8,128,128]{2,1,0:T(8,128)S(1)} collective-permute-done((f32[8,128,128]{2,1,0:T(8,128)}, f32[8,128,128]{2,1,0:T(8,128)S(1)}, u32[]{:S(2)}, u32[]{:S(2)}) %collective-permute-start) | collective-permute-done | bytes 524320 | tf_op jit(solution)/shard_map/while/body/eval_jaxpr/ppermute | solution.py:13
  69.4 0.9 add.139
  70.4 4.3 %collective-permute-start = (f32[8,128,128]{2,1,0:T(8,128)}, f32[8,128,128]{2,1,0:T(8,128)S(1)}, u32[]{:S(2)}, u32[]{:S(2)}) collective-permute-start(f32[8,128,128]{2,1,0:T(8,128)} %get-tuple-element.84), channel_id=1, source_target_pairs={{0,1},{1,2},{2,3},{3,4},{4,5},{5,6},{6,7},{8,9},{9,10},{10,11},{11... | collective-permute-start | bytes 1572872 | tf_op jit(solution)/shard_map/while/body/eval_jaxpr/ppermute | solution.py:13
  74.7 10.3 %collective-permute-done = f32[8,128,128]{2,1,0:T(8,128)S(1)} collective-permute-done((f32[8,128,128]{2,1,0:T(8,128)}, f32[8,128,128]{2,1,0:T(8,128)S(1)}, u32[]{:S(2)}, u32[]{:S(2)}) %collective-permute-start) | collective-permute-done | bytes 524320 | tf_op jit(solution)/shard_map/while/body/eval_jaxpr/ppermute | solution.py:13
  85.0 0.9 add.139
  86.0 4.3 %collective-permute-start = (f32[8,128,128]{2,1,0:T(8,128)}, f32[8,128,128]{2,1,0:T(8,128)S(1)}, u32[]{:S(2)}, u32[]{:S(2)}) collective-permute-start(f32[8,128,128]{2,1,0:T(8,128)} %get-tuple-element.84), channel_id=1, source_target_pairs={{0,1},{1,2},{2,3},{3,4},{4,5},{5,6},{6,7},{8,9},{9,10},{10,11},{11... | collective-permute-start | bytes 1572872 | tf_op jit(solution)/shard_map/while/body/eval_jaxpr/ppermute | solution.py:13
  90.3 9.3 %collective-permute-done = f32[8,128,128]{2,1,0:T(8,128)S(1)} collective-permute-done((f32[8,128,128]{2,1,0:T(8,128)}, f32[8,128,128]{2,1,0:T(8,128)S(1)}, u32[]{:S(2)}, u32[]{:S(2)}) %collective-permute-start) | collective-permute-done | bytes 524320 | tf_op jit(solution)/shard_map/while/body/eval_jaxpr/ppermute | solution.py:13
  99.7 0.9 add.139
  100.7 5.2 %collective-permute-start = (f32[8,128,128]{2,1,0:T(8,128)}, f32[8,128,128]{2,1,0:T(8,128)S(1)}, u32[]{:S(2)}, u32[]{:S(2)}) collective-permute-start(f32[8,128,128]{2,1,0:T(8,128)} %get-tuple-element.84), channel_id=1, source_target_pairs={{0,1},{1,2},{2,3},{3,4},{4,5},{5,6},{6,7},{8,9},{9,10},{10,11},{11... | collective-permute-start | bytes 1572872 | tf_op jit(solution)/shard_map/while/body/eval_jaxpr/ppermute | solution.py:13
  105.9 8.4 %collective-permute-done = f32[8,128,128]{2,1,0:T(8,128)S(1)} collective-permute-done((f32[8,128,128]{2,1,0:T(8,128)}, f32[8,128,128]{2,1,0:T(8,128)S(1)}, u32[]{:S(2)}, u32[]{:S(2)}) %collective-permute-start) | collective-permute-done | bytes 524320 | tf_op jit(solution)/shard_map/while/body/eval_jaxpr/ppermute | solution.py:13
  115.3 5.2 %collective-permute-start = (f32[8,128,128]{2,1,0:T(8,128)}, f32[8,128,128]{2,1,0:T(8,128)S(1)}, u32[]{:S(2)}, u32[]{:S(2)}) collective-permute-start(f32[8,128,128]{2,1,0:T(8,128)} %get-tuple-element.84), channel_id=1, source_target_pairs={{0,1},{1,2},{2,3},{3,4},{4,5},{5,6},{6,7},{8,9},{9,10},{10,11},{11... | collective-permute-start | bytes 1572872 | tf_op jit(solution)/shard_map/while/body/eval_jaxpr/ppermute | solution.py:13
  120.5 7.5 %collective-permute-done = f32[8,128,128]{2,1,0:T(8,128)S(1)} collective-permute-done((f32[8,128,128]{2,1,0:T(8,128)}, f32[8,128,128]{2,1,0:T(8,128)S(1)}, u32[]{:S(2)}, u32[]{:S(2)}) %collective-permute-start) | collective-permute-done | bytes 524320 | tf_op jit(solution)/shard_map/while/body/eval_jaxpr/ppermute | solution.py:13
  129.0 5.2 %collective-permute-start = (f32[8,128,128]{2,1,0:T(8,128)}, f32[8,128,128]{2,1,0:T(8,128)S(1)}, u32[]{:S(2)}, u32[]{:S(2)}) collective-permute-start(f32[8,128,128]{2,1,0:T(8,128)} %get-tuple-element.84), channel_id=1, source_target_pairs={{0,1},{1,2},{2,3},{3,4},{4,5},{5,6},{6,7},{8,9},{9,10},{10,11},{11... | collective-permute-start | bytes 1572872 | tf_op jit(solution)/shard_map/while/body/eval_jaxpr/ppermute | solution.py:13
  134.2 7.0 %collective-permute-done = f32[8,128,128]{2,1,0:T(8,128)S(1)} collective-permute-done((f32[8,128,128]{2,1,0:T(8,128)}, f32[8,128,128]{2,1,0:T(8,128)S(1)}, u32[]{:S(2)}, u32[]{:S(2)}) %collective-permute-start) | collective-permute-done | bytes 524320 | tf_op jit(solution)/shard_map/while/body/eval_jaxpr/ppermute | solution.py:13
  142.2 5.2 %collective-permute-start = (f32[8,128,128]{2,1,0:T(8,128)}, f32[8,128,128]{2,1,0:T(8,128)S(1)}, u32[]{:S(2)}, u32[]{:S(2)}) collective-permute-start(f32[8,128,128]{2,1,0:T(8,128)} %get-tuple-element.84), channel_id=1, source_target_pairs={{0,1},{1,2},{2,3},{3,4},{4,5},{5,6},{6,7},{8,9},{9,10},{10,11},{11... | collective-permute-start | bytes 1572872 | tf_op jit(solution)/shard_map/while/body/eval_jaxpr/ppermute | solution.py:13
  147.4 7.0 %collective-permute-done = f32[8,128,128]{2,1,0:T(8,128)S(1)} collective-permute-done((f32[8,128,128]{2,1,0:T(8,128)}, f32[8,128,128]{2,1,0:T(8,128)S(1)}, u32[]{:S(2)}, u32[]{:S(2)}) %collective-permute-start) | collective-permute-done | bytes 524320 | tf_op jit(solution)/shard_map/while/body/eval_jaxpr/ppermute | solution.py:13
  155.4 3.3 %fusion.30 = (f32[1024,8]{0,1:T(8,128)S(1)}, f32[8,128,1024]{2,1,0:T(8,128)S(1)}) fusion(f32[8,128,1024]{2,1,0:T(8,128)} %fusion, bf16[128,8,8,128]{3,2,1,0:T(8,128)(2,1)S(1)} %fusion.40, f32[8,128,128]{2,1,0:T(8,128)} %get-tuple-element.26), kind=kOutput, calls=%fused_computation.41 | convolution fusion | flops 271704064 | bytes 11042816 | tf_op jit(solution)/shard_map/thd,hde->the/dot_general | solution.py:58
  159.2 2.6 %copy.9 = bf16[1024,1024]{1,0:T(8,128)(2,1)} copy(bf16[1024,1024]{0,1:T(8,128)(2,1)S(1)} %bitcast.64) | data formatting | bytes 4194304 | tf_op jit(solution)/shard_map/convert_element_type | solution.py:64
  (39 shorter events, 8.0 us)
Async XLA Ops:
  0.0 12.9 %copy-start.2 = (bf16[1024,1024]{1,0:T(8,128)(2,1)S(1)}, bf16[1024,1024]{1,0:T(8,128)(2,1)}, u32[]{:S(2)}) copy-start(bf16[1024,1024]{1,0:T(8,128)(2,1)} %param.7) | copy-start | bytes 6291460
  1.7 16.1 %collective-permute-start.1 = (bf16[3,3,1024]{2,1,0:T(4,128)(2,1)S(1)}, bf16[3,3,1024]{2,1,0:T(4,128)(2,1)S(1)}, u32[]{:S(2)}, u32[]{:S(2)}) collective-permute-start(bf16[3,3,1024]{2,1,0:T(4,128)(2,1)S(1)} %pad_maximum_fusion.3), channel_id=1, source_target_pairs={{0,1},{1,2},{2,3},{3,4},{4,5},{5,6},{6,7},{8,9},{9,10},{10,11},{11... | collective-permute-start | bytes 55304 | tf_op jit(solution)/shard_map/ppermute | solution.py:13
  12.9 2.4 %copy-start.3 = (bf16[1024,1024]{1,0:T(8,128)(2,1)S(1)}, bf16[1024,1024]{1,0:T(8,128)(2,1)}, u32[]{:S(2)}) copy-start(bf16[1024,1024]{1,0:T(8,128)(2,1)} %param.9) | copy-start | bytes 6291460
  27.9 7.5 %copy-start.5 = (bf16[1024,1024]{0,1:T(8,128)(2,1)S(1)}, bf16[1024,1024]{0,1:T(8,128)(2,1)}, u32[]{:S(2)}) copy-start(bf16[1024,1024]{0,1:T(8,128)(2,1)} %copy.13) | copy-start | bytes 6291460
  35.4 1.6 %copy-start.4 = (bf16[128,8,8,128]{3,2,1,0:T(8,128)(2,1)}, bf16[128,8,8,128]{3,2,1,0:T(8,128)(2,1)S(1)}, u32[]{:S(2)}) copy-start(bf16[128,8,8,128]{3,2,1,0:T(8,128)(2,1)S(1)} %fusion.39) | copy-start | bytes 6291460
  35.4 3.1 %copy-start.1 = (f32[1024,1024]{1,0:T(8,128)S(1)}, f32[1024,1024]{1,0:T(8,128)}, u32[]{:S(2)}) copy-start(f32[1024,1024]{1,0:T(8,128)} %convert_element_type.54) | copy-start | bytes 12582916
  54.8 14.6 %collective-permute-start = (f32[8,128,128]{2,1,0:T(8,128)}, f32[8,128,128]{2,1,0:T(8,128)S(1)}, u32[]{:S(2)}, u32[]{:S(2)}) collective-permute-start(f32[8,128,128]{2,1,0:T(8,128)} %get-tuple-element.84), channel_id=1, source_target_pairs={{0,1},{1,2},{2,3},{3,4},{4,5},{5,6},{6,7},{8,9},{9,10},{10,11},{11... | collective-permute-start | bytes 1572872 | tf_op jit(solution)/shard_map/while/body/eval_jaxpr/ppermute | solution.py:13
  69.4 1.0 copy-start
  70.4 14.6 %collective-permute-start = (f32[8,128,128]{2,1,0:T(8,128)}, f32[8,128,128]{2,1,0:T(8,128)S(1)}, u32[]{:S(2)}, u32[]{:S(2)}) collective-permute-start(f32[8,128,128]{2,1,0:T(8,128)} %get-tuple-element.84), channel_id=1, source_target_pairs={{0,1},{1,2},{2,3},{3,4},{4,5},{5,6},{6,7},{8,9},{9,10},{10,11},{11... | collective-permute-start | bytes 1572872 | tf_op jit(solution)/shard_map/while/body/eval_jaxpr/ppermute | solution.py:13
  85.0 1.0 copy-start
  86.0 13.7 %collective-permute-start = (f32[8,128,128]{2,1,0:T(8,128)}, f32[8,128,128]{2,1,0:T(8,128)S(1)}, u32[]{:S(2)}, u32[]{:S(2)}) collective-permute-start(f32[8,128,128]{2,1,0:T(8,128)} %get-tuple-element.84), channel_id=1, source_target_pairs={{0,1},{1,2},{2,3},{3,4},{4,5},{5,6},{6,7},{8,9},{9,10},{10,11},{11... | collective-permute-start | bytes 1572872 | tf_op jit(solution)/shard_map/while/body/eval_jaxpr/ppermute | solution.py:13
  99.7 1.0 copy-start
  100.7 13.6 %collective-permute-start = (f32[8,128,128]{2,1,0:T(8,128)}, f32[8,128,128]{2,1,0:T(8,128)S(1)}, u32[]{:S(2)}, u32[]{:S(2)}) collective-permute-start(f32[8,128,128]{2,1,0:T(8,128)} %get-tuple-element.84), channel_id=1, source_target_pairs={{0,1},{1,2},{2,3},{3,4},{4,5},{5,6},{6,7},{8,9},{9,10},{10,11},{11... | collective-permute-start | bytes 1572872 | tf_op jit(solution)/shard_map/while/body/eval_jaxpr/ppermute | solution.py:13
  114.3 1.0 copy-start
  115.3 12.7 %collective-permute-start = (f32[8,128,128]{2,1,0:T(8,128)}, f32[8,128,128]{2,1,0:T(8,128)S(1)}, u32[]{:S(2)}, u32[]{:S(2)}) collective-permute-start(f32[8,128,128]{2,1,0:T(8,128)} %get-tuple-element.84), channel_id=1, source_target_pairs={{0,1},{1,2},{2,3},{3,4},{4,5},{5,6},{6,7},{8,9},{9,10},{10,11},{11... | collective-permute-start | bytes 1572872 | tf_op jit(solution)/shard_map/while/body/eval_jaxpr/ppermute | solution.py:13
  128.0 1.0 copy-start
  129.0 12.2 %collective-permute-start = (f32[8,128,128]{2,1,0:T(8,128)}, f32[8,128,128]{2,1,0:T(8,128)S(1)}, u32[]{:S(2)}, u32[]{:S(2)}) collective-permute-start(f32[8,128,128]{2,1,0:T(8,128)} %get-tuple-element.84), channel_id=1, source_target_pairs={{0,1},{1,2},{2,3},{3,4},{4,5},{5,6},{6,7},{8,9},{9,10},{10,11},{11... | collective-permute-start | bytes 1572872 | tf_op jit(solution)/shard_map/while/body/eval_jaxpr/ppermute | solution.py:13
  141.2 1.0 copy-start
  142.2 12.2 %collective-permute-start = (f32[8,128,128]{2,1,0:T(8,128)}, f32[8,128,128]{2,1,0:T(8,128)S(1)}, u32[]{:S(2)}, u32[]{:S(2)}) collective-permute-start(f32[8,128,128]{2,1,0:T(8,128)} %get-tuple-element.84), channel_id=1, source_target_pairs={{0,1},{1,2},{2,3},{3,4},{4,5},{5,6},{6,7},{8,9},{9,10},{10,11},{11... | collective-permute-start | bytes 1572872 | tf_op jit(solution)/shard_map/while/body/eval_jaxpr/ppermute | solution.py:13
  154.4 1.0 copy-start
  155.4 3.4 %copy-start.6 = (f32[1024]{0:T(1024)S(1)}, f32[1024]{0:T(1024)}, u32[]{:S(2)}) copy-start(f32[1024]{0:T(1024)} %param.11) | copy-start | bytes 12292
where the time goes:
time: 165 us; the launch traced here: 162 us
  waiting for transfers between devices  60.6 us (37%)
  starting transfers between devices  37.8 us (23%)
  other arithmetic  35.2 us (21%)
  matrix products  17.5 us (11%)
  local copies, waits for them, and re-layouts  10.6 us (6%)
    ppermute x8, waiting for transfers between devices, passed_along(): lax.ppermute(value, axis, [(source, source + steps) for source in range(i...  60.6 us
    ppermute x8, starting transfers between devices, passed_along(): lax.ppermute(value, axis, [(source, source + steps) for source in range(i...  37.8 us
    dot_general x1, matrix products, body(): jnp.einsum('hts,she->the', scores, value_h, preferred_element_type=jnp.fl...  13.4 us
    unnamed x2, other arithmetic  10.4 us
    convert_element_type x3, other arithmetic, causal_conv(): rows.astype(jnp.float32)  8.87 us
    convert_element_type x1, other arithmetic, body(): jax.nn.silu(causal_conv(key_rows, earlier[1], conv_weight[1]))  7.52 us
    add x7, other arithmetic, relay_turn(): return (incoming, incoming + local)  6.58 us
    dot_general x1, matrix products, body(): jnp.einsum('thd,hde->the', query_h, prefix_sum.astype(jnp.bfloat16), pref...  3.32 us
  transfers between devices with their start and end apart: 8, of which 7 were waited for; matrix products, arithmetic and copies ran while one was open for 7% of the time, Pallas kernels for 0%

commit v1 on v0

v1 whole, which is shorter than its diff:
```python
import functools

import jax
import jax.numpy as jnp
from jax import lax
from jax.experimental import pallas as pl
from jax.experimental.pallas import tpu as pltpu
from jax.sharding import PartitionSpec as P

HDIM = 128
CONV = 4
GROUP = 4
CHUNK = 128
AUX = 32
FIX = 16
HALF_SCALE = HDIM ** (-0.5)
F32, BF16 = jnp.float32, jnp.bfloat16


def rows_iota(shape):
    return lax.broadcasted_iota(jnp.int32, shape, 0)


def dot(a, b, dims):
    return lax.dot_general(a, b, (dims, ((), ())), preferred_element_type=F32)


def conv_chunk(x_ref, cols, start, taps):
    x = x_ref[start : start + CHUNK, cols].astype(F32)
    if start:
        earlier = x_ref[start - 16 : start, cols].astype(F32)[8:16]
    else:
        earlier = jnp.zeros((8, HDIM), F32)
    x = jnp.concatenate([earlier, x], axis=0)
    x1 = pltpu.roll(x, 1, 0)
    late = taps[3:4] * x + taps[2:3] * x1
    early = taps[1:2] * x + taps[0:1] * x1
    return (late + pltpu.roll(early, 2, 0))[8:]


def silu_of_twice(half):
    return half + half * jnp.tanh(half)


def merged_rows(first16, last16):
    first = first16.astype(F32)[0:8]
    last = last16.astype(F32)[8:16]
    return jnp.where(rows_iota((8, HDIM)) < 4, first, last)


def state_kernel(m_ref, q_first, q_last, k_ref, v_ref, w_ref, kf_ref, vf_ref, msg_ref):
    tokens = k_ref.shape[0]
    for h in range(k_ref.shape[1] // HDIM):
        cols = slice(h * HDIM, (h + 1) * HDIM)
        wk = w_ref[1, :, cols] * 0.5
        wv = w_ref[2, :, cols]
        for start in range(0, tokens, CHUNK):
            kf = silu_of_twice(conv_chunk(k_ref, cols, start, wk))
            if start == 0:
                kf = jnp.where(rows_iota(kf.shape) < CONV - 1, 0.0, kf)
            kf_ref[start : start + CHUNK, cols] = kf.astype(BF16)
            vf_ref[start : start + CHUNK, cols] = conv_chunk(v_ref, cols, start, wv).astype(BF16)
        local = dot(kf_ref[:, cols], vf_ref[:, cols], ((0,), (0,)))
        msg_ref[h, 0:HDIM] = local.astype(BF16)
        mk = merged_rows(k_ref[0:16, cols], k_ref[tokens - 16 : tokens, cols])
        mv = merged_rows(v_ref[0:16, cols], v_ref[tokens - 16 : tokens, cols])
        mq = merged_rows(q_first[:, cols], q_last[:, cols])
        msg_ref[h, HDIM : HDIM + 16] = jnp.concatenate([mk, mv], axis=0).astype(BF16)
        msg_ref[h, HDIM + 16 : HDIM + 32] = jnp.concatenate([mq, mq], axis=0).astype(BF16)


def block_states(m, queries, key_rows, value_rows, conv_weight):
    tokens, width = key_rows.shape
    quarter = width // GROUP
    heads = quarter // HDIM
    last = tokens // 16 - 1
    cols = lambda j, m: (0, j ^ m[0])
    return pl.pallas_call(
        state_kernel,
        grid_spec=pltpu.PrefetchScalarGridSpec(
            num_scalar_prefetch=1,
            grid=(GROUP,),
            in_specs=[
                pl.BlockSpec((16, quarter), cols),
                pl.BlockSpec((16, quarter), lambda j, m: (last, j ^ m[0])),
                pl.BlockSpec((tokens, quarter), cols),
                pl.BlockSpec((tokens, quarter), cols),
                pl.BlockSpec((3, CONV, quarter), lambda j, m: (0, 0, j ^ m[0])),
            ],
            out_specs=[
                pl.BlockSpec((tokens, quarter), cols),
                pl.BlockSpec((tokens, quarter), cols),
                pl.BlockSpec((heads, HDIM + AUX, HDIM), lambda j, m: (j, 0, 0)),
            ],
        ),
        out_shape=[
            jax.ShapeDtypeStruct((tokens, width), BF16),
            jax.ShapeDtypeStruct((tokens, width), BF16),
            jax.ShapeDtypeStruct((GROUP * heads, HDIM + AUX, HDIM), BF16),
        ],
        compiler_params=pltpu.CompilerParams(vmem_limit_bytes=16 << 20),
        cost_estimate=pl.CostEstimate(flops=2 * tokens * width * HDIM, bytes_accessed=8 * tokens * width, transcendentals=tokens * width),
        name="block_states",
    )(m, queries, queries, key_rows, value_rows, conv_weight)


def edge_rows(own, before, taps):
    z = pltpu.roll(jnp.where(rows_iota((8, HDIM)) < 4, own, before), 3, 0)
    y = taps[3:4] * z
    for back in range(1, CONV):
        y = y + taps[3 - back : 4 - back] * pltpu.roll(z, back, 0)
    return y


def edge_only(y):
    rows = rows_iota(y.shape)
    return jnp.where((rows >= 3) & (rows < 6), y, 0.0)


def edge_kv(own, before, w_ref, cols):
    kf = silu_of_twice(edge_rows(own[0:8], before[0:8], w_ref[1, :, cols] * 0.5))
    vf = edge_rows(own[8:16], before[8:16], w_ref[2, :, cols])
    return edge_only(kf), edge_only(vf)


def gather_packets(m_ref, packets, buf):
    for j, packet in enumerate(packets):
        buf[m_ref[0] ^ j] = packet[...]


def total_kernel(has_tail, m_ref, *refs):
    packets, refs = refs[:GROUP], refs[GROUP:]
    if has_tail:
        tail_ref, refs = refs[0], refs[1:]
    w_ref, out_ref, buf = refs
    gather_packets(m_ref, packets, buf)
    for h in range(out_ref.shape[0]):
        cols = slice(h * HDIM, (h + 1) * HDIM)
        before = tail_ref[h].astype(F32) if has_tail else jnp.zeros((AUX, HDIM), F32)
        kfs, vfs = [], []
        total = jnp.zeros((HDIM, HDIM), F32)
        for t in range(GROUP):
            own = buf[t, h, HDIM:].astype(F32)
            kf, vf = edge_kv(own, before, w_ref, cols)
            kfs.append(kf)
            vfs.append(vf)
            before = own
            total = total + buf[t, h, 0:HDIM].astype(F32)
        kf = jnp.concatenate(kfs, axis=0).astype(BF16)
        vf = jnp.concatenate(vfs, axis=0).astype(BF16)
        total = total + dot(kf, vf, ((0,), (0,)))
        out_ref[h, 0:HDIM] = total.astype(BF16)
        out_ref[h, HDIM:] = buf[GROUP - 1, h, HDIM:]


def packet_specs(heads, rows):
    return [pl.BlockSpec((heads, rows, HDIM), lambda i, m: (0, 0, 0))] * GROUP


def group_total(m, packets, tail, conv_weight):
    quarter = conv_weight.shape[2] // GROUP
    heads = quarter // HDIM
    tails = [] if tail is None else [tail]
    return pl.pallas_call(
        functools.partial(total_kernel, tail is not None),
        grid_spec=pltpu.PrefetchScalarGridSpec(
            num_scalar_prefetch=1,
            grid=(1,),
            in_specs=packet_specs(heads, HDIM + AUX)
            + [pl.BlockSpec((heads, AUX, HDIM), lambda i, m: (0, 0, 0))] * len(tails)
            + [pl.BlockSpec((3, CONV, quarter), lambda i, m: (0, 0, m[0]))],
            out_specs=pl.BlockSpec((heads, HDIM + AUX, HDIM), lambda i, m: (0, 0, 0)),
            scratch_shapes=[pltpu.VMEM((GROUP, heads, HDIM + AUX, HDIM), BF16)],
        ),
        out_shape=jax.ShapeDtypeStruct((heads, HDIM + AUX, HDIM), BF16),
        compiler_params=pltpu.CompilerParams(vmem_limit_bytes=8 << 20),
        name="group_total",
    )(m, *packets, *tails, conv_weight)


def prefix_kernel(m_ref, p0, p1, p2, p3, x_ref, w_ref, gain_ref, o0, o1, o2, o3, buf, out):
    gather_packets(m_ref, (p0, p1, p2, p3), buf)
    later = (m_ref[1] > 0).astype(F32)
    heads = x_ref.shape[0]
    for h in range(heads):
        cols = slice(h * HDIM, (h + 1) * HDIM)
        gain = gain_ref[:, cols]
        prefix = x_ref[h, 0:HDIM].astype(F32) * later
        before = x_ref[h, HDIM:].astype(F32) * later
        for t in range(GROUP):
            own = buf[t, h, HDIM:].astype(F32)
            kf, vf = edge_kv(own, before, w_ref, cols)
            qf = silu_of_twice(edge_rows(own[16:24], before[16:24], w_ref[0, :, cols] * 0.5)) * HALF_SCALE
            blank = jnp.zeros((8, HDIM), F32)
            kf = jnp.concatenate([kf, blank], axis=0).astype(BF16)
            vf = jnp.concatenate([vf, blank], axis=0).astype(BF16)
            qf = jnp.concatenate([edge_only(qf), blank], axis=0).astype(BF16)
            scores = dot(qf, kf, ((1,), (1,)))
            causal = rows_iota(scores.shape) >= lax.broadcasted_iota(jnp.int32, scores.shape, 1)
            scores = jnp.where(causal, scores, 0.0).astype(BF16)
            o = dot(scores, vf, ((1,), (0,))) + dot(qf, prefix.astype(BF16), ((1,), (0,)))
            o = o * lax.rsqrt(jnp.mean(o * o, axis=1, keepdims=True) + 1e-06) * gain
            shifted = prefix + dot(kf, vf, ((0,), (0,)))
            out[t, h, 0:HDIM] = shifted.astype(BF16)
            out[t, h, HDIM:] = jnp.concatenate([pltpu.roll(o[0:8], 5, 0), blank], axis=0).astype(BF16)
            prefix = shifted + buf[t, h, 0:HDIM].astype(F32)
            before = own
    for j, o_ref in enumerate((o0, o1, o2, o3)):
        o_ref[...] = out[m_ref[0] ^ j]


def member_prefixes(m, packets, incoming, conv_weight, gain):
    quarter = conv_weight.shape[2] // GROUP
    heads = quarter // HDIM
    out = jax.ShapeDtypeStruct((heads, HDIM + FIX, HDIM), BF16)
    return pl.pallas_call(
        prefix_kernel,
        grid_spec=pltpu.PrefetchScalarGridSpec(
            num_scalar_prefetch=1,
            grid=(1,),
            in_specs=packet_specs(heads, HDIM + AUX)
            + [
                pl.BlockSpec((heads, HDIM + AUX, HDIM), lambda i, m: (0, 0, 0)),
                pl.BlockSpec((3, CONV, quarter), lambda i, m: (0, 0, m[0])),
                pl.BlockSpec((1, quarter), lambda i, m: (0, m[0])),
            ],
            out_specs=packet_specs(heads, HDIM + FIX),
            scratch_shapes=[
                pltpu.VMEM((GROUP, heads, HDIM + AUX, HDIM), BF16),
                pltpu.VMEM((GROUP, heads, HDIM + FIX, HDIM), BF16),
            ],
        ),
        out_shape=[out] * GROUP,
        compiler_params=pltpu.CompilerParams(vmem_limit_bytes=8 << 20),
        name="member_prefixes",
    )(m, *packets, incoming, conv_weight, gain)


def inner_kernel(q_ref, kf_ref, vf_ref, w_ref, qf_ref, inner_ref):
    tokens = q_ref.shape[0]
    shape = (CHUNK, CHUNK)
    causal = rows_iota(shape) >= lax.broadcasted_iota(jnp.int32, shape, 1)
    for h in range(q_ref.shape[1] // HDIM):
        cols = slice(h * HDIM, (h + 1) * HDIM)
        wq = w_ref[0, :, cols] * 0.5
        state = None
        for start in range(0, tokens, CHUNK):
            rows = slice(start, start + CHUNK)
            qf = (silu_of_twice(conv_chunk(q_ref, cols, start, wq)) * HALF_SCALE).astype(BF16)
            qf_ref[rows, cols] = qf
            kf, vf = kf_ref[rows, cols], vf_ref[rows, cols]
            scores = jnp.where(causal, dot(qf, kf, ((1,), (1,))), 0.0).astype(BF16)
            if state is None:
                inner = dot(scores, vf, ((1,), (0,)))
                state = dot(kf, vf, ((0,), (0,)))
            else:
                left = jnp.concatenate([scores, qf], axis=1)
                right = jnp.concatenate([vf, state.astype(BF16)], axis=0)
                inner = dot(left, right, ((1,), (0,)))
                if start + CHUNK < tokens:
                    state = state + dot(kf, vf, ((0,), (0,)))
            inner_ref[rows, cols] = inner


def inner_attention(queries, kf, vf, conv_weight):
    tokens, width = queries.shape
    quarter = width // GROUP
    block = pl.BlockSpec((tokens, quarter), lambda j: (0, j))
    return pl.pallas_call(
        inner_kernel,
        grid=(GROUP,),
        in_specs=[block, block, block, pl.BlockSpec((3, CONV, quarter), lambda j: (0, 0, j))],
        out_specs=[block, block],
        out_shape=[
            jax.ShapeDtypeStruct((tokens, width), BF16),
            jax.ShapeDtypeStruct((tokens, width), F32),
        ],
        compiler_params=pltpu.CompilerParams(vmem_limit_bytes=16 << 20),
        cost_estimate=pl.CostEstimate(flops=8 * tokens * width * HDIM, bytes_accessed=12 * tokens * width, transcendentals=tokens * width),
        name="inner_attention",
    )(queries, kf, vf, conv_weight)


def finish_kernel(m_ref, p0, p1, p2, p3, qf_ref, inner_ref, gain_ref, out_ref, buf):
    step = pl.program_id(0)

    @pl.when(step == 0)
    def _():
        gather_packets(m_ref, (p0, p1, p2, p3), buf)

    heads = p0.shape[0]
    for index in range(GROUP * heads):
        t, h = index // heads, index % heads
        cols = slice(index * HDIM, (index + 1) * HDIM)
        o = inner_ref[:, cols] + dot(qf_ref[:, cols], buf[t, h, 0:HDIM], ((1,), (0,)))
        o = o * lax.rsqrt(jnp.mean(o * o, axis=1, keepdims=True) + 1e-06) * gain_ref[:, cols]
        out_ref[:, cols] = o.astype(BF16)

    @pl.when(step == 0)
    def _():
        for index in range(GROUP * heads):
            t, h = index // heads, index % heads
            cols = slice(index * HDIM, (index + 1) * HDIM)
            there = rows_iota((FIX, HDIM)) < CONV - 1
            fixed = buf[t, h, HDIM:].astype(F32)
            out_ref[0:FIX, cols] = jnp.where(there, fixed, out_ref[0:FIX, cols].astype(F32)).astype(BF16)


def finish(m, prefixes, qf, inner, gain):
    tokens, width = qf.shape
    heads = width // GROUP // HDIM
    rows = tokens // 4
    block = pl.BlockSpec((rows, width), lambda i, m: (i, 0))
    return pl.pallas_call(
        finish_kernel,
        grid_spec=pltpu.PrefetchScalarGridSpec(
            num_scalar_prefetch=1,
            grid=(tokens // rows,),
            in_specs=packet_specs(heads, HDIM + FIX)
            + [block, block, pl.BlockSpec((1, width), lambda i, m: (0, 0))],
            out_specs=block,
            scratch_shapes=[pltpu.VMEM((GROUP, heads, HDIM + FIX, HDIM), BF16)],
        ),
        out_shape=jax.ShapeDtypeStruct((tokens, width), BF16),
        compiler_params=pltpu.CompilerParams(vmem_limit_bytes=16 << 20),
        name="finish",
    )(m, *prefixes, qf, inner, gain)


def swapped(value, bits):
    count = lax.axis_size("ctx")
    return lax.ppermute(value, "ctx", [(s, s ^ bits) for s in range(count)])


def to_next_group(value):
    count = lax.axis_size("ctx")
    return lax.ppermute(value, "ctx", [(s, s + GROUP) for s in range(count - GROUP)])


def body(queries, key_rows, value_rows, conv_weight, head_gain):
    width = queries.shape[1]
    heads = width // GROUP // HDIM
    groups = lax.axis_size("ctx") // GROUP
    place = lax.axis_index("ctx")
    m = jnp.stack([place % GROUP, place // GROUP]).astype(jnp.int32)
    gain = head_gain.reshape(1, width)
    kf, vf, messages = block_states(m, queries, key_rows, value_rows, conv_weight)
    packets = [messages[0:heads]]
    packets += [swapped(messages[j * heads : (j + 1) * heads], j) for j in range(1, GROUP)]
    if groups == 2:
        incoming = swapped(group_total(m, packets, None, conv_weight), GROUP)
    else:
        last = jnp.stack(packets)[m[0] ^ (GROUP - 1)][:, HDIM:]
        tail = to_next_group(last)
        total = group_total(m, packets, tail, conv_weight)[:, 0:HDIM].astype(F32)
        prefix, passed = jnp.zeros_like(total), total
        for _ in range(groups - 1):
            prefix = to_next_group(passed)
            passed = prefix + total
        incoming = jnp.concatenate([prefix.astype(BF16), tail], axis=1)
    qf, inner = inner_attention(queries, kf, vf, conv_weight)
    sends = member_prefixes(m, packets, incoming, conv_weight, gain)
    prefixes = [sends[0]] + [swapped(sends[j], j) for j in range(1, GROUP)]
    return finish(m, prefixes, qf, inner, gain)


def solution(mesh):
    return jax.shard_map(
        body,
        mesh=mesh,
        in_specs=(
            P(("mp", "ctx"), None),
            P(("mp", "ctx"), None),
            P(("mp", "ctx"), None),
            P("mp", None, None),
            P("mp"),
        ),
        out_specs=P(("mp", "ctx"), None),
        check_vma=False,
    )
```

time: 165 us -> 49.2 us (0.30); the launches traced: 162 us -> 48.9 us
  waiting for transfers between devices: 60.6 us -> 7.04 us
  other arithmetic: 35.2 us -> 0.07 us
  starting transfers between devices: 37.8 us -> 11 us
  Pallas kernels: 0 us -> 25.1 us
  matrix products: 17.5 us -> 0 us
  local copies, waits for them, and re-layouts: 10.6 us -> 5.6 us
    ppermute x8 -> x7, waiting for transfers between devices: 60.6 us -> 7.04 us  [swapped(): return lax.ppermute(value, 'ctx', [(s, s ^ bits) for s in range(count)])]
    ppermute x8 -> x7, starting transfers between devices: 37.8 us -> 11 us  [swapped(): return lax.ppermute(value, 'ctx', [(s, s ^ bits) for s in range(count)])]
    pallas_call x0 -> x5, Pallas kernels: none -> 25.1 us  [the longest x1 11.7 us: inner_attention(): pl.pallas_call(inner_kernel, grid=(GROUP,), in_specs=[block, block, block...]
    dot_general x3 -> x0, matrix products: 17.5 us -> none  [the longest x1 13.4 us: body(): jnp.einsum('hts,she->the', scores, value_h, preferred_element_type=jnp.fl...]
    convert_element_type x6 -> x0, other arithmetic: 16.9 us -> none  [the longest x3 8.87 us: causal_conv(): rows.astype(jnp.float32)]
    unnamed x2 -> x0, other arithmetic: 10.4 us -> none
    add x7 -> x0, other arithmetic: 6.58 us -> none  [relay_turn(): return (incoming, incoming + local)]
    unnamed x13 -> x14, local copies, waits for them, and re-layouts: 2.36 us -> 5.58 us
  transfers between devices with their start and end apart: 8 -> 7, of which waited for: 7 -> 4; matrix products, arithmetic and copies ran while one was open for 7% -> 0% of each run, Pallas kernels for 0% -> 24%
where the time goes in v1:
time: 49.2 us; the launch traced here: 48.9 us
  Pallas kernels  25.1 us (51%)
  starting transfers between devices  11 us (22%)
  waiting for transfers between devices  7.04 us (14%)
  local copies, waits for them, and re-layouts  5.6 us (11%)
    pallas_call x1, Pallas kernels, inner_attention(): pl.pallas_call(inner_kernel, grid=(GROUP,), in_specs=[block, block, block...  11.7 us
    ppermute x7, starting transfers between devices, swapped(): return lax.ppermute(value, 'ctx', [(s, s ^ bits) for s in range(count)])  11 us
    pallas_call x1, Pallas kernels, block_states(): pl.pallas_call(state_kernel, grid_spec=pltpu.PrefetchScalarGridSpec(num_s...  7.71 us
    ppermute x7, waiting for transfers between devices, swapped(): return lax.ppermute(value, 'ctx', [(s, s ^ bits) for s in range(count)])  7.04 us
    unnamed x14, local copies, waits for them, and re-layouts  5.58 us
    pallas_call x1, Pallas kernels, finish(): pl.pallas_call(finish_kernel, grid_spec=pltpu.PrefetchScalarGridSpec(num_...  3.76 us
    pallas_call x1, Pallas kernels, member_prefixes(): pl.pallas_call(prefix_kernel, grid_spec=pltpu.PrefetchScalarGridSpec(num_...  1.15 us
  transfers between devices with their start and end apart: 7, of which 4 were waited for; matrix products, arithmetic and copies ran while one was open for 0% of the time, Pallas kernels for 24%

profile of v1, /device:TPU:0, one launch (start us, length us, event | category | flops | bytes accessed | tf_op | source)
XLA Modules:
  0.0 48.9 jit_solution(10360002289873063919)
XLA Ops:
  0.0 0.1 pad_add_fusion.m_ref
  0.1 0.0 copy-start
  0.1 1.6 %copy-done = bf16[1024,1024]{1,0:T(8,128)(2,1)S(1)} copy-done((bf16[1024,1024]{1,0:T(8,128)(2,1)S(1)}, bf16[1024,1024]{1,0:T(8,128)(2,1)}, u32[]{:S(2)}) %copy-start) | copy-done | bytes 2097176
  1.7 0.0 copy-start.2
  1.7 1.6 %copy-done.2 = bf16[1024,1024]{1,0:T(8,128)(2,1)S(1)} copy-done((bf16[1024,1024]{1,0:T(8,128)(2,1)S(1)}, bf16[1024,1024]{1,0:T(8,128)(2,1)}, u32[]{:S(2)}) %copy-start.2) | copy-done | bytes 2097176
  3.3 0.0 copy-start.3
  3.3 1.6 %copy-done.3 = bf16[1024,1024]{1,0:T(8,128)(2,1)S(1)} copy-done((bf16[1024,1024]{1,0:T(8,128)(2,1)S(1)}, bf16[1024,1024]{1,0:T(8,128)(2,1)}, u32[]{:S(2)}) %copy-start.3) | copy-done | bytes 2097176
  4.9 0.0 copy-start.4
  4.9 0.8 %copy-done.4 = f32[3,4,1024]{2,1,0:T(4,128)S(1)} copy-done((f32[3,4,1024]{2,1,0:T(4,128)S(1)}, f32[3,4,1024]{2,1,0:T(4,128)}, u32[]{:S(2)}) %copy-start.4) | copy-done | bytes 49176
  5.6 0.0 copy-start.6
  5.7 7.7 %block_states.1 = (bf16[1024,1024]{1,0:T(8,128)(2,1)S(1)}, bf16[1024,1024]{1,0:T(8,128)(2,1)S(1)}, bf16[8,160,128]{2,1,0:T(8,128)(2,1)S(1)}) custom-call(s32[2]{0:T(128)S(1)} %pad_add_fusion.m_ref, bf16[1024,1024]{1,0:T(8,128)(2,1)S(1)} %copy-done, bf16[1024,1024]{1,0:T(8,128)(2,1)S(1)} %copy-done, bf16[1024,1024]{1,0:T(8,128)(2,1)S(1)} %copy-done.2, ...), custom_call_target="tpu_custom_call" | custom-call | flops 268435456 | bytes 8388608 | tf_op jit(solution)/shard_map/block_states/pallas_call | solution.py:78
  13.4 4.0 %collective-permute-start.2 = (bf16[2,160,128]{2,1,0:T(8,128)(2,1)S(1)}, bf16[2,160,128]{2,1,0:T(8,128)(2,1)S(1)}, u32[]{:S(2)}, u32[]{:S(2)}) collective-permute-start(bf16[2,160,128]{2,1,0:T(8,128)(2,1)S(1)} %get-tuple-element.23), channel_id=1, source_target_pairs={{0,3},{1,2},{2,1},{3,0},{4,7},{5,6},{6,5},{7,4},{8,11},{9,10},{10,... | collective-permute-start | bytes 245768 | tf_op jit(solution)/shard_map/ppermute | solution.py:332
  17.4 0.4 collective-permute-start.1
  17.9 0.2 collective-permute-start
  18.1 2.2 %collective-permute-done.2.refs_3_.p3 = bf16[2,160,128]{2,1,0:T(8,128)(2,1)S(1)} collective-permute-done((bf16[2,160,128]{2,1,0:T(8,128)(2,1)S(1)}, bf16[2,160,128]{2,1,0:T(8,128)(2,1)S(1)}, u32[]{:S(2)}, u32[]{:S(2)}) %collective-permute-start.2) | collective-permute-done | bytes 81952 | tf_op jit(solution)/shard_map/ppermute | solution.py:332
  20.3 1.8 %collective-permute-done.1.refs_2_.p2 = bf16[2,160,128]{2,1,0:T(8,128)(2,1)S(1)} collective-permute-done((bf16[2,160,128]{2,1,0:T(8,128)(2,1)S(1)}, bf16[2,160,128]{2,1,0:T(8,128)(2,1)S(1)}, u32[]{:S(2)}, u32[]{:S(2)}) %collective-permute-start.1) | collective-permute-done | bytes 81952 | tf_op jit(solution)/shard_map/ppermute | solution.py:332
  22.1 0.3 collective-permute-done.refs_1_.p1
  22.3 0.8 %group_total.1 = bf16[2,160,128]{2,1,0:T(8,128)(2,1)S(1)} custom-call(s32[2]{0:T(128)S(1)} %pad_add_fusion.m_ref, bf16[2,160,128]{2,1,0:T(8,128)(2,1)S(1)} %get-tuple-element.26.refs_0_.p0, bf16[2,160,128]{2,1,0:T(8,128)(2,1)S(1)} %collective-permute-done.refs_1_.p1, bf16[2,160,128]{2,1,0:T(8,128)(2,1)S(1)} %collective-permute-done.1.refs_2_.p2, ...), custom_call_target="tpu_custom_call" | custom-call | tf_op jit(solution)/shard_map/group_total/pallas_call | solution.py:164
  23.1 2.7 %collective-permute-start.3 = (bf16[2,160,128]{2,1,0:T(8,128)(2,1)S(1)}, bf16[2,160,128]{2,1,0:T(8,128)(2,1)S(1)}, u32[]{:S(2)}, u32[]{:S(2)}) collective-permute-start(bf16[2,160,128]{2,1,0:T(8,128)(2,1)S(1)} %group_total.1), channel_id=1, source_target_pairs={{0,4},{1,5},{2,6},{3,7},{4,0},{5,1},{6,2},{7,3},{8,12},{9,13},{10,... | collective-permute-start | bytes 245768 | tf_op jit(solution)/shard_map/ppermute | solution.py:332
  25.8 2.8 %collective-permute-done.3.x_ref = bf16[2,160,128]{2,1,0:T(8,128)(2,1)S(1)} collective-permute-done((bf16[2,160,128]{2,1,0:T(8,128)(2,1)S(1)}, bf16[2,160,128]{2,1,0:T(8,128)(2,1)S(1)}, u32[]{:S(2)}, u32[]{:S(2)}) %collective-permute-start.3) | collective-permute-done | bytes 81952 | tf_op jit(solution)/shard_map/ppermute | solution.py:332
  28.6 0.0 copy-done.6
  28.6 1.1 %member_prefixes.1 = (bf16[2,144,128]{2,1,0:T(8,128)(2,1)S(1)}, bf16[2,144,128]{2,1,0:T(8,128)(2,1)S(1)}, bf16[2,144,128]{2,1,0:T(8,128)(2,1)S(1)}, bf16[2,144,128]{2,1,0:T(8,128)(2,1)S(1)}) custom-call(s32[2]{0:T(128)S(1)} %pad_add_fusion.m_ref, bf16[2,160,128]{2,1,0:T(8,128)(2,1)S(1)} %get-tuple-element.26.refs_0_.p0, ...), custom_call_target="tpu_custom_call" | custom-call | tf_op jit(solution)/shard_map/member_prefixes/pallas_call | solution.py:216
  29.7 2.1 %collective-permute-start.4 = (bf16[2,144,128]{2,1,0:T(8,128)(2,1)S(1)}, bf16[2,144,128]{2,1,0:T(8,128)(2,1)S(1)}, u32[]{:S(2)}, u32[]{:S(2)}) collective-permute-start(bf16[2,144,128]{2,1,0:T(8,128)(2,1)S(1)} %get-tuple-element.16), channel_id=1, source_target_pairs={{0,1},{1,0},{2,3},{3,2},{4,5},{5,4},{6,7},{7,6},{8,9},{9,8},{10,11... | collective-permute-start | bytes 221192 | tf_op jit(solution)/shard_map/ppermute | solution.py:332
  31.9 0.5 %collective-permute-start.5 = (bf16[2,144,128]{2,1,0:T(8,128)(2,1)S(1)}, bf16[2,144,128]{2,1,0:T(8,128)(2,1)S(1)}, u32[]{:S(2)}, u32[]{:S(2)}) collective-permute-start(bf16[2,144,128]{2,1,0:T(8,128)(2,1)S(1)} %get-tuple-element.17), channel_id=1, source_target_pairs={{0,2},{1,3},{2,0},{3,1},{4,6},{5,7},{6,4},{7,5},{8,10},{9,11},{10,... | collective-permute-start | bytes 221192 | tf_op jit(solution)/shard_map/ppermute | solution.py:332
  32.4 1.0 %collective-permute-start.6 = (bf16[2,144,128]{2,1,0:T(8,128)(2,1)S(1)}, bf16[2,144,128]{2,1,0:T(8,128)(2,1)S(1)}, u32[]{:S(2)}, u32[]{:S(2)}) collective-permute-start(bf16[2,144,128]{2,1,0:T(8,128)(2,1)S(1)} %get-tuple-element.18), channel_id=1, source_target_pairs={{0,3},{1,2},{2,1},{3,0},{4,7},{5,6},{6,5},{7,4},{8,11},{9,10},{10,... | collective-permute-start | bytes 221192 | tf_op jit(solution)/shard_map/ppermute | solution.py:332
  33.4 0.0 copy-done.1
  33.4 0.0 copy-done.5
  33.4 11.7 %inner_attention.1 = (bf16[1024,1024]{1,0:T(8,128)(2,1)S(1)}, f32[1024,1024]{1,0:T(8,128)S(1)}) custom-call(bf16[1024,1024]{1,0:T(8,128)(2,1)S(1)} %copy-done.1, bf16[1024,1024]{1,0:T(8,128)(2,1)S(1)} %get-tuple-element.19.kf_ref, bf16[1024,1024]{1,0:T(8,128)(2,1)S(1)} %get-tuple-element.20.vf_ref, f32[3,4,1024]{2,1,0:T(4,128)S(1)} %copy-done.5), custom_call_target="tpu_custom_call" | custom-call | flops 1073741824 | bytes 12582912 | tf_op jit(solution)/shard_map/inner_attention/pallas_call | solution.py:269
  45.2 0.0 collective-permute-done.4.p1
  45.2 0.0 collective-permute-done.5.p2
  45.2 0.0 collective-permute-done.6.p3
  45.2 3.8 %finish.1 = bf16[1024,1024]{1,0:T(8,128)(2,1)} custom-call(s32[2]{0:T(128)S(1)} %pad_add_fusion.m_ref, bf16[2,144,128]{2,1,0:T(8,128)(2,1)S(1)} %get-tuple-element.15.p0, bf16[2,144,128]{2,1,0:T(8,128)(2,1)S(1)} %collective-permute-done.4.p1, bf16[2,144,128]{2,1,0:T(8,128)(2,1)S(1)} %collective-permute-done.5.p2, ...), custom_call_target="tpu_custom_call" | custom-call | tf_op jit(solution)/shard_map/finish/pallas_call | solution.py:314
  (3 shorter events, 0.0 us)
Async XLA Ops:
  0.1 1.6 %copy-start = (bf16[1024,1024]{1,0:T(8,128)(2,1)S(1)}, bf16[1024,1024]{1,0:T(8,128)(2,1)}, u32[]{:S(2)}) copy-start(bf16[1024,1024]{1,0:T(8,128)(2,1)} %q_ref.1) | copy-start | bytes 6291460
  1.7 1.6 %copy-start.2 = (bf16[1024,1024]{1,0:T(8,128)(2,1)S(1)}, bf16[1024,1024]{1,0:T(8,128)(2,1)}, u32[]{:S(2)}) copy-start(bf16[1024,1024]{1,0:T(8,128)(2,1)} %k_ref.1) | copy-start | bytes 6291460
  3.3 1.6 %copy-start.3 = (bf16[1024,1024]{1,0:T(8,128)(2,1)S(1)}, bf16[1024,1024]{1,0:T(8,128)(2,1)}, u32[]{:S(2)}) copy-start(bf16[1024,1024]{1,0:T(8,128)(2,1)} %v_ref.1) | copy-start | bytes 6291460
  4.9 0.8 %copy-start.4 = (f32[3,4,1024]{2,1,0:T(4,128)S(1)}, f32[3,4,1024]{2,1,0:T(4,128)}, u32[]{:S(2)}) copy-start(f32[3,4,1024]{2,1,0:T(4,128)} %w_ref.5) | copy-start | bytes 147460
  5.6 22.9 %copy-start.6 = (f32[1024]{0:T(1024)S(1)}, f32[1024]{0:T(1024)}, u32[]{:S(2)}) copy-start(f32[1024]{0:T(1024)} %param.9) | copy-start | bytes 12292
  5.7 27.8 %copy-start.1 = (bf16[1024,1024]{1,0:T(8,128)(2,1)S(1)}, bf16[1024,1024]{1,0:T(8,128)(2,1)}, u32[]{:S(2)}) copy-start(bf16[1024,1024]{1,0:T(8,128)(2,1)} %q_ref.1) | copy-start | bytes 6291460
  5.7 27.8 %copy-start.5 = (f32[3,4,1024]{2,1,0:T(4,128)S(1)}, f32[3,4,1024]{2,1,0:T(4,128)}, u32[]{:S(2)}) copy-start(f32[3,4,1024]{2,1,0:T(4,128)} %w_ref.5) | copy-start | bytes 147460
  13.4 6.9 %collective-permute-start.2 = (bf16[2,160,128]{2,1,0:T(8,128)(2,1)S(1)}, bf16[2,160,128]{2,1,0:T(8,128)(2,1)S(1)}, u32[]{:S(2)}, u32[]{:S(2)}) collective-permute-start(bf16[2,160,128]{2,1,0:T(8,128)(2,1)S(1)} %get-tuple-element.23), channel_id=1, source_target_pairs={{0,3},{1,2},{2,1},{3,0},{4,7},{5,6},{6,5},{7,4},{8,11},{9,10},{10,... | collective-permute-start | bytes 245768 | tf_op jit(solution)/shard_map/ppermute | solution.py:332
  17.4 4.6 %collective-permute-start.1 = (bf16[2,160,128]{2,1,0:T(8,128)(2,1)S(1)}, bf16[2,160,128]{2,1,0:T(8,128)(2,1)S(1)}, u32[]{:S(2)}, u32[]{:S(2)}) collective-permute-start(bf16[2,160,128]{2,1,0:T(8,128)(2,1)S(1)} %get-tuple-element.24), channel_id=1, source_target_pairs={{0,2},{1,3},{2,0},{3,1},{4,6},{5,7},{6,4},{7,5},{8,10},{9,11},{10,... | collective-permute-start | bytes 245768 | tf_op jit(solution)/shard_map/ppermute | solution.py:332
  17.9 4.4 %collective-permute-start = (bf16[2,160,128]{2,1,0:T(8,128)(2,1)S(1)}, bf16[2,160,128]{2,1,0:T(8,128)(2,1)S(1)}, u32[]{:S(2)}, u32[]{:S(2)}) collective-permute-start(bf16[2,160,128]{2,1,0:T(8,128)(2,1)S(1)} %get-tuple-element.25), channel_id=1, source_target_pairs={{0,1},{1,0},{2,3},{3,2},{4,5},{5,4},{6,7},{7,6},{8,9},{9,8},{10,11... | collective-permute-start | bytes 245768 | tf_op jit(solution)/shard_map/ppermute | solution.py:332
  23.1 5.4 %collective-permute-start.3 = (bf16[2,160,128]{2,1,0:T(8,128)(2,1)S(1)}, bf16[2,160,128]{2,1,0:T(8,128)(2,1)S(1)}, u32[]{:S(2)}, u32[]{:S(2)}) collective-permute-start(bf16[2,160,128]{2,1,0:T(8,128)(2,1)S(1)} %group_total.1), channel_id=1, source_target_pairs={{0,4},{1,5},{2,6},{3,7},{4,0},{5,1},{6,2},{7,3},{8,12},{9,13},{10,... | collective-permute-start | bytes 245768 | tf_op jit(solution)/shard_map/ppermute | solution.py:332
  29.7 15.4 %collective-permute-start.4 = (bf16[2,144,128]{2,1,0:T(8,128)(2,1)S(1)}, bf16[2,144,128]{2,1,0:T(8,128)(2,1)S(1)}, u32[]{:S(2)}, u32[]{:S(2)}) collective-permute-start(bf16[2,144,128]{2,1,0:T(8,128)(2,1)S(1)} %get-tuple-element.16), channel_id=1, source_target_pairs={{0,1},{1,0},{2,3},{3,2},{4,5},{5,4},{6,7},{7,6},{8,9},{9,8},{10,11... | collective-permute-start | bytes 221192 | tf_op jit(solution)/shard_map/ppermute | solution.py:332
  31.9 13.3 %collective-permute-start.5 = (bf16[2,144,128]{2,1,0:T(8,128)(2,1)S(1)}, bf16[2,144,128]{2,1,0:T(8,128)(2,1)S(1)}, u32[]{:S(2)}, u32[]{:S(2)}) collective-permute-start(bf16[2,144,128]{2,1,0:T(8,128)(2,1)S(1)} %get-tuple-element.17), channel_id=1, source_target_pairs={{0,2},{1,3},{2,0},{3,1},{4,6},{5,7},{6,4},{7,5},{8,10},{9,11},{10,... | collective-permute-start | bytes 221192 | tf_op jit(solution)/shard_map/ppermute | solution.py:332
  32.4 12.8 %collective-permute-start.6 = (bf16[2,144,128]{2,1,0:T(8,128)(2,1)S(1)}, bf16[2,144,128]{2,1,0:T(8,128)(2,1)S(1)}, u32[]{:S(2)}, u32[]{:S(2)}) collective-permute-start(bf16[2,144,128]{2,1,0:T(8,128)(2,1)S(1)} %get-tuple-element.18), channel_id=1, source_target_pairs={{0,3},{1,2},{2,1},{3,0},{4,7},{5,6},{6,5},{7,4},{8,11},{9,10},{10,... | collective-permute-start | bytes 221192 | tf_op jit(solution)/shard_map/ppermute | solution.py:332

commit v2 on v1

--- a/solution.py
+++ b/solution.py
@@ -10,10 +10,14 @@
 HDIM = 128
 CONV = 4
 GROUP = 4
-CHUNK = 128
+ROWS = 256
+CHUNK = 256
+PIECES = (3, 3, 2)
+PARTS = 2
+AHEAD = 2
 AUX = 32
 FIX = 16
-HALF_SCALE = HDIM ** (-0.5)
+SCALE = HDIM ** (-0.5)
 F32, BF16 = jnp.float32, jnp.bfloat16
 
 
@@ -25,12 +29,9 @@
     return lax.dot_general(a, b, (dims, ((), ())), preferred_element_type=F32)
 
 
-def conv_chunk(x_ref, cols, start, taps):
-    x = x_ref[start : start + CHUNK, cols].astype(F32)
-    if start:
-        earlier = x_ref[start - 16 : start, cols].astype(F32)[8:16]
-    else:
-        earlier = jnp.zeros((8, HDIM), F32)
+def conv_rows(x, earlier, taps):
+    x = x.astype(F32)
+    earlier = jnp.zeros((8, HDIM), F32) if earlier is None else earlier.astype(F32)[8:16]
     x = jnp.concatenate([earlier, x], axis=0)
     x1 = pltpu.roll(x, 1, 0)
     late = taps[3:4] * x + taps[2:3] * x1
@@ -48,60 +49,91 @@
     return jnp.where(rows_iota((8, HDIM)) < 4, first, last)
 
 
-def state_kernel(m_ref, q_first, q_last, k_ref, v_ref, w_ref, kf_ref, vf_ref, msg_ref):
-    tokens = k_ref.shape[0]
-    for h in range(k_ref.shape[1] // HDIM):
-        cols = slice(h * HDIM, (h + 1) * HDIM)
+def state_kernel(m_ref, q_hbm, k_hbm, v_hbm, w_hbm, kf_ref, vf_ref, msg_ref, k_buf, v_buf, edge, w_ref, k_sem, v_sem, sem):
+    heads, tokens = k_buf.shape[0:2]
+
+    def fetch(source, target, semaphore, h):
+        cols = pl.ds(pl.multiple_of(h * HDIM, HDIM), HDIM)
+        return pltpu.make_async_copy(source.at[:, cols], target.at[h], semaphore.at[h])
+
+    small = [
+        pltpu.make_async_copy(w_hbm, w_ref, sem.at[0]),
+        pltpu.make_async_copy(q_hbm.at[0:16], edge.at[0], sem.at[1]),
+        pltpu.make_async_copy(q_hbm.at[tokens - 16 : tokens], edge.at[1], sem.at[2]),
+    ]
+    small[0].start()
+    for h in range(AHEAD):
+        fetch(k_hbm, k_buf, k_sem, h).start()
+        fetch(v_hbm, v_buf, v_sem, h).start()
+    small[1].start()
+    small[2].start()
+    for copy in small:
+        copy.wait()
+
+    def one_head(h, carry):
+        @pl.when(h + AHEAD < heads)
+        def _():
+            fetch(k_hbm, k_buf, k_sem, h + AHEAD).start()
+            fetch(v_hbm, v_buf, v_sem, h + AHEAD).start()
+
+        fetch(k_hbm, k_buf, k_sem, h).wait()
+        fetch(v_hbm, v_buf, v_sem, h).wait()
+        cols = pl.ds(pl.multiple_of(h * HDIM, HDIM), HDIM)
         wk = w_ref[1, :, cols] * 0.5
         wv = w_ref[2, :, cols]
-        for start in range(0, tokens, CHUNK):
-            kf = silu_of_twice(conv_chunk(k_ref, cols, start, wk))
+        local = jnp.zeros((HDIM, HDIM), F32)
+        for start in range(0, tokens, ROWS):
+            rows = slice(start, start + ROWS)
+            above = slice(start - 16, start)
+            kf = silu_of_twice(conv_rows(k_buf[h, rows], k_buf[h, above] if start else None, wk))
             if start == 0:
                 kf = jnp.where(rows_iota(kf.shape) < CONV - 1, 0.0, kf)
-            kf_ref[start : start + CHUNK, cols] = kf.astype(BF16)
-            vf_ref[start : start + CHUNK, cols] = conv_chunk(v_ref, cols, start, wv).astype(BF16)
-        local = dot(kf_ref[:, cols], vf_ref[:, cols], ((0,), (0,)))
-        msg_ref[h, 0:HDIM] = local.astype(BF16)
-        mk = merged_rows(k_ref[0:16, cols], k_ref[tokens - 16 : tokens, cols])
-        mv = merged_rows(v_ref[0:16, cols], v_ref[tokens - 16 : tokens, cols])
-        mq = merged_rows(q_first[:, cols], q_last[:, cols])
-        msg_ref[h, HDIM : HDIM + 16] = jnp.concatenate([mk, mv], axis=0).astype(BF16)
-        msg_ref[h, HDIM + 16 : HDIM + 32] = jnp.concatenate([mq, mq], axis=0).astype(BF16)
+            kf = kf.astype(BF16)
+            vf = conv_rows(v_buf[h, rows], v_buf[h, above] if start else None, wv).astype(BF16)
+            kf_ref[h, rows] = kf
+            vf_ref[h, rows] = vf
+            local = local + dot(kf, vf, ((0,), (0,)))
+        per = heads // GROUP
+        place = (lax.div(h, per) ^ m_ref[0]) * per + lax.rem(h, per)
+        msg_ref[place, 0:HDIM] = local.astype(BF16)
+        mk = merged_rows(k_buf[h, 0:16], k_buf[h, tokens - 16 : tokens])
+        mv = merged_rows(v_buf[h, 0:16], v_buf[h, tokens - 16 : tokens])
+        mq = merged_rows(edge[0, :, cols], edge[1, :, cols])
+        msg_ref[place, HDIM : HDIM + 16] = jnp.concatenate([mk, mv], axis=0).astype(BF16)
+        msg_ref[place, HDIM + 16 : HDIM + 32] = jnp.concatenate([mq, mq], axis=0).astype(BF16)
+        return carry
+
+    lax.fori_loop(0, heads, one_head, 0)
+
+
+VMEM = pl.BlockSpec(memory_space=pltpu.VMEM)
+SMEM = pl.BlockSpec(memory_space=pltpu.SMEM)
+HBM = pl.BlockSpec(memory_space=pltpu.HBM)
 
 
 def block_states(m, queries, key_rows, value_rows, conv_weight):
     tokens, width = key_rows.shape
-    quarter = width // GROUP
-    heads = quarter // HDIM
-    last = tokens // 16 - 1
-    cols = lambda j, m: (0, j ^ m[0])
+    heads = width // HDIM
+    features = jax.ShapeDtypeStruct((heads, tokens, HDIM), BF16)
+    arrays = [pltpu.with_memory_space_constraint(a, pltpu.HBM) for a in (queries, key_rows, value_rows, conv_weight)]
     return pl.pallas_call(
         state_kernel,
-        grid_spec=pltpu.PrefetchScalarGridSpec(
-            num_scalar_prefetch=1,
-            grid=(GROUP,),
-            in_specs=[
-                pl.BlockSpec((16, quarter), cols),
-                pl.BlockSpec((16, quarter), lambda j, m: (last, j ^ m[0])),
-                pl.BlockSpec((tokens, quarter), cols),
-                pl.BlockSpec((tokens, quarter), cols),
-                pl.BlockSpec((3, CONV, quarter), lambda j, m: (0, 0, j ^ m[0])),
-            ],
-            out_specs=[
-                pl.BlockSpec((tokens, quarter), cols),
-                pl.BlockSpec((tokens, quarter), cols),
-                pl.BlockSpec((heads, HDIM + AUX, HDIM), lambda j, m: (j, 0, 0)),
-            ],
-        ),
-        out_shape=[
-            jax.ShapeDtypeStruct((tokens, width), BF16),
-            jax.ShapeDtypeStruct((tokens, width), BF16),
-            jax.ShapeDtypeStruct((GROUP * heads, HDIM + AUX, HDIM), BF16),
+        in_specs=[SMEM, HBM, HBM, HBM, HBM],
+        out_specs=[VMEM] * 3,
+        out_shape=[features, features, jax.ShapeDtypeStruct((heads, HDIM + AUX, HDIM), BF16)],
+        scratch_shapes=[
+            pltpu.VMEM((heads, tokens, HDIM), BF16),
+            pltpu.VMEM((heads, tokens, HDIM), BF16),
+            pltpu.VMEM((2, 16, width), BF16),
+            pltpu.VMEM(conv_weight.shape, F32),
+            pltpu.SemaphoreType.DMA((heads,)),
+            pltpu.SemaphoreType.DMA((heads,)),
+            pltpu.SemaphoreType.DMA((3,)),
         ],
-        compiler_params=pltpu.CompilerParams(vmem_limit_bytes=16 << 20),
+        compiler_params=pltpu.CompilerParams(vmem_limit_bytes=24 << 20),
         cost_estimate=pl.CostEstimate(flops=2 * tokens * width * HDIM, bytes_accessed=8 * tokens * width, transcendentals=tokens * width),
         name="block_states",
-    )(m, queries, queries, key_rows, value_rows, conv_weight)
+    )(m, *arrays)
 
 
 def edge_rows(own, before, taps):
@@ -190,7 +222,7 @@
         for t in range(GROUP):
             own = buf[t, h, HDIM:].astype(F32)
             kf, vf = edge_kv(own, before, w_ref, cols)
-            qf = silu_of_twice(edge_rows(own[16:24], before[16:24], w_ref[0, :, cols] * 0.5)) * HALF_SCALE
+            qf = silu_of_twice(edge_rows(own[16:24], before[16:24], w_ref[0, :, cols] * 0.5)) * SCALE
             blank = jnp.zeros((8, HDIM), F32)
             kf = jnp.concatenate([kf, blank], axis=0).astype(BF16)
             vf = jnp.concatenate([vf, blank], axis=0).astype(BF16)
@@ -236,95 +268,99 @@
     )(m, *packets, incoming, conv_weight, gain)
 
 
-def inner_kernel(q_ref, kf_ref, vf_ref, w_ref, qf_ref, inner_ref):
-    tokens = q_ref.shape[0]
+def inner_kernel(first, q_ref, kf_ref, vf_ref, w_ref, qf_ref, inner_ref):
+    heads, tokens = qf_ref.shape[0:2]
     shape = (CHUNK, CHUNK)
     causal = rows_iota(shape) >= lax.broadcasted_iota(jnp.int32, shape, 1)
-    for h in range(q_ref.shape[1] // HDIM):
-        cols = slice(h * HDIM, (h + 1) * HDIM)
+    for h in range(heads):
+        cols = slice((first + h) * HDIM, (first + h + 1) * HDIM)
         wq = w_ref[0, :, cols] * 0.5
         state = None
         for start in range(0, tokens, CHUNK):
             rows = slice(start, start + CHUNK)
-            qf = (silu_of_twice(conv_chunk(q_ref, cols, start, wq)) * HALF_SCALE).astype(BF16)
-            qf_ref[rows, cols] = qf
-            kf, vf = kf_ref[rows, cols], vf_ref[rows, cols]
+            above = q_ref[start - 16 : start, cols] if start else None
+            qf = (silu_of_twice(conv_rows(q_ref[rows, cols], above, wq)) * SCALE).astype(BF16)
+            qf_ref[h, rows] = qf
+            kf, vf = kf_ref[first + h, rows], vf_ref[first + h, rows]
             scores = jnp.where(causal, dot(qf, kf, ((1,), (1,))), 0.0).astype(BF16)
-            if state is None:
-                inner = dot(scores, vf, ((1,), (0,)))
-                state = dot(kf, vf, ((0,), (0,)))
-            else:
-                left = jnp.concatenate([scores, qf], axis=1)
-                right = jnp.concatenate([vf, state.astype(BF16)], axis=0)
-                inner = dot(left, right, ((1,), (0,)))
-                if start + CHUNK < tokens:
-                    state = state + dot(kf, vf, ((0,), (0,)))
-            inner_ref[rows, cols] = inner
-
-
-def inner_attention(queries, kf, vf, conv_weight):
-    tokens, width = queries.shape
-    quarter = width // GROUP
-    block = pl.BlockSpec((tokens, quarter), lambda j: (0, j))
+            inner = dot(scores, vf, ((1,), (0,)))
+            if state is not None:
+                inner = inner + dot(qf, state.astype(BF16), ((1,), (0,)))
+            inner_ref[h, rows] = inner
+            if start + CHUNK < tokens:
+                new = dot(kf, vf, ((0,), (0,)))
+                state = new if state is None else state + new
+
+
+def inner_attention(first, count, queries, kf, vf, conv_weight):
+    heads, tokens = kf.shape[0:2]
     return pl.pallas_call(
-        inner_kernel,
-        grid=(GROUP,),
-        in_specs=[block, block, block, pl.BlockSpec((3, CONV, quarter), lambda j: (0, 0, j))],
-        out_specs=[block, block],
+        functools.partial(inner_kernel, first),
+        in_specs=[VMEM] * 4,
+        out_specs=[VMEM] * 2,
         out_shape=[
-            jax.ShapeDtypeStruct((tokens, width), BF16),
-            jax.ShapeDtypeStruct((tokens, width), F32),
+            jax.ShapeDtypeStruct((count, tokens, HDIM), BF16),
+            jax.ShapeDtypeStruct((count, tokens, HDIM), F32),
         ],
-        compiler_params=pltpu.CompilerParams(vmem_limit_bytes=16 << 20),
-        cost_estimate=pl.CostEstimate(flops=8 * tokens * width * HDIM, bytes_accessed=12 * tokens * width, transcendentals=tokens * width),
+        compiler_params=pltpu.CompilerParams(vmem_limit_bytes=24 << 20),
+        cost_estimate=pl.CostEstimate(
+            flops=8 * count * tokens * HDIM * HDIM,
+            bytes_accessed=12 * tokens * count * HDIM,
+            transcendentals=tokens * count * HDIM,
+        ),
         name="inner_attention",
     )(queries, kf, vf, conv_weight)
 
 
-def finish_kernel(m_ref, p0, p1, p2, p3, qf_ref, inner_ref, gain_ref, out_ref, buf):
-    step = pl.program_id(0)
-
-    @pl.when(step == 0)
-    def _():
-        gather_packets(m_ref, (p0, p1, p2, p3), buf)
-
+def finish_kernel(pieces, m_ref, p0, p1, p2, p3, *refs):
+    qf_refs, inner_refs, refs = refs[0:pieces], refs[pieces : 2 * pieces], refs[2 * pieces :]
+    gain_ref, out_hbm, buf, out_buf, sem = refs
+    gather_packets(m_ref, (p0, p1, p2, p3), buf)
     heads = p0.shape[0]
-    for index in range(GROUP * heads):
-        t, h = index // heads, index % heads
-        cols = slice(index * HDIM, (index + 1) * HDIM)
-        o = inner_ref[:, cols] + dot(qf_ref[:, cols], buf[t, h, 0:HDIM], ((1,), (0,)))
-        o = o * lax.rsqrt(jnp.mean(o * o, axis=1, keepdims=True) + 1e-06) * gain_ref[:, cols]
-        out_ref[:, cols] = o.astype(BF16)
-
-    @pl.when(step == 0)
-    def _():
-        for index in range(GROUP * heads):
-            t, h = index // heads, index % heads
-            cols = slice(index * HDIM, (index + 1) * HDIM)
-            there = rows_iota((FIX, HDIM)) < CONV - 1
-            fixed = buf[t, h, HDIM:].astype(F32)
-            out_ref[0:FIX, cols] = jnp.where(there, fixed, out_ref[0:FIX, cols].astype(F32)).astype(BF16)
-
-
-def finish(m, prefixes, qf, inner, gain):
-    tokens, width = qf.shape
+    tokens = qf_refs[0].shape[1]
+    part = tokens // sem.shape[0]
+
+    def send(c):
+        rows = slice(c * part, (c + 1) * part)
+        return pltpu.make_async_copy(out_buf.at[rows], out_hbm.at[rows], sem.at[c])
+
+    for c in range(sem.shape[0]):
+        rows = slice(c * part, (c + 1) * part)
+        index = 0
+        for qf_ref, inner_ref in zip(qf_refs, inner_refs):
+            for i in range(qf_ref.shape[0]):
+                t, h = index // heads, index % heads
+                cols = slice(index * HDIM, (index + 1) * HDIM)
+                o = inner_ref[i, rows] + dot(qf_ref[i, rows], buf[t, h, 0:HDIM], ((1,), (0,)))
+                o = o * lax.rsqrt(jnp.mean(o * o, axis=1, keepdims=True) + 1e-06) * gain_ref[:, cols]
+                if c == 0:
+                    fixed = buf[t, h, HDIM:].astype(F32)
+                    there = rows_iota((FIX, HDIM)) < CONV - 1
+                    o = jnp.concatenate([jnp.where(there, fixed, o[0:FIX]), o[FIX:]], axis=0)
+                out_buf[rows, cols] = o.astype(BF16)
+                index += 1
+        send(c).start()
+    for c in range(sem.shape[0]):
+        send(c).wait()
+
+
+def finish(m, prefixes, qfs, inners, gain):
+    tokens = qfs[0].shape[1]
+    width = gain.shape[1]
     heads = width // GROUP // HDIM
-    rows = tokens // 4
-    block = pl.BlockSpec((rows, width), lambda i, m: (i, 0))
     return pl.pallas_call(
-        finish_kernel,
-        grid_spec=pltpu.PrefetchScalarGridSpec(
-            num_scalar_prefetch=1,
-            grid=(tokens // rows,),
-            in_specs=packet_specs(heads, HDIM + FIX)
-            + [block, block, pl.BlockSpec((1, width), lambda i, m: (0, 0))],
-            out_specs=block,
-            scratch_shapes=[pltpu.VMEM((GROUP, heads, HDIM + FIX, HDIM), BF16)],
-        ),
+        functools.partial(finish_kernel, len(qfs)),
+        in_specs=[SMEM] + [VMEM] * (GROUP + 2 * len(qfs) + 1),
+        out_specs=HBM,
         out_shape=jax.ShapeDtypeStruct((tokens, width), BF16),
-        compiler_params=pltpu.CompilerParams(vmem_limit_bytes=16 << 20),
+        scratch_shapes=[
+            pltpu.VMEM((GROUP, heads, HDIM + FIX, HDIM), BF16),
+            pltpu.VMEM((tokens, width), BF16),
+            pltpu.SemaphoreType.DMA((PARTS,)),
+        ],
+        compiler_params=pltpu.CompilerParams(vmem_limit_bytes=24 << 20),
         name="finish",
-    )(m, *prefixes, qf, inner, gain)
+    )(m, *prefixes, *qfs, *inners, gain)
 
 
 def swapped(value, bits):
@@ -345,8 +381,22 @@
     m = jnp.stack([place % GROUP, place // GROUP]).astype(jnp.int32)
     gain = head_gain.reshape(1, width)
     kf, vf, messages = block_states(m, queries, key_rows, value_rows, conv_weight)
+    bounds = [0]
+    for piece in PIECES:
+        bounds.append(bounds[-1] + piece * (width // HDIM) // 8)
+    qfs, inners = [], []
+
+    def beside(piece, arrays):
+        first, end = bounds[piece : piece + 2]
+        qf, inner = inner_attention(first, end - first, queries, kf, vf, conv_weight)
+        arrays, qf, inner = lax.optimization_barrier((arrays, qf, inner))
+        qfs.append(qf)
+        inners.append(inner)
+        return arrays
+
     packets = [messages[0:heads]]
     packets += [swapped(messages[j * heads : (j + 1) * heads], j) for j in range(1, GROUP)]
+    packets = beside(0, packets)
     if groups == 2:
         incoming = swapped(group_total(m, packets, None, conv_weight), GROUP)
     else:
@@ -358,10 +408,11 @@
             prefix = to_next_group(passed)
             passed = prefix + total
         incoming = jnp.concatenate([prefix.astype(BF16), tail], axis=1)
-    qf, inner = inner_attention(queries, kf, vf, conv_weight)
+    incoming = beside(1, incoming)
     sends = member_prefixes(m, packets, incoming, conv_weight, gain)
     prefixes = [sends[0]] + [swapped(sends[j], j) for j in range(1, GROUP)]
-    return finish(m, prefixes, qf, inner, gain)
+    prefixes = beside(2, prefixes)
+    return finish(m, prefixes, qfs, inners, gain)
 
 
 def solution(mesh):

time: 49.2 us -> 35.2 us (0.72)
  Pallas kernels: 25.1 us -> 16.4 us
  local copies, waits for them, and re-layouts: 5.6 us -> 0.04 us
  waiting for transfers between devices: 7.04 us -> 7.7 us
    pallas_call x3 -> x5, Pallas kernels: 23.2 us -> 14.4 us  [the longest x1 7.22 us: block_states(): pl.pallas_call(state_kernel, in_specs=[SMEM, HBM, HBM, HBM, HBM], out_spe...]
    unnamed x14 -> x6, local copies, waits for them, and re-layouts: 5.58 us -> 0.01 us
    ppermute x7, waiting for transfers between devices: 7.04 us -> 7.7 us  [swapped(): return lax.ppermute(value, 'ctx', [(s, s ^ bits) for s in range(count)])]
  transfers between devices with their start and end apart: 7 -> 7, of which waited for: 4 -> 5; matrix products, arithmetic and copies ran while one was open for 0% -> 0% of each run, Pallas kernels for 24% -> 12%
where the time goes in v2:
time: 35.2 us; the launch traced here: 35.1 us
  Pallas kernels  16.4 us (47%)
  starting transfers between devices  10.8 us (31%)
  waiting for transfers between devices  7.7 us (22%)
    ppermute x7, starting transfers between devices, swapped(): return lax.ppermute(value, 'ctx', [(s, s ^ bits) for s in range(count)])  10.8 us
    ppermute x7, waiting for transfers between devices, swapped(): return lax.ppermute(value, 'ctx', [(s, s ^ bits) for s in range(count)])  7.7 us
    pallas_call x1, Pallas kernels, block_states(): pl.pallas_call(state_kernel, in_specs=[SMEM, HBM, HBM, HBM, HBM], out_spe...  7.22 us
    pallas_call x3, Pallas kernels, inner_attention(): pl.pallas_call(functools.partial(inner_kernel, first), in_specs=[VMEM] *...  4.28 us
    pallas_call x1, Pallas kernels, finish(): pl.pallas_call(functools.partial(finish_kernel, len(qfs)), in_specs=[SMEM...  2.92 us
    pallas_call x1, Pallas kernels, member_prefixes(): pl.pallas_call(prefix_kernel, grid_spec=pltpu.PrefetchScalarGridSpec(num_...  1.15 us
    pallas_call x1, Pallas kernels, group_total(): pl.pallas_call(functools.partial(total_kernel, tail is not None), grid_sp...  0.79 us
  transfers between devices with their start and end apart: 7, of which 5 were waited for; matrix products, arithmetic and copies ran while one was open for 0% of the time, Pallas kernels for 12%

profile of v2, /device:TPU:0, one launch (start us, length us, event | category | flops | bytes accessed | tf_op | source)
XLA Modules:
  0.0 35.1 jit_solution(3274392223197507421)
XLA Ops:
  0.0 0.1 pad_add_fusion.m_ref
  0.1 0.0 copy-start
  0.1 0.0 copy-start.1
  0.1 7.2 %block_states.1 = (bf16[8,1024,128]{2,1,0:T(8,128)(2,1)S(1)}, bf16[8,1024,128]{2,1,0:T(8,128)(2,1)S(1)}, bf16[8,160,128]{2,1,0:T(8,128)(2,1)S(1)}) custom-call(s32[2]{0:T(128)S(1)} %pad_add_fusion.m_ref, bf16[1024,1024]{1,0:T(8,128)(2,1)} %q_ref.5, bf16[1024,1024]{1,0:T(8,128)(2,1)} %k_hbm.1, bf16[1024,1024]{1,0:T(8,128)(2,1)} %v_hbm.1, f32[3,4,1024]{2,1,0:T(4,128)} %w_ref.7), custom_call_target="tpu_custom_call" | custom-call | flops 268435456 | bytes 8388608 | tf_op jit(solution)/shard_map/block_states/pallas_call | solution.py:119
  7.3 3.0 %collective-permute-start = (bf16[2,160,128]{2,1,0:T(8,128)(2,1)S(1)}, bf16[2,160,128]{2,1,0:T(8,128)(2,1)S(1)}, u32[]{:S(2)}, u32[]{:S(2)}) collective-permute-start(bf16[2,160,128]{2,1,0:T(8,128)(2,1)S(1)} %get-tuple-element.63), channel_id=1, source_target_pairs={{0,1},{1,0},{2,3},{3,2},{4,5},{5,4},{6,7},{7,6},{8,9},{9,8},{10,11... | collective-permute-start | bytes 245768 | tf_op jit(solution)/shard_map/ppermute | solution.py:368
  10.4 1.6 %collective-permute-start.1 = (bf16[2,160,128]{2,1,0:T(8,128)(2,1)S(1)}, bf16[2,160,128]{2,1,0:T(8,128)(2,1)S(1)}, u32[]{:S(2)}, u32[]{:S(2)}) collective-permute-start(bf16[2,160,128]{2,1,0:T(8,128)(2,1)S(1)} %get-tuple-element.62), channel_id=1, source_target_pairs={{0,2},{1,3},{2,0},{3,1},{4,6},{5,7},{6,4},{7,5},{8,10},{9,11},{10,... | collective-permute-start | bytes 245768 | tf_op jit(solution)/shard_map/ppermute | solution.py:368
  12.0 0.0 collective-permute-start.2
  12.0 0.0 copy-done
  12.0 0.0 copy-done.1
  12.0 1.6 %inner_attention.3 = (bf16[3,1024,128]{2,1,0:T(8,128)(2,1)S(1)}, f32[3,1024,128]{2,1,0:T(8,128)S(1)}) custom-call(bf16[1024,1024]{1,0:T(8,128)(2,1)S(1)} %copy-done, bf16[8,1024,128]{2,1,0:T(8,128)(2,1)S(1)} %get-tuple-element.34.kf_ref, bf16[8,1024,128]{2,1,0:T(8,128)(2,1)S(1)} %get-tuple-element.35.vf_ref, f32[3,4,1024]{2,1,0:T(4,128)S(1)} %copy-done.1), custom_call_target="tpu_custom_call" | custom-call | flops 402653184 | bytes 4718592 | tf_op jit(solution)/shard_map/inner_attention/pallas_call | solution.py:297
  13.5 0.0 collective-permute-done.refs_1_.p1
  13.5 2.0 %collective-permute-done.1.refs_2_.p2 = bf16[2,160,128]{2,1,0:T(8,128)(2,1)S(1)} collective-permute-done((bf16[2,160,128]{2,1,0:T(8,128)(2,1)S(1)}, bf16[2,160,128]{2,1,0:T(8,128)(2,1)S(1)}, u32[]{:S(2)}, u32[]{:S(2)}) %collective-permute-start.1) | collective-permute-done | bytes 81952 | tf_op jit(solution)/shard_map/ppermute | solution.py:368
  15.5 1.8 %collective-permute-done.2.refs_3_.p3 = bf16[2,160,128]{2,1,0:T(8,128)(2,1)S(1)} collective-permute-done((bf16[2,160,128]{2,1,0:T(8,128)(2,1)S(1)}, bf16[2,160,128]{2,1,0:T(8,128)(2,1)S(1)}, u32[]{:S(2)}, u32[]{:S(2)}) %collective-permute-start.2) | collective-permute-done | bytes 81952 | tf_op jit(solution)/shard_map/ppermute | solution.py:368
  17.3 0.8 %group_total.1 = bf16[2,160,128]{2,1,0:T(8,128)(2,1)S(1)} custom-call(s32[2]{0:T(128)S(1)} %pad_add_fusion.m_ref, bf16[2,160,128]{2,1,0:T(8,128)(2,1)S(1)} %get-tuple-element.38.refs_0_.p0, bf16[2,160,128]{2,1,0:T(8,128)(2,1)S(1)} %collective-permute-done.refs_1_.p1, bf16[2,160,128]{2,1,0:T(8,128)(2,1)S(1)} %collective-permute-done.1.refs_2_.p2, ...), custom_call_target="tpu_custom_call" | custom-call | tf_op jit(solution)/shard_map/group_total/pallas_call | solution.py:196
  18.1 0.0 copy-start.2
  18.1 2.7 %collective-permute-start.3 = (bf16[2,160,128]{2,1,0:T(8,128)(2,1)S(1)}, bf16[2,160,128]{2,1,0:T(8,128)(2,1)S(1)}, u32[]{:S(2)}, u32[]{:S(2)}) collective-permute-start(bf16[2,160,128]{2,1,0:T(8,128)(2,1)S(1)} %group_total.1), channel_id=1, source_target_pairs={{0,4},{1,5},{2,6},{3,7},{4,0},{5,1},{6,2},{7,3},{8,12},{9,13},{10,... | collective-permute-start | bytes 245768 | tf_op jit(solution)/shard_map/ppermute | solution.py:368
  20.7 1.6 %inner_attention.4 = (bf16[3,1024,128]{2,1,0:T(8,128)(2,1)S(1)}, f32[3,1024,128]{2,1,0:T(8,128)S(1)}) custom-call(bf16[1024,1024]{1,0:T(8,128)(2,1)S(1)} %copy-done, bf16[8,1024,128]{2,1,0:T(8,128)(2,1)S(1)} %get-tuple-element.34.kf_ref, bf16[8,1024,128]{2,1,0:T(8,128)(2,1)S(1)} %get-tuple-element.35.vf_ref, f32[3,4,1024]{2,1,0:T(4,128)S(1)} %copy-done.1), custom_call_target="tpu_custom_call" | custom-call | flops 402653184 | bytes 4718592 | tf_op jit(solution)/shard_map/inner_attention/pallas_call | solution.py:297
  22.3 2.0 %collective-permute-done.3.x_ref = bf16[2,160,128]{2,1,0:T(8,128)(2,1)S(1)} collective-permute-done((bf16[2,160,128]{2,1,0:T(8,128)(2,1)S(1)}, bf16[2,160,128]{2,1,0:T(8,128)(2,1)S(1)}, u32[]{:S(2)}, u32[]{:S(2)}) %collective-permute-start.3) | collective-permute-done | bytes 81952 | tf_op jit(solution)/shard_map/ppermute | solution.py:368
  24.3 0.0 copy-done.2
  24.3 1.1 %member_prefixes.1 = (bf16[2,144,128]{2,1,0:T(8,128)(2,1)S(1)}, bf16[2,144,128]{2,1,0:T(8,128)(2,1)S(1)}, bf16[2,144,128]{2,1,0:T(8,128)(2,1)S(1)}, bf16[2,144,128]{2,1,0:T(8,128)(2,1)S(1)}) custom-call(s32[2]{0:T(128)S(1)} %pad_add_fusion.m_ref, bf16[2,160,128]{2,1,0:T(8,128)(2,1)S(1)} %get-tuple-element.38.refs_0_.p0, ...), custom_call_target="tpu_custom_call" | custom-call | tf_op jit(solution)/shard_map/member_prefixes/pallas_call | solution.py:248
  25.5 0.7 %collective-permute-start.4 = (bf16[2,144,128]{2,1,0:T(8,128)(2,1)S(1)}, bf16[2,144,128]{2,1,0:T(8,128)(2,1)S(1)}, u32[]{:S(2)}, u32[]{:S(2)}) collective-permute-start(bf16[2,144,128]{2,1,0:T(8,128)(2,1)S(1)} %get-tuple-element.46), channel_id=1, source_target_pairs={{0,1},{1,0},{2,3},{3,2},{4,5},{5,4},{6,7},{7,6},{8,9},{9,8},{10,11... | collective-permute-start | bytes 221192 | tf_op jit(solution)/shard_map/ppermute | solution.py:368
  26.2 0.5 %collective-permute-start.5 = (bf16[2,144,128]{2,1,0:T(8,128)(2,1)S(1)}, bf16[2,144,128]{2,1,0:T(8,128)(2,1)S(1)}, u32[]{:S(2)}, u32[]{:S(2)}) collective-permute-start(bf16[2,144,128]{2,1,0:T(8,128)(2,1)S(1)} %get-tuple-element.47), channel_id=1, source_target_pairs={{0,2},{1,3},{2,0},{3,1},{4,6},{5,7},{6,4},{7,5},{8,10},{9,11},{10,... | collective-permute-start | bytes 221192 | tf_op jit(solution)/shard_map/ppermute | solution.py:368
  26.6 2.4 %collective-permute-start.6 = (bf16[2,144,128]{2,1,0:T(8,128)(2,1)S(1)}, bf16[2,144,128]{2,1,0:T(8,128)(2,1)S(1)}, u32[]{:S(2)}, u32[]{:S(2)}) collective-permute-start(bf16[2,144,128]{2,1,0:T(8,128)(2,1)S(1)} %get-tuple-element.48), channel_id=1, source_target_pairs={{0,3},{1,2},{2,1},{3,0},{4,7},{5,6},{6,5},{7,4},{8,11},{9,10},{10,... | collective-permute-start | bytes 221192 | tf_op jit(solution)/shard_map/ppermute | solution.py:368
  29.0 1.2 %inner_attention.5 = (bf16[2,1024,128]{2,1,0:T(8,128)(2,1)S(1)}, f32[2,1024,128]{2,1,0:T(8,128)S(1)}) custom-call(bf16[1024,1024]{1,0:T(8,128)(2,1)S(1)} %copy-done, bf16[8,1024,128]{2,1,0:T(8,128)(2,1)S(1)} %get-tuple-element.34.kf_ref, bf16[8,1024,128]{2,1,0:T(8,128)(2,1)S(1)} %get-tuple-element.35.vf_ref, f32[3,4,1024]{2,1,0:T(4,128)S(1)} %copy-done.1), custom_call_target="tpu_custom_call" | custom-call | flops 268435456 | bytes 3145728 | tf_op jit(solution)/shard_map/inner_attention/pallas_call | solution.py:297
  30.2 0.0 collective-permute-done.4.p1
  30.2 0.3 collective-permute-done.5.p2
  30.5 1.6 %collective-permute-done.6.p3 = bf16[2,144,128]{2,1,0:T(8,128)(2,1)S(1)} collective-permute-done((bf16[2,144,128]{2,1,0:T(8,128)(2,1)S(1)}, bf16[2,144,128]{2,1,0:T(8,128)(2,1)S(1)}, u32[]{:S(2)}, u32[]{:S(2)}) %collective-permute-start.6) | collective-permute-done | bytes 73760 | tf_op jit(solution)/shard_map/ppermute | solution.py:368
  32.2 2.9 %finish.1 = bf16[1024,1024]{1,0:T(8,128)(2,1)} custom-call(s32[2]{0:T(128)S(1)} %pad_add_fusion.m_ref, bf16[2,144,128]{2,1,0:T(8,128)(2,1)S(1)} %get-tuple-element.51.p0, bf16[2,144,128]{2,1,0:T(8,128)(2,1)S(1)} %collective-permute-done.4.p1, bf16[2,144,128]{2,1,0:T(8,128)(2,1)S(1)} %collective-permute-done.5.p2, ...), custom_call_target="tpu_custom_call" | custom-call | tf_op jit(solution)/shard_map/finish/pallas_call | solution.py:351
  (1 shorter events, 0.0 us)
Async XLA Ops:
  0.1 11.9 %copy-start = (bf16[1024,1024]{1,0:T(8,128)(2,1)S(1)}, bf16[1024,1024]{1,0:T(8,128)(2,1)}, u32[]{:S(2)}) copy-start(bf16[1024,1024]{1,0:T(8,128)(2,1)} %q_ref.5) | copy-start | bytes 6291460
  0.1 11.9 %copy-start.1 = (f32[3,4,1024]{2,1,0:T(4,128)S(1)}, f32[3,4,1024]{2,1,0:T(4,128)}, u32[]{:S(2)}) copy-start(f32[3,4,1024]{2,1,0:T(4,128)} %w_ref.7) | copy-start | bytes 147460
  7.3 6.2 %collective-permute-start = (bf16[2,160,128]{2,1,0:T(8,128)(2,1)S(1)}, bf16[2,160,128]{2,1,0:T(8,128)(2,1)S(1)}, u32[]{:S(2)}, u32[]{:S(2)}) collective-permute-start(bf16[2,160,128]{2,1,0:T(8,128)(2,1)S(1)} %get-tuple-element.63), channel_id=1, source_target_pairs={{0,1},{1,0},{2,3},{3,2},{4,5},{5,4},{6,7},{7,6},{8,9},{9,8},{10,11... | collective-permute-start | bytes 245768 | tf_op jit(solution)/shard_map/ppermute | solution.py:368
  10.4 5.1 %collective-permute-start.1 = (bf16[2,160,128]{2,1,0:T(8,128)(2,1)S(1)}, bf16[2,160,128]{2,1,0:T(8,128)(2,1)S(1)}, u32[]{:S(2)}, u32[]{:S(2)}) collective-permute-start(bf16[2,160,128]{2,1,0:T(8,128)(2,1)S(1)} %get-tuple-element.62), channel_id=1, source_target_pairs={{0,2},{1,3},{2,0},{3,1},{4,6},{5,7},{6,4},{7,5},{8,10},{9,11},{10,... | collective-permute-start | bytes 245768 | tf_op jit(solution)/shard_map/ppermute | solution.py:368
  12.0 5.3 %collective-permute-start.2 = (bf16[2,160,128]{2,1,0:T(8,128)(2,1)S(1)}, bf16[2,160,128]{2,1,0:T(8,128)(2,1)S(1)}, u32[]{:S(2)}, u32[]{:S(2)}) collective-permute-start(bf16[2,160,128]{2,1,0:T(8,128)(2,1)S(1)} %get-tuple-element.61), channel_id=1, source_target_pairs={{0,3},{1,2},{2,1},{3,0},{4,7},{5,6},{6,5},{7,4},{8,11},{9,10},{10,... | collective-permute-start | bytes 245768 | tf_op jit(solution)/shard_map/ppermute | solution.py:368
  18.1 6.2 %copy-start.2 = (f32[1024]{0:T(1024)S(1)}, f32[1024]{0:T(1024)}, u32[]{:S(2)}) copy-start(f32[1024]{0:T(1024)} %param.9) | copy-start | bytes 12292
  18.1 6.2 %collective-permute-start.3 = (bf16[2,160,128]{2,1,0:T(8,128)(2,1)S(1)}, bf16[2,160,128]{2,1,0:T(8,128)(2,1)S(1)}, u32[]{:S(2)}, u32[]{:S(2)}) collective-permute-start(bf16[2,160,128]{2,1,0:T(8,128)(2,1)S(1)} %group_total.1), channel_id=1, source_target_pairs={{0,4},{1,5},{2,6},{3,7},{4,0},{5,1},{6,2},{7,3},{8,12},{9,13},{10,... | collective-permute-start | bytes 245768 | tf_op jit(solution)/shard_map/ppermute | solution.py:368
  25.5 4.7 %collective-permute-start.4 = (bf16[2,144,128]{2,1,0:T(8,128)(2,1)S(1)}, bf16[2,144,128]{2,1,0:T(8,128)(2,1)S(1)}, u32[]{:S(2)}, u32[]{:S(2)}) collective-permute-start(bf16[2,144,128]{2,1,0:T(8,128)(2,1)S(1)} %get-tuple-element.46), channel_id=1, source_target_pairs={{0,1},{1,0},{2,3},{3,2},{4,5},{5,4},{6,7},{7,6},{8,9},{9,8},{10,11... | collective-permute-start | bytes 221192 | tf_op jit(solution)/shard_map/ppermute | solution.py:368
  26.2 4.4 %collective-permute-start.5 = (bf16[2,144,128]{2,1,0:T(8,128)(2,1)S(1)}, bf16[2,144,128]{2,1,0:T(8,128)(2,1)S(1)}, u32[]{:S(2)}, u32[]{:S(2)}) collective-permute-start(bf16[2,144,128]{2,1,0:T(8,128)(2,1)S(1)} %get-tuple-element.47), channel_id=1, source_target_pairs={{0,2},{1,3},{2,0},{3,1},{4,6},{5,7},{6,4},{7,5},{8,10},{9,11},{10,... | collective-permute-start | bytes 221192 | tf_op jit(solution)/shard_map/ppermute | solution.py:368
  26.6 5.5 %collective-permute-start.6 = (bf16[2,144,128]{2,1,0:T(8,128)(2,1)S(1)}, bf16[2,144,128]{2,1,0:T(8,128)(2,1)S(1)}, u32[]{:S(2)}, u32[]{:S(2)}) collective-permute-start(bf16[2,144,128]{2,1,0:T(8,128)(2,1)S(1)} %get-tuple-element.48), channel_id=1, source_target_pairs={{0,3},{1,2},{2,1},{3,0},{4,7},{5,6},{6,5},{7,4},{8,11},{9,10},{10,... | collective-permute-start | bytes 221192 | tf_op jit(solution)/shard_map/ppermute | solution.py:368

commit v3 on v2

--- a/solution.py
+++ b/solution.py
@@ -13,9 +13,10 @@
 ROWS = 256
 CHUNK = 256
 PIECES = (3, 3, 2)
-PARTS = 2
-AHEAD = 2
+PARTS = 8
+PAIR = 2
 AUX = 32
+TAIL = 16
 FIX = 16
 SCALE = HDIM ** (-0.5)
 F32, BF16 = jnp.float32, jnp.bfloat16
@@ -49,12 +50,22 @@
     return jnp.where(rows_iota((8, HDIM)) < 4, first, last)
 
 
-def state_kernel(m_ref, q_hbm, k_hbm, v_hbm, w_hbm, kf_ref, vf_ref, msg_ref, k_buf, v_buf, edge, w_ref, k_sem, v_sem, sem):
+def conv_from(wide, rows, taps):
+    at = lambda back: wide[rows.start + 8 - back : rows.stop + 8 - back]
+    return (taps[3:4] * at(0) + taps[2:3] * at(1)) + (taps[1:2] * at(2) + taps[0:1] * at(3))
+
+
+def state_kernel(m_ref, q_hbm, k_hbm, v_hbm, w_hbm, kf_ref, vf_ref, msg_ref, k_buf, v_buf, wide, edge, w_ref, k_sem, v_sem, sem):
     heads, tokens = k_buf.shape[0:2]
 
     def fetch(source, target, semaphore, h):
         cols = pl.ds(pl.multiple_of(h * HDIM, HDIM), HDIM)
         return pltpu.make_async_copy(source.at[:, cols], target.at[h], semaphore.at[h])
+
+    def fetch_pair(first):
+        for source, target, semaphore in ((k_hbm, k_buf, k_sem), (v_hbm, v_buf, v_sem)):
+            for u in range(PAIR):
+                fetch(source, target, semaphore, first + u).start()
 
     small = [
         pltpu.make_async_copy(w_hbm, w_ref, sem.at[0]),
@@ -62,48 +73,63 @@
         pltpu.make_async_copy(q_hbm.at[tokens - 16 : tokens], edge.at[1], sem.at[2]),
     ]
     small[0].start()
-    for h in range(AHEAD):
-        fetch(k_hbm, k_buf, k_sem, h).start()
-        fetch(v_hbm, v_buf, v_sem, h).start()
+    fetch_pair(0)
     small[1].start()
     small[2].start()
-    for copy in small:
-        copy.wait()
-
-    def one_head(h, carry):
-        @pl.when(h + AHEAD < heads)
+    for u in range(PAIR):
+        for a in range(2):
+            wide[u, a, 0:8] = jnp.zeros((8, HDIM), F32)
+    small[0].wait()
+
+    def some_heads(i, carry):
+        first = i * PAIR
+
+        @pl.when(first + PAIR < heads)
         def _():
-            fetch(k_hbm, k_buf, k_sem, h + AHEAD).start()
-            fetch(v_hbm, v_buf, v_sem, h + AHEAD).start()
-
-        fetch(k_hbm, k_buf, k_sem, h).wait()
-        fetch(v_hbm, v_buf, v_sem, h).wait()
-        cols = pl.ds(pl.multiple_of(h * HDIM, HDIM), HDIM)
-        wk = w_ref[1, :, cols] * 0.5
-        wv = w_ref[2, :, cols]
-        local = jnp.zeros((HDIM, HDIM), F32)
-        for start in range(0, tokens, ROWS):
-            rows = slice(start, start + ROWS)
-            above = slice(start - 16, start)
-            kf = silu_of_twice(conv_rows(k_buf[h, rows], k_buf[h, above] if start else None, wk))
-            if start == 0:
-                kf = jnp.where(rows_iota(kf.shape) < CONV - 1, 0.0, kf)
-            kf = kf.astype(BF16)
-            vf = conv_rows(v_buf[h, rows], v_buf[h, above] if start else None, wv).astype(BF16)
-            kf_ref[h, rows] = kf
-            vf_ref[h, rows] = vf
-            local = local + dot(kf, vf, ((0,), (0,)))
+            fetch_pair(first + PAIR)
+
+        for u in range(PAIR):
+            fetch(k_hbm, k_buf, k_sem, first + u).wait()
+        for u in range(PAIR):
+            h = first + u
+            wk = w_ref[1, :, pl.ds(pl.multiple_of(h * HDIM, HDIM), HDIM)] * 0.5
+            for start in range(0, tokens, ROWS):
+                rows = slice(start, start + ROWS)
+                wide[u, 0, start + 8 : start + 8 + ROWS] = k_buf[h, rows].astype(F32)
+                kf = silu_of_twice(conv_from(wide.at[u, 0], rows, wk))
+                if start == 0:
+                    kf = jnp.where(rows_iota(kf.shape) < CONV - 1, 0.0, kf)
+                kf_ref[h, rows] = kf.astype(BF16)
+        for u in range(PAIR):
+            fetch(v_hbm, v_buf, v_sem, first + u).wait()
+        for u in range(PAIR):
+            h = first + u
+            cols = pl.ds(pl.multiple_of(h * HDIM, HDIM), HDIM)
+            wv = w_ref[2, :, cols]
+            local = jnp.zeros((HDIM, HDIM), F32)
+            for start in range(0, tokens, ROWS):
+                rows = slice(start, start + ROWS)
+                wide[u, 1, start + 8 : start + 8 + ROWS] = v_buf[h, rows].astype(F32)
+                vf = conv_from(wide.at[u, 1], rows, wv).astype(BF16)
+                vf_ref[h, rows] = vf
+                local = local + dot(kf_ref[h, rows], vf, ((0,), (0,)))
+            per = heads // GROUP
+            place = (lax.div(h, per) ^ m_ref[0]) * per + lax.rem(h, per)
+            msg_ref[place, 0:HDIM] = local.astype(BF16)
+            mk = merged_rows(k_buf[h, 0:16], k_buf[h, tokens - 16 : tokens])
+            mv = merged_rows(v_buf[h, 0:16], v_buf[h, tokens - 16 : tokens])
+            msg_ref[place, HDIM : HDIM + 16] = jnp.concatenate([mk, mv], axis=0).astype(BF16)
+        return carry
+
+    lax.fori_loop(0, heads // PAIR, some_heads, 0)
+    small[1].wait()
+    small[2].wait()
+    for h in range(heads):
+        cols = slice(h * HDIM, (h + 1) * HDIM)
         per = heads // GROUP
-        place = (lax.div(h, per) ^ m_ref[0]) * per + lax.rem(h, per)
-        msg_ref[place, 0:HDIM] = local.astype(BF16)
-        mk = merged_rows(k_buf[h, 0:16], k_buf[h, tokens - 16 : tokens])
-        mv = merged_rows(v_buf[h, 0:16], v_buf[h, tokens - 16 : tokens])
+        place = (h // per ^ m_ref[0]) * per + h % per
         mq = merged_rows(edge[0, :, cols], edge[1, :, cols])
-        msg_ref[place, HDIM : HDIM + 16] = jnp.concatenate([mk, mv], axis=0).astype(BF16)
         msg_ref[place, HDIM + 16 : HDIM + 32] = jnp.concatenate([mq, mq], axis=0).astype(BF16)
-        return carry
-
-    lax.fori_loop(0, heads, one_head, 0)
 
 
 VMEM = pl.BlockSpec(memory_space=pltpu.VMEM)
@@ -124,6 +150,7 @@
         scratch_shapes=[
             pltpu.VMEM((heads, tokens, HDIM), BF16),
             pltpu.VMEM((heads, tokens, HDIM), BF16),
+            pltpu.VMEM((PAIR, 2, tokens + 8, HDIM), F32),
             pltpu.VMEM((2, 16, width), BF16),
             pltpu.VMEM(conv_weight.shape, F32),
             pltpu.SemaphoreType.DMA((heads,)),
@@ -160,29 +187,47 @@
         buf[m_ref[0] ^ j] = packet[...]
 
 
+def gather_edges(m_ref, packets, buf):
+    for j, packet in enumerate(packets):
+        buf[m_ref[0] ^ j] = packet[:, HDIM:]
+
+
 def total_kernel(has_tail, m_ref, *refs):
     packets, refs = refs[:GROUP], refs[GROUP:]
     if has_tail:
         tail_ref, refs = refs[0], refs[1:]
     w_ref, out_ref, buf = refs
-    gather_packets(m_ref, packets, buf)
+    gather_edges(m_ref, packets, buf)
     for h in range(out_ref.shape[0]):
         cols = slice(h * HDIM, (h + 1) * HDIM)
         before = tail_ref[h].astype(F32) if has_tail else jnp.zeros((AUX, HDIM), F32)
         kfs, vfs = [], []
-        total = jnp.zeros((HDIM, HDIM), F32)
+        total = sum(packet[h, 0:HDIM].astype(F32) for packet in packets)
         for t in range(GROUP):
-            own = buf[t, h, HDIM:].astype(F32)
+            own = buf[t, h].astype(F32)
             kf, vf = edge_kv(own, before, w_ref, cols)
             kfs.append(kf)
             vfs.append(vf)
             before = own
-            total = total + buf[t, h, 0:HDIM].astype(F32)
         kf = jnp.concatenate(kfs, axis=0).astype(BF16)
         vf = jnp.concatenate(vfs, axis=0).astype(BF16)
         total = total + dot(kf, vf, ((0,), (0,)))
         out_ref[h, 0:HDIM] = total.astype(BF16)
-        out_ref[h, HDIM:] = buf[GROUP - 1, h, HDIM:]
+        out_ref[h, HDIM:] = pack_tail(before).astype(BF16)
+
+
+def pack_tail(raw):
+    k = jnp.where(rows_iota((8, HDIM)) < 4, pltpu.roll(raw[16:24], 3, 0), raw[0:8])
+    return jnp.concatenate([k, raw[8:16]], axis=0)
+
+
+def unpack_tail(tail):
+    q = pltpu.roll(tail[0:8], 5, 0)
+    return jnp.concatenate([tail, q, q], axis=0)
+
+
+def whole(a):
+    return pl.BlockSpec(a.shape, lambda i, m: (0,) * len(a.shape))
 
 
 def packet_specs(heads, rows):
@@ -201,47 +246,93 @@
             in_specs=packet_specs(heads, HDIM + AUX)
             + [pl.BlockSpec((heads, AUX, HDIM), lambda i, m: (0, 0, 0))] * len(tails)
             + [pl.BlockSpec((3, CONV, quarter), lambda i, m: (0, 0, m[0]))],
-            out_specs=pl.BlockSpec((heads, HDIM + AUX, HDIM), lambda i, m: (0, 0, 0)),
-            scratch_shapes=[pltpu.VMEM((GROUP, heads, HDIM + AUX, HDIM), BF16)],
+            out_specs=pl.BlockSpec((heads, HDIM + TAIL, HDIM), lambda i, m: (0, 0, 0)),
+            scratch_shapes=[pltpu.VMEM((GROUP, heads, AUX, HDIM), BF16)],
         ),
-        out_shape=jax.ShapeDtypeStruct((heads, HDIM + AUX, HDIM), BF16),
+        out_shape=jax.ShapeDtypeStruct((heads, HDIM + TAIL, HDIM), BF16),
         compiler_params=pltpu.CompilerParams(vmem_limit_bytes=8 << 20),
         name="group_total",
     )(m, *packets, *tails, conv_weight)
 
 
-def prefix_kernel(m_ref, p0, p1, p2, p3, x_ref, w_ref, gain_ref, o0, o1, o2, o3, buf, out):
+def edge_features(own, before, w_ref, cols):
+    kf, vf = edge_kv(own, before, w_ref, cols)
+    qf = silu_of_twice(edge_rows(own[16:24], before[16:24], w_ref[0, :, cols] * 0.5)) * SCALE
+    blank = jnp.zeros((8, HDIM), F32)
+    qf, kf, vf = (jnp.concatenate([a, blank], axis=0).astype(BF16) for a in (edge_only(qf), kf, vf))
+    scores = dot(qf, kf, ((1,), (1,)))
+    causal = rows_iota(scores.shape) >= lax.broadcasted_iota(jnp.int32, scores.shape, 1)
+    scores = jnp.where(causal, scores, 0.0).astype(BF16)
+    return qf, dot(scores, vf, ((1,), (0,))), dot(kf, vf, ((0,), (0,)))
+
+
+def edges_kernel(m_ref, p0, p1, p2, p3, w_ref, qf_ref, inner_ref, before_ref, with_ref, first_ref, buf):
     gather_packets(m_ref, (p0, p1, p2, p3), buf)
+    for h in range(p0.shape[0]):
+        cols = slice(h * HDIM, (h + 1) * HDIM)
+        first_ref[h] = buf[0, h, HDIM:]
+        state = buf[0, h, 0:HDIM].astype(F32)
+        for t in range(1, GROUP):
+            own, before = buf[t, h, HDIM:].astype(F32), buf[t - 1, h, HDIM:].astype(F32)
+            qf, inner, first = edge_features(own, before, w_ref, cols)
+            qf_ref[t - 1, h] = qf
+            inner_ref[t - 1, h] = inner
+            before_ref[t - 1, h] = state
+            state = state + first
+            with_ref[t - 1, h] = state
+            state = state + buf[t, h, 0:HDIM].astype(F32)
+
+
+def member_edges(m, packets, conv_weight):
+    quarter = conv_weight.shape[2] // GROUP
+    heads = quarter // HDIM
+    shapes = [
+        jax.ShapeDtypeStruct((GROUP - 1, heads, 16, HDIM), BF16),
+        jax.ShapeDtypeStruct((GROUP - 1, heads, 16, HDIM), F32),
+        jax.ShapeDtypeStruct((GROUP - 1, heads, HDIM, HDIM), F32),
+        jax.ShapeDtypeStruct((GROUP - 1, heads, HDIM, HDIM), F32),
+        jax.ShapeDtypeStruct((heads, AUX, HDIM), BF16),
+    ]
+    return pl.pallas_call(
+        edges_kernel,
+        grid_spec=pltpu.PrefetchScalarGridSpec(
+            num_scalar_prefetch=1,
+            grid=(1,),
+            in_specs=packet_specs(heads, HDIM + AUX) + [pl.BlockSpec((3, CONV, quarter), lambda i, m: (0, 0, m[0]))],
+            out_specs=[whole(s) for s in shapes],
+            scratch_shapes=[pltpu.VMEM((GROUP, heads, HDIM + AUX, HDIM), BF16)],
+        ),
+        out_shape=shapes,
+        compiler_params=pltpu.CompilerParams(vmem_limit_bytes=8 << 20),
+        name="member_edges",
+    )(m, *packets, conv_weight)
+
+
+def prefix_kernel(m_ref, qf_ref, inner_ref, before_ref, with_ref, first_ref, x_ref, w_ref, gain_ref, o0, o1, o2, o3, out):
     later = (m_ref[1] > 0).astype(F32)
-    heads = x_ref.shape[0]
-    for h in range(heads):
+    blank = jnp.zeros((8, HDIM), F32)
+    for h in range(x_ref.shape[0]):
         cols = slice(h * HDIM, (h + 1) * HDIM)
-        gain = gain_ref[:, cols]
-        prefix = x_ref[h, 0:HDIM].astype(F32) * later
-        before = x_ref[h, HDIM:].astype(F32) * later
+        base = x_ref[h, 0:HDIM].astype(F32) * later
+        tail = unpack_tail(x_ref[h, HDIM:].astype(F32) * later)
+        qf, inner, first = edge_features(first_ref[h].astype(F32), tail, w_ref, cols)
+        prefix = base
+        base = base + first
+        shifted = base
         for t in range(GROUP):
-            own = buf[t, h, HDIM:].astype(F32)
-            kf, vf = edge_kv(own, before, w_ref, cols)
-            qf = silu_of_twice(edge_rows(own[16:24], before[16:24], w_ref[0, :, cols] * 0.5)) * SCALE
-            blank = jnp.zeros((8, HDIM), F32)
-            kf = jnp.concatenate([kf, blank], axis=0).astype(BF16)
-            vf = jnp.concatenate([vf, blank], axis=0).astype(BF16)
-            qf = jnp.concatenate([edge_only(qf), blank], axis=0).astype(BF16)
-            scores = dot(qf, kf, ((1,), (1,)))
-            causal = rows_iota(scores.shape) >= lax.broadcasted_iota(jnp.int32, scores.shape, 1)
-            scores = jnp.where(causal, scores, 0.0).astype(BF16)
-            o = dot(scores, vf, ((1,), (0,))) + dot(qf, prefix.astype(BF16), ((1,), (0,)))
-            o = o * lax.rsqrt(jnp.mean(o * o, axis=1, keepdims=True) + 1e-06) * gain
-            shifted = prefix + dot(kf, vf, ((0,), (0,)))
+            if t:
+                qf, inner = qf_ref[t - 1, h], inner_ref[t - 1, h]
+                prefix = base + before_ref[t - 1, h]
+                shifted = base + with_ref[t - 1, h]
+            o = inner + dot(qf, prefix.astype(BF16), ((1,), (0,)))
+            o = o * lax.rsqrt(jnp.mean(o * o, axis=1, keepdims=True) + 1e-06) * gain_ref[:, cols]
             out[t, h, 0:HDIM] = shifted.astype(BF16)
             out[t, h, HDIM:] = jnp.concatenate([pltpu.roll(o[0:8], 5, 0), blank], axis=0).astype(BF16)
-            prefix = shifted + buf[t, h, 0:HDIM].astype(F32)
-            before = own
     for j, o_ref in enumerate((o0, o1, o2, o3)):
         o_ref[...] = out[m_ref[0] ^ j]
 
 
-def member_prefixes(m, packets, incoming, conv_weight, gain):
+def member_prefixes(m, edges, incoming, conv_weight, gain):
     quarter = conv_weight.shape[2] // GROUP
     heads = quarter // HDIM
     out = jax.ShapeDtypeStruct((heads, HDIM + FIX, HDIM), BF16)
@@ -250,22 +341,19 @@
         grid_spec=pltpu.PrefetchScalarGridSpec(
             num_scalar_prefetch=1,
             grid=(1,),
-            in_specs=packet_specs(heads, HDIM + AUX)
+            in_specs=[whole(a) for a in edges]
             + [
-                pl.BlockSpec((heads, HDIM + AUX, HDIM), lambda i, m: (0, 0, 0)),
+                whole(incoming),
                 pl.BlockSpec((3, CONV, quarter), lambda i, m: (0, 0, m[0])),
                 pl.BlockSpec((1, quarter), lambda i, m: (0, m[0])),
             ],
             out_specs=packet_specs(heads, HDIM + FIX),
-            scratch_shapes=[
-                pltpu.VMEM((GROUP, heads, HDIM + AUX, HDIM), BF16),
-                pltpu.VMEM((GROUP, heads, HDIM + FIX, HDIM), BF16),
-            ],
+            scratch_shapes=[pltpu.VMEM((GROUP, heads, HDIM + FIX, HDIM), BF16)],
         ),
         out_shape=[out] * GROUP,
         compiler_params=pltpu.CompilerParams(vmem_limit_bytes=8 << 20),
         name="member_prefixes",
-    )(m, *packets, incoming, conv_weight, gain)
+    )(m, *edges, incoming, conv_weight, gain)
 
 
 def inner_kernel(first, q_ref, kf_ref, vf_ref, w_ref, qf_ref, inner_ref):
@@ -403,13 +491,15 @@
         last = jnp.stack(packets)[m[0] ^ (GROUP - 1)][:, HDIM:]
         tail = to_next_group(last)
         total = group_total(m, packets, tail, conv_weight)[:, 0:HDIM].astype(F32)
+        tail = jnp.concatenate([tail[:, 21:24], tail[:, 3:16]], axis=1)
         prefix, passed = jnp.zeros_like(total), total
         for _ in range(groups - 1):
             prefix = to_next_group(passed)
             passed = prefix + total
         incoming = jnp.concatenate([prefix.astype(BF16), tail], axis=1)
-    incoming = beside(1, incoming)
-    sends = member_prefixes(m, packets, incoming, conv_weight, gain)
+    edges = member_edges(m, packets, conv_weight)
+    incoming, edges = beside(1, (incoming, edges))
+    sends = member_prefixes(m, edges, incoming, conv_weight, gain)
     prefixes = [sends[0]] + [swapped(sends[j], j) for j in range(1, GROUP)]
     prefixes = beside(2, prefixes)
     return finish(m, prefixes, qfs, inners, gain)

time: 35.2 us -> 33.9 us (0.963)
  waiting for transfers between devices: 7.7 us -> 6.37 us
    ppermute x7, waiting for transfers between devices: 7.7 us -> 6.37 us  [swapped(): return lax.ppermute(value, 'ctx', [(s, s ^ bits) for s in range(count)])]
    pallas_call x0 -> x1, Pallas kernels: none -> 1.15 us  [member_edges(): pl.pallas_call(edges_kernel, grid_spec=pltpu.PrefetchScalarGridSpec(num_s...]
    pallas_call x1, Pallas kernels: 7.22 us -> 6.28 us  [block_states(): pl.pallas_call(state_kernel, in_specs=[SMEM, HBM, HBM, HBM, HBM], out_spe...]
  transfers between devices with their start and end apart: 7 -> 7, of which waited for: 5 -> 5; matrix products, arithmetic and copies ran while one was open for 0% -> 0% of each run, Pallas kernels for 12% -> 16%
where the time goes in v3:
time: 33.9 us; the launch traced here: 33.8 us
  Pallas kernels  16.4 us (48%)
  starting transfers between devices  10.8 us (32%)
  waiting for transfers between devices  6.37 us (19%)
    ppermute x7, starting transfers between devices, swapped(): return lax.ppermute(value, 'ctx', [(s, s ^ bits) for s in range(count)])  10.8 us
    ppermute x7, waiting for transfers between devices, swapped(): return lax.ppermute(value, 'ctx', [(s, s ^ bits) for s in range(count)])  6.37 us
    pallas_call x1, Pallas kernels, block_states(): pl.pallas_call(state_kernel, in_specs=[SMEM, HBM, HBM, HBM, HBM], out_spe...  6.28 us
    pallas_call x3, Pallas kernels, inner_attention(): pl.pallas_call(functools.partial(inner_kernel, first), in_specs=[VMEM] *...  4.28 us
    pallas_call x1, Pallas kernels, finish(): pl.pallas_call(functools.partial(finish_kernel, len(qfs)), in_specs=[SMEM...  2.74 us
    pallas_call x1, Pallas kernels, member_prefixes(): pl.pallas_call(prefix_kernel, grid_spec=pltpu.PrefetchScalarGridSpec(num_...  1.15 us
    pallas_call x1, Pallas kernels, member_edges(): pl.pallas_call(edges_kernel, grid_spec=pltpu.PrefetchScalarGridSpec(num_s...  1.15 us
    pallas_call x1, Pallas kernels, group_total(): pl.pallas_call(functools.partial(total_kernel, tail is not None), grid_sp...  0.77 us
  transfers between devices with their start and end apart: 7, of which 5 were waited for; matrix products, arithmetic and copies ran while one was open for 0% of the time, Pallas kernels for 16%

profile of v3, /device:TPU:0, one launch (start us, length us, event | category | flops | bytes accessed | tf_op | source)
XLA Modules:
  0.0 33.8 jit_solution(5720781303664648320)
XLA Ops:
  0.0 0.1 pad_add_fusion.m_ref
  0.1 0.0 copy-start
  0.1 0.0 copy-start.1
  0.1 6.3 %block_states.1 = (bf16[8,1024,128]{2,1,0:T(8,128)(2,1)S(1)}, bf16[8,1024,128]{2,1,0:T(8,128)(2,1)S(1)}, bf16[8,160,128]{2,1,0:T(8,128)(2,1)S(1)}) custom-call(s32[2]{0:T(128)S(1)} %pad_add_fusion.m_ref, bf16[1024,1024]{1,0:T(8,128)(2,1)} %q_ref.5, bf16[1024,1024]{1,0:T(8,128)(2,1)} %k_hbm.1, bf16[1024,1024]{1,0:T(8,128)(2,1)} %v_hbm.1, f32[3,4,1024]{2,1,0:T(4,128)} %w_ref.9), custom_call_target="tpu_custom_call" | custom-call | flops 268435456 | bytes 8388608 | tf_op jit(solution)/shard_map/block_states/pallas_call | solution.py:145
  6.4 3.0 %collective-permute-start = (bf16[2,160,128]{2,1,0:T(8,128)(2,1)S(1)}, bf16[2,160,128]{2,1,0:T(8,128)(2,1)S(1)}, u32[]{:S(2)}, u32[]{:S(2)}) collective-permute-start(bf16[2,160,128]{2,1,0:T(8,128)(2,1)S(1)} %get-tuple-element.83), channel_id=1, source_target_pairs={{0,1},{1,0},{2,3},{3,2},{4,5},{5,4},{6,7},{7,6},{8,9},{9,8},{10,11... | collective-permute-start | bytes 245768 | tf_op jit(solution)/shard_map/ppermute | solution.py:456
  9.4 1.6 %collective-permute-start.1 = (bf16[2,160,128]{2,1,0:T(8,128)(2,1)S(1)}, bf16[2,160,128]{2,1,0:T(8,128)(2,1)S(1)}, u32[]{:S(2)}, u32[]{:S(2)}) collective-permute-start(bf16[2,160,128]{2,1,0:T(8,128)(2,1)S(1)} %get-tuple-element.82), channel_id=1, source_target_pairs={{0,2},{1,3},{2,0},{3,1},{4,6},{5,7},{6,4},{7,5},{8,10},{9,11},{10,... | collective-permute-start | bytes 245768 | tf_op jit(solution)/shard_map/ppermute | solution.py:456
  11.0 0.0 collective-permute-start.2
  11.0 0.0 copy-done
  11.0 0.0 copy-done.1
  11.0 1.6 %inner_attention.3 = (bf16[3,1024,128]{2,1,0:T(8,128)(2,1)S(1)}, f32[3,1024,128]{2,1,0:T(8,128)S(1)}) custom-call(bf16[1024,1024]{1,0:T(8,128)(2,1)S(1)} %copy-done, bf16[8,1024,128]{2,1,0:T(8,128)(2,1)S(1)} %get-tuple-element.44.kf_ref, bf16[8,1024,128]{2,1,0:T(8,128)(2,1)S(1)} %get-tuple-element.45.vf_ref, f32[3,4,1024]{2,1,0:T(4,128)S(1)} %copy-done.1), custom_call_target="tpu_custom_call" | custom-call | flops 402653184 | bytes 4718592 | tf_op jit(solution)/shard_map/inner_attention/pallas_call | solution.py:385
  12.6 0.0 collective-permute-done.refs_1_.p1
  12.6 2.0 %collective-permute-done.1.refs_2_.p2 = bf16[2,160,128]{2,1,0:T(8,128)(2,1)S(1)} collective-permute-done((bf16[2,160,128]{2,1,0:T(8,128)(2,1)S(1)}, bf16[2,160,128]{2,1,0:T(8,128)(2,1)S(1)}, u32[]{:S(2)}, u32[]{:S(2)}) %collective-permute-start.1) | collective-permute-done | bytes 81952 | tf_op jit(solution)/shard_map/ppermute | solution.py:456
  14.6 1.8 %collective-permute-done.2.refs_3_.p3 = bf16[2,160,128]{2,1,0:T(8,128)(2,1)S(1)} collective-permute-done((bf16[2,160,128]{2,1,0:T(8,128)(2,1)S(1)}, bf16[2,160,128]{2,1,0:T(8,128)(2,1)S(1)}, u32[]{:S(2)}, u32[]{:S(2)}) %collective-permute-start.2) | collective-permute-done | bytes 81952 | tf_op jit(solution)/shard_map/ppermute | solution.py:456
  16.4 0.8 %group_total.1 = bf16[2,144,128]{2,1,0:T(8,128)(2,1)S(1)} custom-call(s32[2]{0:T(128)S(1)} %pad_add_fusion.m_ref, bf16[2,160,128]{2,1,0:T(8,128)(2,1)S(1)} %get-tuple-element.48.refs_0_.p0, bf16[2,160,128]{2,1,0:T(8,128)(2,1)S(1)} %collective-permute-done.refs_1_.p1, bf16[2,160,128]{2,1,0:T(8,128)(2,1)S(1)} %collective-permute-done.1.refs_2_.p2, ...), custom_call_target="tpu_custom_call" | custom-call | tf_op jit(solution)/shard_map/group_total/pallas_call | solution.py:241
  17.1 0.0 copy-start.2
  17.1 2.7 %collective-permute-start.3 = (bf16[2,144,128]{2,1,0:T(8,128)(2,1)S(1)}, bf16[2,144,128]{2,1,0:T(8,128)(2,1)S(1)}, u32[]{:S(2)}, u32[]{:S(2)}) collective-permute-start(bf16[2,144,128]{2,1,0:T(8,128)(2,1)S(1)} %group_total.1), channel_id=1, source_target_pairs={{0,4},{1,5},{2,6},{3,7},{4,0},{5,1},{6,2},{7,3},{8,12},{9,13},{10,... | collective-permute-start | bytes 221192 | tf_op jit(solution)/shard_map/ppermute | solution.py:456
  19.8 1.6 %inner_attention.4 = (bf16[3,1024,128]{2,1,0:T(8,128)(2,1)S(1)}, f32[3,1024,128]{2,1,0:T(8,128)S(1)}) custom-call(bf16[1024,1024]{1,0:T(8,128)(2,1)S(1)} %copy-done, bf16[8,1024,128]{2,1,0:T(8,128)(2,1)S(1)} %get-tuple-element.44.kf_ref, bf16[8,1024,128]{2,1,0:T(8,128)(2,1)S(1)} %get-tuple-element.45.vf_ref, f32[3,4,1024]{2,1,0:T(4,128)S(1)} %copy-done.1), custom_call_target="tpu_custom_call" | custom-call | flops 402653184 | bytes 4718592 | tf_op jit(solution)/shard_map/inner_attention/pallas_call | solution.py:385
  21.4 1.1 %member_edges.1 = (bf16[3,2,16,128]{3,2,1,0:T(8,128)(2,1)S(1)}, f32[3,2,16,128]{3,2,1,0:T(8,128)S(1)}, f32[3,2,128,128]{3,2,1,0:T(8,128)S(1)}, f32[3,2,128,128]{3,2,1,0:T(8,128)S(1)}, bf16[2,32,128]{2,1,0:T(8,128)(2,1)S(1)}) custom-call(s32[2]{0:T(128)S(1)} %pad_add_fusion.m_ref, bf16[2,160,128]{2,1,0:T(8,128)(2,1)S(1)} %get-tuple-element.48.refs_0_.p0, ...), custom_call_target="tpu_custom_call" | custom-call | tf_op jit(solution)/shard_map/member_edges/pallas_call | solution.py:296
  22.5 0.7 %collective-permute-done.3.x_ref = bf16[2,144,128]{2,1,0:T(8,128)(2,1)S(1)} collective-permute-done((bf16[2,144,128]{2,1,0:T(8,128)(2,1)S(1)}, bf16[2,144,128]{2,1,0:T(8,128)(2,1)S(1)}, u32[]{:S(2)}, u32[]{:S(2)}) %collective-permute-start.3) | collective-permute-done | bytes 73760 | tf_op jit(solution)/shard_map/ppermute | solution.py:456
  23.2 0.0 copy-done.2
  23.2 1.2 %member_prefixes.1 = (bf16[2,144,128]{2,1,0:T(8,128)(2,1)S(1)}, bf16[2,144,128]{2,1,0:T(8,128)(2,1)S(1)}, bf16[2,144,128]{2,1,0:T(8,128)(2,1)S(1)}, bf16[2,144,128]{2,1,0:T(8,128)(2,1)S(1)}) custom-call(s32[2]{0:T(128)S(1)} %pad_add_fusion.m_ref, bf16[3,2,16,128]{3,2,1,0:T(8,128)(2,1)S(1)} %get-tuple-element.59.qf_ref, ...), custom_call_target="tpu_custom_call" | custom-call | tf_op jit(solution)/shard_map/member_prefixes/pallas_call | solution.py:339
  24.4 0.7 %collective-permute-start.4 = (bf16[2,144,128]{2,1,0:T(8,128)(2,1)S(1)}, bf16[2,144,128]{2,1,0:T(8,128)(2,1)S(1)}, u32[]{:S(2)}, u32[]{:S(2)}) collective-permute-start(bf16[2,144,128]{2,1,0:T(8,128)(2,1)S(1)} %get-tuple-element.66), channel_id=1, source_target_pairs={{0,1},{1,0},{2,3},{3,2},{4,5},{5,4},{6,7},{7,6},{8,9},{9,8},{10,11... | collective-permute-start | bytes 221192 | tf_op jit(solution)/shard_map/ppermute | solution.py:456
  25.0 0.5 %collective-permute-start.5 = (bf16[2,144,128]{2,1,0:T(8,128)(2,1)S(1)}, bf16[2,144,128]{2,1,0:T(8,128)(2,1)S(1)}, u32[]{:S(2)}, u32[]{:S(2)}) collective-permute-start(bf16[2,144,128]{2,1,0:T(8,128)(2,1)S(1)} %get-tuple-element.67), channel_id=1, source_target_pairs={{0,2},{1,3},{2,0},{3,1},{4,6},{5,7},{6,4},{7,5},{8,10},{9,11},{10,... | collective-permute-start | bytes 221192 | tf_op jit(solution)/shard_map/ppermute | solution.py:456
  25.6 2.3 %collective-permute-start.6 = (bf16[2,144,128]{2,1,0:T(8,128)(2,1)S(1)}, bf16[2,144,128]{2,1,0:T(8,128)(2,1)S(1)}, u32[]{:S(2)}, u32[]{:S(2)}) collective-permute-start(bf16[2,144,128]{2,1,0:T(8,128)(2,1)S(1)} %get-tuple-element.68), channel_id=1, source_target_pairs={{0,3},{1,2},{2,1},{3,0},{4,7},{5,6},{6,5},{7,4},{8,11},{9,10},{10,... | collective-permute-start | bytes 221192 | tf_op jit(solution)/shard_map/ppermute | solution.py:456
  27.9 1.2 %inner_attention.5 = (bf16[2,1024,128]{2,1,0:T(8,128)(2,1)S(1)}, f32[2,1024,128]{2,1,0:T(8,128)S(1)}) custom-call(bf16[1024,1024]{1,0:T(8,128)(2,1)S(1)} %copy-done, bf16[8,1024,128]{2,1,0:T(8,128)(2,1)S(1)} %get-tuple-element.44.kf_ref, bf16[8,1024,128]{2,1,0:T(8,128)(2,1)S(1)} %get-tuple-element.45.vf_ref, f32[3,4,1024]{2,1,0:T(4,128)S(1)} %copy-done.1), custom_call_target="tpu_custom_call" | custom-call | flops 268435456 | bytes 3145728 | tf_op jit(solution)/shard_map/inner_attention/pallas_call | solution.py:385
  29.1 0.0 collective-permute-done.4.p1
  29.1 0.3 collective-permute-done.5.p2
  29.4 1.6 %collective-permute-done.6.p3 = bf16[2,144,128]{2,1,0:T(8,128)(2,1)S(1)} collective-permute-done((bf16[2,144,128]{2,1,0:T(8,128)(2,1)S(1)}, bf16[2,144,128]{2,1,0:T(8,128)(2,1)S(1)}, u32[]{:S(2)}, u32[]{:S(2)}) %collective-permute-start.6) | collective-permute-done | bytes 73760 | tf_op jit(solution)/shard_map/ppermute | solution.py:456
  31.0 2.7 %finish.1 = bf16[1024,1024]{1,0:T(8,128)(2,1)} custom-call(s32[2]{0:T(128)S(1)} %pad_add_fusion.m_ref, bf16[2,144,128]{2,1,0:T(8,128)(2,1)S(1)} %get-tuple-element.71.p0, bf16[2,144,128]{2,1,0:T(8,128)(2,1)S(1)} %collective-permute-done.4.p1, bf16[2,144,128]{2,1,0:T(8,128)(2,1)S(1)} %collective-permute-done.5.p2, ...), custom_call_target="tpu_custom_call" | custom-call | tf_op jit(solution)/shard_map/finish/pallas_call | solution.py:439
  (1 shorter events, 0.0 us)
Async XLA Ops:
  0.1 10.9 %copy-start = (bf16[1024,1024]{1,0:T(8,128)(2,1)S(1)}, bf16[1024,1024]{1,0:T(8,128)(2,1)}, u32[]{:S(2)}) copy-start(bf16[1024,1024]{1,0:T(8,128)(2,1)} %q_ref.5) | copy-start | bytes 6291460
  0.1 10.9 %copy-start.1 = (f32[3,4,1024]{2,1,0:T(4,128)S(1)}, f32[3,4,1024]{2,1,0:T(4,128)}, u32[]{:S(2)}) copy-start(f32[3,4,1024]{2,1,0:T(4,128)} %w_ref.9) | copy-start | bytes 147460
  6.4 6.2 %collective-permute-start = (bf16[2,160,128]{2,1,0:T(8,128)(2,1)S(1)}, bf16[2,160,128]{2,1,0:T(8,128)(2,1)S(1)}, u32[]{:S(2)}, u32[]{:S(2)}) collective-permute-start(bf16[2,160,128]{2,1,0:T(8,128)(2,1)S(1)} %get-tuple-element.83), channel_id=1, source_target_pairs={{0,1},{1,0},{2,3},{3,2},{4,5},{5,4},{6,7},{7,6},{8,9},{9,8},{10,11... | collective-permute-start | bytes 245768 | tf_op jit(solution)/shard_map/ppermute | solution.py:456
  9.4 5.1 %collective-permute-start.1 = (bf16[2,160,128]{2,1,0:T(8,128)(2,1)S(1)}, bf16[2,160,128]{2,1,0:T(8,128)(2,1)S(1)}, u32[]{:S(2)}, u32[]{:S(2)}) collective-permute-start(bf16[2,160,128]{2,1,0:T(8,128)(2,1)S(1)} %get-tuple-element.82), channel_id=1, source_target_pairs={{0,2},{1,3},{2,0},{3,1},{4,6},{5,7},{6,4},{7,5},{8,10},{9,11},{10,... | collective-permute-start | bytes 245768 | tf_op jit(solution)/shard_map/ppermute | solution.py:456
  11.0 5.3 %collective-permute-start.2 = (bf16[2,160,128]{2,1,0:T(8,128)(2,1)S(1)}, bf16[2,160,128]{2,1,0:T(8,128)(2,1)S(1)}, u32[]{:S(2)}, u32[]{:S(2)}) collective-permute-start(bf16[2,160,128]{2,1,0:T(8,128)(2,1)S(1)} %get-tuple-element.81), channel_id=1, source_target_pairs={{0,3},{1,2},{2,1},{3,0},{4,7},{5,6},{6,5},{7,4},{8,11},{9,10},{10,... | collective-permute-start | bytes 245768 | tf_op jit(solution)/shard_map/ppermute | solution.py:456
  17.1 6.1 %copy-start.2 = (f32[1024]{0:T(1024)S(1)}, f32[1024]{0:T(1024)}, u32[]{:S(2)}) copy-start(f32[1024]{0:T(1024)} %param.9) | copy-start | bytes 12292
  17.1 6.1 %collective-permute-start.3 = (bf16[2,144,128]{2,1,0:T(8,128)(2,1)S(1)}, bf16[2,144,128]{2,1,0:T(8,128)(2,1)S(1)}, u32[]{:S(2)}, u32[]{:S(2)}) collective-permute-start(bf16[2,144,128]{2,1,0:T(8,128)(2,1)S(1)} %group_total.1), channel_id=1, source_target_pairs={{0,4},{1,5},{2,6},{3,7},{4,0},{5,1},{6,2},{7,3},{8,12},{9,13},{10,... | collective-permute-start | bytes 221192 | tf_op jit(solution)/shard_map/ppermute | solution.py:456
  24.4 4.7 %collective-permute-start.4 = (bf16[2,144,128]{2,1,0:T(8,128)(2,1)S(1)}, bf16[2,144,128]{2,1,0:T(8,128)(2,1)S(1)}, u32[]{:S(2)}, u32[]{:S(2)}) collective-permute-start(bf16[2,144,128]{2,1,0:T(8,128)(2,1)S(1)} %get-tuple-element.66), channel_id=1, source_target_pairs={{0,1},{1,0},{2,3},{3,2},{4,5},{5,4},{6,7},{7,6},{8,9},{9,8},{10,11... | collective-permute-start | bytes 221192 | tf_op jit(solution)/shard_map/ppermute | solution.py:456
  25.0 4.4 %collective-permute-start.5 = (bf16[2,144,128]{2,1,0:T(8,128)(2,1)S(1)}, bf16[2,144,128]{2,1,0:T(8,128)(2,1)S(1)}, u32[]{:S(2)}, u32[]{:S(2)}) collective-permute-start(bf16[2,144,128]{2,1,0:T(8,128)(2,1)S(1)} %get-tuple-element.67), channel_id=1, source_target_pairs={{0,2},{1,3},{2,0},{3,1},{4,6},{5,7},{6,4},{7,5},{8,10},{9,11},{10,... | collective-permute-start | bytes 221192 | tf_op jit(solution)/shard_map/ppermute | solution.py:456
  25.6 5.5 %collective-permute-start.6 = (bf16[2,144,128]{2,1,0:T(8,128)(2,1)S(1)}, bf16[2,144,128]{2,1,0:T(8,128)(2,1)S(1)}, u32[]{:S(2)}, u32[]{:S(2)}) collective-permute-start(bf16[2,144,128]{2,1,0:T(8,128)(2,1)S(1)} %get-tuple-element.68), channel_id=1, source_target_pairs={{0,3},{1,2},{2,1},{3,0},{4,7},{5,6},{6,5},{7,4},{8,11},{9,10},{10,... | collective-permute-start | bytes 221192 | tf_op jit(solution)/shard_map/ppermute | solution.py:456

commit v4 on v3

v4 whole, which is shorter than its diff:
```python
import functools

import jax
import jax.numpy as jnp
from jax import lax
from jax.experimental import pallas as pl
from jax.experimental.pallas import tpu as pltpu
from jax.sharding import PartitionSpec as P

HDIM = 128
CONV = 4
GROUP = 4
ROWS = 256
CHUNK = 256
PARTS = 4
PAIR = 2
AUX = 32
TAIL = 16
FIX = 16
SCALE = HDIM ** (-0.5)
F32, BF16 = jnp.float32, jnp.bfloat16


def rows_iota(shape):
    return lax.broadcasted_iota(jnp.int32, shape, 0)


def dot(a, b, dims):
    return lax.dot_general(a, b, (dims, ((), ())), preferred_element_type=F32)


def conv_rows(x, earlier, taps):
    x = x.astype(F32)
    earlier = jnp.zeros((8, HDIM), F32) if earlier is None else earlier.astype(F32)[8:16]
    x = jnp.concatenate([earlier, x], axis=0)
    x1 = pltpu.roll(x, 1, 0)
    late = taps[3:4] * x + taps[2:3] * x1
    early = taps[1:2] * x + taps[0:1] * x1
    return (late + pltpu.roll(early, 2, 0))[8:]


def silu_of_twice(half):
    return half + half * jnp.tanh(half)


def merged_rows(first16, last16):
    first = first16.astype(F32)[0:8]
    last = last16.astype(F32)[8:16]
    return jnp.where(rows_iota((8, HDIM)) < 4, first, last)


def conv_from(wide, rows, taps):
    at = lambda back: wide[rows.start + 8 - back : rows.stop + 8 - back]
    return (taps[3:4] * at(0) + taps[2:3] * at(1)) + (taps[1:2] * at(2) + taps[0:1] * at(3))


def state_kernel(m_ref, q_hbm, k_hbm, v_hbm, w_hbm, kf_ref, vf_ref, msg_ref, q_ref, w_ref, k_buf, v_buf, wide, k_sem, v_sem, sem):
    heads, tokens = k_buf.shape[0:2]

    def fetch(source, target, semaphore, h):
        cols = pl.ds(pl.multiple_of(h * HDIM, HDIM), HDIM)
        return pltpu.make_async_copy(source.at[:, cols], target.at[h], semaphore.at[h])

    def fetch_pair(first):
        for source, target, semaphore in ((k_hbm, k_buf, k_sem), (v_hbm, v_buf, v_sem)):
            for u in range(PAIR):
                fetch(source, target, semaphore, first + u).start()

    fetch_taps = pltpu.make_async_copy(w_hbm, w_ref, sem.at[0])
    fetch_queries = pltpu.make_async_copy(q_hbm, q_ref, sem.at[1])
    fetch_taps.start()
    fetch_pair(0)
    for u in range(PAIR):
        for a in range(2):
            wide[u, a, 0:8] = jnp.zeros((8, HDIM), F32)
    fetch_taps.wait()

    def some_heads(i, carry):
        first = i * PAIR

        @pl.when(first + PAIR < heads)
        def _():
            fetch_pair(first + PAIR)

        @pl.when(first + 2 * PAIR == heads)
        def _():
            fetch_queries.start()

        for u in range(PAIR):
            fetch(k_hbm, k_buf, k_sem, first + u).wait()
        for u in range(PAIR):
            h = first + u
            wk = w_ref[1, :, pl.ds(pl.multiple_of(h * HDIM, HDIM), HDIM)] * 0.5
            for start in range(0, tokens, ROWS):
                rows = slice(start, start + ROWS)
                wide[u, 0, start + 8 : start + 8 + ROWS] = k_buf[h, rows].astype(F32)
                kf = silu_of_twice(conv_from(wide.at[u, 0], rows, wk))
                if start == 0:
                    kf = jnp.where(rows_iota(kf.shape) < CONV - 1, 0.0, kf)
                kf_ref[h, rows] = kf.astype(BF16)
        for u in range(PAIR):
            fetch(v_hbm, v_buf, v_sem, first + u).wait()
        for u in range(PAIR):
            h = first + u
            cols = pl.ds(pl.multiple_of(h * HDIM, HDIM), HDIM)
            wv = w_ref[2, :, cols]
            local = jnp.zeros((HDIM, HDIM), F32)
            for start in range(0, tokens, ROWS):
                rows = slice(start, start + ROWS)
                wide[u, 1, start + 8 : start + 8 + ROWS] = v_buf[h, rows].astype(F32)
                vf = conv_from(wide.at[u, 1], rows, wv).astype(BF16)
                vf_ref[h, rows] = vf
                local = local + dot(kf_ref[h, rows], vf, ((0,), (0,)))
            per = heads // GROUP
            place = (lax.div(h, per) ^ m_ref[0]) * per + lax.rem(h, per)
            msg_ref[place, 0:HDIM] = local.astype(BF16)
            mk = merged_rows(k_buf[h, 0:16], k_buf[h, tokens - 16 : tokens])
            mv = merged_rows(v_buf[h, 0:16], v_buf[h, tokens - 16 : tokens])
            msg_ref[place, HDIM : HDIM + 16] = jnp.concatenate([mk, mv], axis=0).astype(BF16)
        return carry

    lax.fori_loop(0, heads // PAIR, some_heads, 0)
    fetch_queries.wait()
    for h in range(heads):
        cols = slice(h * HDIM, (h + 1) * HDIM)
        per = heads // GROUP
        place = (h // per ^ m_ref[0]) * per + h % per
        mq = merged_rows(q_ref[0:16, cols], q_ref[tokens - 16 : tokens, cols])
        msg_ref[place, HDIM + 16 : HDIM + 32] = jnp.concatenate([mq, mq], axis=0).astype(BF16)


VMEM = pl.BlockSpec(memory_space=pltpu.VMEM)
SMEM = pl.BlockSpec(memory_space=pltpu.SMEM)
HBM = pl.BlockSpec(memory_space=pltpu.HBM)


def block_states(m, queries, key_rows, value_rows, conv_weight):
    tokens, width = key_rows.shape
    heads = width // HDIM
    features = jax.ShapeDtypeStruct((heads, tokens, HDIM), BF16)
    arrays = [pltpu.with_memory_space_constraint(a, pltpu.HBM) for a in (queries, key_rows, value_rows, conv_weight)]
    return pl.pallas_call(
        state_kernel,
        in_specs=[SMEM, HBM, HBM, HBM, HBM],
        out_specs=[VMEM] * 5,
        out_shape=[
            features,
            features,
            jax.ShapeDtypeStruct((heads, HDIM + AUX, HDIM), BF16),
            jax.ShapeDtypeStruct(queries.shape, BF16),
            jax.ShapeDtypeStruct(conv_weight.shape, F32),
        ],
        scratch_shapes=[
            pltpu.VMEM((heads, tokens, HDIM), BF16),
            pltpu.VMEM((heads, tokens, HDIM), BF16),
            pltpu.VMEM((PAIR, 2, tokens + 8, HDIM), F32),
            pltpu.SemaphoreType.DMA((heads,)),
            pltpu.SemaphoreType.DMA((heads,)),
            pltpu.SemaphoreType.DMA((2,)),
        ],
        compiler_params=pltpu.CompilerParams(vmem_limit_bytes=24 << 20),
        cost_estimate=pl.CostEstimate(flops=2 * tokens * width * HDIM, bytes_accessed=8 * tokens * width, transcendentals=tokens * width),
        name="block_states",
    )(m, *arrays)


def taps_of(w_ref, which, m, h, per):
    return w_ref[which, :, pl.ds(pl.multiple_of((m * per + h) * HDIM, HDIM), HDIM)]


def edge_rows(own, before, taps):
    z = pltpu.roll(jnp.where(rows_iota((8, HDIM)) < 4, own, before), 3, 0)
    y = taps[3:4] * z
    for back in range(1, CONV):
        y = y + taps[3 - back : 4 - back] * pltpu.roll(z, back, 0)
    return y


def edge_only(y):
    rows = rows_iota(y.shape)
    return jnp.where((rows >= 3) & (rows < 6), y, 0.0)


def edge_kv(own, before, wk, wv):
    kf = silu_of_twice(edge_rows(own[0:8], before[0:8], wk * 0.5))
    vf = edge_rows(own[8:16], before[8:16], wv)
    return edge_only(kf), edge_only(vf)


def gather_packets(m_ref, packets, buf):
    for j, packet in enumerate(packets):
        buf[m_ref[0] ^ j] = packet[...]


def gather_edges(m_ref, packets, buf):
    for j, packet in enumerate(packets):
        buf[m_ref[0] ^ j] = packet[:, HDIM:]


def total_kernel(has_tail, m_ref, *refs):
    packets, refs = refs[:GROUP], refs[GROUP:]
    if has_tail:
        tail_ref, refs = refs[0], refs[1:]
    w_ref, out_ref, buf = refs
    gather_edges(m_ref, packets, buf)
    per = out_ref.shape[0]
    for h in range(per):
        wk, wv = (taps_of(w_ref, which, m_ref[0], h, per) for which in (1, 2))
        before = tail_ref[h].astype(F32) if has_tail else jnp.zeros((AUX, HDIM), F32)
        kfs, vfs = [], []
        total = sum(packet[h, 0:HDIM].astype(F32) for packet in packets)
        for t in range(GROUP):
            own = buf[t, h].astype(F32)
            kf, vf = edge_kv(own, before, wk, wv)
            kfs.append(kf)
            vfs.append(vf)
            before = own
        kf = jnp.concatenate(kfs, axis=0).astype(BF16)
        vf = jnp.concatenate(vfs, axis=0).astype(BF16)
        total = total + dot(kf, vf, ((0,), (0,)))
        out_ref[h, 0:HDIM] = total.astype(BF16)
        out_ref[h, HDIM:] = pack_tail(before).astype(BF16)


def pack_tail(raw):
    k = jnp.where(rows_iota((8, HDIM)) < 4, pltpu.roll(raw[16:24], 3, 0), raw[0:8])
    return jnp.concatenate([k, raw[8:16]], axis=0)


def unpack_tail(tail):
    q = pltpu.roll(tail[0:8], 5, 0)
    return jnp.concatenate([tail, q, q], axis=0)


def group_total(m, packets, tail, conv_weight):
    heads = packets[0].shape[0]
    tails = [] if tail is None else [tail]
    return pl.pallas_call(
        functools.partial(total_kernel, tail is not None),
        in_specs=[SMEM] + [VMEM] * (GROUP + len(tails) + 1),
        out_specs=VMEM,
        out_shape=jax.ShapeDtypeStruct((heads, HDIM + TAIL, HDIM), BF16),
        scratch_shapes=[pltpu.VMEM((GROUP, heads, AUX, HDIM), BF16)],
        compiler_params=pltpu.CompilerParams(vmem_limit_bytes=8 << 20),
        name="group_total",
    )(m, *packets, *tails, conv_weight)


def edge_features(own, before, wq, wk, wv):
    kf, vf = edge_kv(own, before, wk, wv)
    qf = silu_of_twice(edge_rows(own[16:24], before[16:24], wq * 0.5)) * SCALE
    blank = jnp.zeros((8, HDIM), F32)
    qf, kf, vf = (jnp.concatenate([a, blank], axis=0).astype(BF16) for a in (edge_only(qf), kf, vf))
    scores = dot(qf, kf, ((1,), (1,)))
    causal = rows_iota(scores.shape) >= lax.broadcasted_iota(jnp.int32, scores.shape, 1)
    scores = jnp.where(causal, scores, 0.0).astype(BF16)
    return qf, dot(scores, vf, ((1,), (0,))), dot(kf, vf, ((0,), (0,)))


def edges_kernel(m_ref, p0, p1, p2, p3, w_ref, qf_ref, inner_ref, before_ref, with_ref, first_ref, buf):
    gather_packets(m_ref, (p0, p1, p2, p3), buf)
    per = p0.shape[0]
    for h in range(per):
        taps = [taps_of(w_ref, which, m_ref[0], h, per) for which in range(3)]
        first_ref[h] = buf[0, h, HDIM:]
        state = buf[0, h, 0:HDIM].astype(F32)
        for t in range(1, GROUP):
            own, before = buf[t, h, HDIM:].astype(F32), buf[t - 1, h, HDIM:].astype(F32)
            qf, inner, first = edge_features(own, before, *taps)
            qf_ref[t - 1, h] = qf
            inner_ref[t - 1, h] = inner
            before_ref[t - 1, h] = state
            state = state + first
            with_ref[t - 1, h] = state
            state = state + buf[t, h, 0:HDIM].astype(F32)


def member_edges(m, packets, conv_weight):
    heads = packets[0].shape[0]
    later = GROUP - 1
    return pl.pallas_call(
        edges_kernel,
        in_specs=[SMEM] + [VMEM] * (GROUP + 1),
        out_specs=[VMEM] * 5,
        out_shape=[
            jax.ShapeDtypeStruct((later, heads, 16, HDIM), BF16),
            jax.ShapeDtypeStruct((later, heads, 16, HDIM), F32),
            jax.ShapeDtypeStruct((later, heads, HDIM, HDIM), F32),
            jax.ShapeDtypeStruct((later, heads, HDIM, HDIM), F32),
            jax.ShapeDtypeStruct((heads, AUX, HDIM), BF16),
        ],
        scratch_shapes=[pltpu.VMEM((GROUP, heads, HDIM + AUX, HDIM), BF16)],
        compiler_params=pltpu.CompilerParams(vmem_limit_bytes=8 << 20),
        name="member_edges",
    )(m, *packets, conv_weight)


def prefix_kernel(m_ref, qf_ref, inner_ref, before_ref, with_ref, first_ref, x_ref, w_ref, gain_ref, o0, o1, o2, o3, out):
    later = (m_ref[1] > 0).astype(F32)
    blank = jnp.zeros((8, HDIM), F32)
    per = x_ref.shape[0]
    for h in range(per):
        taps = [taps_of(w_ref, which, m_ref[0], h, per) for which in range(3)]
        gain = gain_ref[:, pl.ds(pl.multiple_of((m_ref[0] * per + h) * HDIM, HDIM), HDIM)]
        base = x_ref[h, 0:HDIM].astype(F32) * later
        tail = unpack_tail(x_ref[h, HDIM:].astype(F32) * later)
        qf, inner, first = edge_features(first_ref[h].astype(F32), tail, *taps)
        prefix = base
        base = base + first
        shifted = base
        for t in range(GROUP):
            if t:
                qf, inner = qf_ref[t - 1, h], inner_ref[t - 1, h]
                prefix = base + before_ref[t - 1, h]
                shifted = base + with_ref[t - 1, h]
            o = inner + dot(qf, prefix.astype(BF16), ((1,), (0,)))
            o = o * lax.rsqrt(jnp.mean(o * o, axis=1, keepdims=True) + 1e-06) * gain
            out[t, h, 0:HDIM] = shifted.astype(BF16)
            out[t, h, HDIM:] = jnp.concatenate([pltpu.roll(o[0:8], 5, 0), blank], axis=0).astype(BF16)
    for j, o_ref in enumerate((o0, o1, o2, o3)):
        o_ref[...] = out[m_ref[0] ^ j]


def member_prefixes(m, edges, incoming, conv_weight, gain):
    heads = incoming.shape[0]
    out = jax.ShapeDtypeStruct((heads, HDIM + FIX, HDIM), BF16)
    return pl.pallas_call(
        prefix_kernel,
        in_specs=[SMEM] + [VMEM] * (len(edges) + 3),
        out_specs=[VMEM] * GROUP,
        out_shape=[out] * GROUP,
        scratch_shapes=[pltpu.VMEM((GROUP, heads, HDIM + FIX, HDIM), BF16)],
        compiler_params=pltpu.CompilerParams(vmem_limit_bytes=8 << 20),
        name="member_prefixes",
    )(m, *edges, incoming, conv_weight, gain)


def inner_kernel(quarters, m_ref, q_ref, kf_ref, vf_ref, w_ref, qf_ref, inner_ref):
    heads, tokens = qf_ref.shape[0:2]
    per = heads // len(quarters)
    shape = (CHUNK, CHUNK)
    causal = rows_iota(shape) >= lax.broadcasted_iota(jnp.int32, shape, 1)
    for place in range(heads):
        h = (m_ref[0] ^ quarters[place // per]) * per + place % per
        cols = pl.ds(pl.multiple_of(h * HDIM, HDIM), HDIM)
        wq = w_ref[0, :, cols] * 0.5
        state = None
        for start in range(0, tokens, CHUNK):
            rows = slice(start, start + CHUNK)
            above = q_ref[start - 16 : start, cols] if start else None
            qf = (silu_of_twice(conv_rows(q_ref[rows, cols], above, wq)) * SCALE).astype(BF16)
            qf_ref[place, rows] = qf
            kf, vf = kf_ref[h, rows], vf_ref[h, rows]
            scores = jnp.where(causal, dot(qf, kf, ((1,), (1,))), 0.0).astype(BF16)
            inner = dot(scores, vf, ((1,), (0,)))
            if state is not None:
                inner = inner + dot(qf, state.astype(BF16), ((1,), (0,)))
            inner_ref[place, rows] = inner
            if start + CHUNK < tokens:
                new = dot(kf, vf, ((0,), (0,)))
                state = new if state is None else state + new


def inner_attention(quarters, m, queries, kf, vf, conv_weight):
    heads, tokens = kf.shape[0:2]
    count = heads // GROUP * len(quarters)
    return pl.pallas_call(
        functools.partial(inner_kernel, quarters),
        in_specs=[SMEM] + [VMEM] * 4,
        out_specs=[VMEM] * 2,
        out_shape=[
            jax.ShapeDtypeStruct((count, tokens, HDIM), BF16),
            jax.ShapeDtypeStruct((count, tokens, HDIM), F32),
        ],
        compiler_params=pltpu.CompilerParams(vmem_limit_bytes=24 << 20),
        cost_estimate=pl.CostEstimate(
            flops=8 * count * tokens * HDIM * HDIM,
            bytes_accessed=12 * tokens * count * HDIM,
            transcendentals=tokens * count * HDIM,
        ),
        name="inner_attention",
    )(m, queries, kf, vf, conv_weight)


def finish_kernel(quarters, places, aliased, m_ref, gain_ref, *refs):
    n = len(quarters)
    packets, qf_refs, inner_refs, refs = refs[0:n], refs[n : 2 * n], refs[2 * n : 3 * n], refs[3 * n + aliased :]
    out_hbm, out_buf, sem = refs
    per = packets[0].shape[0]
    tokens = out_buf.shape[1]
    part = tokens // PARTS
    there = rows_iota((FIX, HDIM)) < CONV - 1
    copies = []
    for i in range(n):
        quarter = m_ref[0] ^ quarters[i]
        for c in range(PARTS):
            rows = slice(c * part, (c + 1) * part)
            for h in range(per):
                place = places[i] * per + h
                gain = gain_ref[:, pl.ds(pl.multiple_of((quarter * per + h) * HDIM, HDIM), HDIM)]
                o = inner_refs[i][place, rows] + dot(qf_refs[i][place, rows], packets[i][h, 0:HDIM], ((1,), (0,)))
                o = o * lax.rsqrt(jnp.mean(o * o, axis=1, keepdims=True) + 1e-06) * gain
                if c == 0:
                    fixed = packets[i][h, HDIM:].astype(F32)
                    o = jnp.concatenate([jnp.where(there, fixed, o[0:FIX]), o[FIX:]], axis=0)
                out_buf[i, rows, h * HDIM : (h + 1) * HDIM] = o.astype(BF16)
            cols = pl.ds(pl.multiple_of(quarter * per * HDIM, per * HDIM), per * HDIM)
            copies.append(pltpu.make_async_copy(out_buf.at[i, rows], out_hbm.at[rows, cols], sem.at[i, c]))
            copies[-1].start()
    for copy in copies:
        copy.wait()


def finish(quarters, m, prefixes, pieces, places, gain, begun=None):
    tokens = pieces[0][0].shape[1]
    width = gain.shape[1]
    n = len(quarters)
    others = [] if begun is None else [begun]
    return pl.pallas_call(
        functools.partial(finish_kernel, quarters, places, len(others)),
        in_specs=[SMEM] + [VMEM] * (1 + 3 * n) + [HBM] * len(others),
        out_specs=HBM,
        out_shape=jax.ShapeDtypeStruct((tokens, width), BF16),
        input_output_aliases={2 + 3 * n: 0} if others else {},
        scratch_shapes=[
            pltpu.VMEM((n, tokens, width // GROUP), BF16),
            pltpu.SemaphoreType.DMA((n, PARTS)),
        ],
        compiler_params=pltpu.CompilerParams(vmem_limit_bytes=24 << 20),
        cost_estimate=pl.CostEstimate(
            flops=2 * n * tokens * width // GROUP * HDIM,
            bytes_accessed=8 * n * tokens * width // GROUP,
            transcendentals=n * tokens * width // GROUP // HDIM,
        ),
        name="finish",
    )(m, gain, *prefixes, *[p[0] for p in pieces], *[p[1] for p in pieces], *others)


def swapped(value, bits):
    count = lax.axis_size("ctx")
    return lax.ppermute(value, "ctx", [(s, s ^ bits) for s in range(count)])


def to_next_group(value):
    count = lax.axis_size("ctx")
    return lax.ppermute(value, "ctx", [(s, s + GROUP) for s in range(count - GROUP)])


def body(queries, key_rows, value_rows, conv_weight, head_gain):
    width = queries.shape[1]
    heads = width // GROUP // HDIM
    groups = lax.axis_size("ctx") // GROUP
    place = lax.axis_index("ctx")
    m = jnp.stack([place % GROUP, place // GROUP]).astype(jnp.int32)
    gain = head_gain.reshape(1, width)
    kf, vf, messages, queries, conv_weight = block_states(m, queries, key_rows, value_rows, conv_weight)

    def beside(quarters, arrays):
        piece = inner_attention(quarters, m, queries, kf, vf, conv_weight)
        return lax.optimization_barrier((arrays, piece))

    packets = [messages[0:heads]]
    packets += [swapped(messages[j * heads : (j + 1) * heads], j) for j in range(1, GROUP)]
    packets, piece01 = beside((0, 1), packets)
    if groups == 2:
        incoming = swapped(group_total(m, packets, None, conv_weight), GROUP)
    else:
        last = jnp.stack(packets)[m[0] ^ (GROUP - 1)][:, HDIM:]
        tail = to_next_group(last)
        total = group_total(m, packets, tail, conv_weight)[:, 0:HDIM].astype(F32)
        tail = jnp.concatenate([tail[:, 21:24], tail[:, 3:16]], axis=1)
        prefix, passed = jnp.zeros_like(total), total
        for _ in range(groups - 1):
            prefix = to_next_group(passed)
            passed = prefix + total
        incoming = jnp.concatenate([prefix.astype(BF16), tail], axis=1)
    edges = member_edges(m, packets, conv_weight)
    (incoming, edges), piece2 = beside((2,), (incoming, edges))
    sends = member_prefixes(m, edges, incoming, conv_weight, gain)
    near = [swapped(sends[j], j) for j in (1, 2)]
    far = swapped(sends[3], 3)
    near, piece3 = beside((3,), near)
    out = finish((0, 1, 2), m, [sends[0]] + near, [piece01, piece01, piece2], (0, 1, 0), gain)
    return finish((3,), m, [far], [piece3], (0,), gain, out)


def solution(mesh):
    return jax.shard_map(
        body,
        mesh=mesh,
        in_specs=(
            P(("mp", "ctx"), None),
            P(("mp", "ctx"), None),
            P(("mp", "ctx"), None),
            P("mp", None, None),
            P("mp"),
        ),
        out_specs=P(("mp", "ctx"), None),
        check_vma=False,
    )
```

time: 33.9 us -> 34 us (level)
  Pallas kernels: 16.4 us -> 19.5 us
  waiting for transfers between devices: 6.37 us -> 3.29 us
    pallas_call x7 -> x8, Pallas kernels: 10.1 us -> 13.3 us  [the longest x3 6 us: inner_attention(): pl.pallas_call(functools.partial(inner_kernel, quarters), in_specs=[SMEM]...]
    ppermute x7, waiting for transfers between devices: 6.37 us -> 3.29 us  [swapped(): return lax.ppermute(value, 'ctx', [(s, s ^ bits) for s in range(count)])]
  transfers between devices with their start and end apart: 7 -> 7, of which waited for: 5 -> 3; matrix products, arithmetic and copies ran while one was open for 0% -> 0% of each run, Pallas kernels for 16% -> 28%
where the time goes in v4:
time: 34 us; the launch traced here: 33.8 us
  Pallas kernels  19.5 us (57%)
  starting transfers between devices  10.8 us (32%)
  waiting for transfers between devices  3.29 us (10%)
    ppermute x7, starting transfers between devices, swapped(): return lax.ppermute(value, 'ctx', [(s, s ^ bits) for s in range(count)])  10.8 us
    pallas_call x1, Pallas kernels, block_states(): pl.pallas_call(state_kernel, in_specs=[SMEM, HBM, HBM, HBM, HBM], out_spe...  6.22 us
    pallas_call x3, Pallas kernels, inner_attention(): pl.pallas_call(functools.partial(inner_kernel, quarters), in_specs=[SMEM]...  6 us
    pallas_call x2, Pallas kernels, finish(): pl.pallas_call(functools.partial(finish_kernel, quarters, places, len(oth...  4.23 us
    ppermute x7, waiting for transfers between devices, swapped(): return lax.ppermute(value, 'ctx', [(s, s ^ bits) for s in range(count)])  3.29 us
    pallas_call x1, Pallas kernels, member_prefixes(): pl.pallas_call(prefix_kernel, in_specs=[SMEM] + [VMEM] * (len(edges) + 3)...  1.15 us
    pallas_call x1, Pallas kernels, member_edges(): pl.pallas_call(edges_kernel, in_specs=[SMEM] + [VMEM] * (GROUP + 1), out_...  1.15 us
    pallas_call x1, Pallas kernels, group_total(): pl.pallas_call(functools.partial(total_kernel, tail is not None), in_spec...  0.77 us
  transfers between devices with their start and end apart: 7, of which 3 were waited for; matrix products, arithmetic and copies ran while one was open for 0% of the time, Pallas kernels for 28%

profile of v4, /device:TPU:0, one launch (start us, length us, event | category | flops | bytes accessed | tf_op | source)
XLA Modules:
  0.0 33.8 jit_solution(17779589915693408857)
XLA Ops:
  0.0 0.1 pad_add_fusion.m_ref
  0.1 6.2 %block_states.1 = (bf16[8,1024,128]{2,1,0:T(8,128)(2,1)S(1)}, bf16[8,1024,128]{2,1,0:T(8,128)(2,1)S(1)}, bf16[8,160,128]{2,1,0:T(8,128)(2,1)S(1)}, bf16[1024,1024]{1,0:T(8,128)(2,1)S(1)}, f32[3,4,1024]{2,1,0:T(4,128)S(1)}) custom-call(s32[2]{0:T(128)S(1)} %pad_add_fusion.m_ref, bf16[1024,1024]{1,0:T(8,128)(2,1)} %q_hbm.1, bf16[1024,1024]{1,0:T(8,128)(2,1)} %k_hbm.1, ...), custom_call_target="tpu_custom_call" | custom-call | flops 268435456 | bytes 8388608 | tf_op jit(solution)/shard_map/block_states/pallas_call | solution.py:142
  6.3 3.0 %collective-permute-start = (bf16[2,160,128]{2,1,0:T(8,128)(2,1)S(1)}, bf16[2,160,128]{2,1,0:T(8,128)(2,1)S(1)}, u32[]{:S(2)}, u32[]{:S(2)}) collective-permute-start(bf16[2,160,128]{2,1,0:T(8,128)(2,1)S(1)} %get-tuple-element.83), channel_id=1, source_target_pairs={{0,1},{1,0},{2,3},{3,2},{4,5},{5,4},{6,7},{7,6},{8,9},{9,8},{10,11... | collective-permute-start | bytes 245768 | tf_op jit(solution)/shard_map/ppermute | solution.py:441
  9.4 1.6 %collective-permute-start.1 = (bf16[2,160,128]{2,1,0:T(8,128)(2,1)S(1)}, bf16[2,160,128]{2,1,0:T(8,128)(2,1)S(1)}, u32[]{:S(2)}, u32[]{:S(2)}) collective-permute-start(bf16[2,160,128]{2,1,0:T(8,128)(2,1)S(1)} %get-tuple-element.82), channel_id=1, source_target_pairs={{0,2},{1,3},{2,0},{3,1},{4,6},{5,7},{6,4},{7,5},{8,10},{9,11},{10,... | collective-permute-start | bytes 245768 | tf_op jit(solution)/shard_map/ppermute | solution.py:441
  10.9 0.0 collective-permute-start.2
  10.9 2.6 %inner_attention.3 = (bf16[4,1024,128]{2,1,0:T(8,128)(2,1)S(1)}, f32[4,1024,128]{2,1,0:T(8,128)S(1)}) custom-call(s32[2]{0:T(128)S(1)} %pad_add_fusion.m_ref, bf16[1024,1024]{1,0:T(8,128)(2,1)S(1)} %get-tuple-element.44.q_ref, bf16[8,1024,128]{2,1,0:T(8,128)(2,1)S(1)} %get-tuple-element.45.kf_ref, bf16[8,1024,128]{2,1,0:T(8,128)(2,1)S(1)} %get-tuple-element.46.vf_ref, ...), custom_call_target="tpu_custom_call" | custom-call | flops 536870912 | bytes 6291456 | tf_op jit(solution)/shard_map/inner_attention/pallas_call | solution.py:367
  13.5 0.0 collective-permute-done.refs_1_.p1
  13.5 1.0 %collective-permute-done.1.refs_2_.p2 = bf16[2,160,128]{2,1,0:T(8,128)(2,1)S(1)} collective-permute-done((bf16[2,160,128]{2,1,0:T(8,128)(2,1)S(1)}, bf16[2,160,128]{2,1,0:T(8,128)(2,1)S(1)}, u32[]{:S(2)}, u32[]{:S(2)}) %collective-permute-start.1) | collective-permute-done | bytes 81952 | tf_op jit(solution)/shard_map/ppermute | solution.py:441
  14.5 1.8 %collective-permute-done.2.refs_3_.p3 = bf16[2,160,128]{2,1,0:T(8,128)(2,1)S(1)} collective-permute-done((bf16[2,160,128]{2,1,0:T(8,128)(2,1)S(1)}, bf16[2,160,128]{2,1,0:T(8,128)(2,1)S(1)}, u32[]{:S(2)}, u32[]{:S(2)}) %collective-permute-start.2) | collective-permute-done | bytes 81952 | tf_op jit(solution)/shard_map/ppermute | solution.py:441
  16.3 0.8 %group_total.1 = bf16[2,144,128]{2,1,0:T(8,128)(2,1)S(1)} custom-call(s32[2]{0:T(128)S(1)} %pad_add_fusion.m_ref, bf16[2,160,128]{2,1,0:T(8,128)(2,1)S(1)} %get-tuple-element.50.refs_0_.p0, bf16[2,160,128]{2,1,0:T(8,128)(2,1)S(1)} %collective-permute-done.refs_1_.p1, bf16[2,160,128]{2,1,0:T(8,128)(2,1)S(1)} %collective-permute-done.1.refs_2_.p2, ...), custom_call_target="tpu_custom_call" | custom-call | tf_op jit(solution)/shard_map/group_total/pallas_call | solution.py:238
  17.1 0.0 copy-start
  17.1 2.7 %collective-permute-start.3 = (bf16[2,144,128]{2,1,0:T(8,128)(2,1)S(1)}, bf16[2,144,128]{2,1,0:T(8,128)(2,1)S(1)}, u32[]{:S(2)}, u32[]{:S(2)}) collective-permute-start(bf16[2,144,128]{2,1,0:T(8,128)(2,1)S(1)} %group_total.1), channel_id=1, source_target_pairs={{0,4},{1,5},{2,6},{3,7},{4,0},{5,1},{6,2},{7,3},{8,12},{9,13},{10,... | collective-permute-start | bytes 221192 | tf_op jit(solution)/shard_map/ppermute | solution.py:441
  19.7 1.7 %inner_attention.4 = (bf16[2,1024,128]{2,1,0:T(8,128)(2,1)S(1)}, f32[2,1024,128]{2,1,0:T(8,128)S(1)}) custom-call(s32[2]{0:T(128)S(1)} %pad_add_fusion.m_ref, bf16[1024,1024]{1,0:T(8,128)(2,1)S(1)} %get-tuple-element.44.q_ref, bf16[8,1024,128]{2,1,0:T(8,128)(2,1)S(1)} %get-tuple-element.45.kf_ref, bf16[8,1024,128]{2,1,0:T(8,128)(2,1)S(1)} %get-tuple-element.46.vf_ref, ...), custom_call_target="tpu_custom_call" | custom-call | flops 268435456 | bytes 3145728 | tf_op jit(solution)/shard_map/inner_attention/pallas_call | solution.py:367
  21.5 1.1 %member_edges.1 = (bf16[3,2,16,128]{3,2,1,0:T(8,128)(2,1)S(1)}, f32[3,2,16,128]{3,2,1,0:T(8,128)S(1)}, f32[3,2,128,128]{3,2,1,0:T(8,128)S(1)}, f32[3,2,128,128]{3,2,1,0:T(8,128)S(1)}, bf16[2,32,128]{2,1,0:T(8,128)(2,1)S(1)}) custom-call(s32[2]{0:T(128)S(1)} %pad_add_fusion.m_ref, bf16[2,160,128]{2,1,0:T(8,128)(2,1)S(1)} %get-tuple-element.50.refs_0_.p0, ...), custom_call_target="tpu_custom_call" | custom-call | tf_op jit(solution)/shard_map/member_edges/pallas_call | solution.py:281
  22.6 0.5 %collective-permute-done.3.x_ref = bf16[2,144,128]{2,1,0:T(8,128)(2,1)S(1)} collective-permute-done((bf16[2,144,128]{2,1,0:T(8,128)(2,1)S(1)}, bf16[2,144,128]{2,1,0:T(8,128)(2,1)S(1)}, u32[]{:S(2)}, u32[]{:S(2)}) %collective-permute-start.3) | collective-permute-done | bytes 73760 | tf_op jit(solution)/shard_map/ppermute | solution.py:441
  23.1 0.0 copy-done
  23.1 1.2 %member_prefixes.1 = (bf16[2,144,128]{2,1,0:T(8,128)(2,1)S(1)}, bf16[2,144,128]{2,1,0:T(8,128)(2,1)S(1)}, bf16[2,144,128]{2,1,0:T(8,128)(2,1)S(1)}, bf16[2,144,128]{2,1,0:T(8,128)(2,1)S(1)}) custom-call(s32[2]{0:T(128)S(1)} %pad_add_fusion.m_ref, bf16[3,2,16,128]{3,2,1,0:T(8,128)(2,1)S(1)} %get-tuple-element.61.qf_ref, ...), custom_call_target="tpu_custom_call" | custom-call | tf_op jit(solution)/shard_map/member_prefixes/pallas_call | solution.py:327
  24.3 0.7 %collective-permute-start.5 = (bf16[2,144,128]{2,1,0:T(8,128)(2,1)S(1)}, bf16[2,144,128]{2,1,0:T(8,128)(2,1)S(1)}, u32[]{:S(2)}, u32[]{:S(2)}) collective-permute-start(bf16[2,144,128]{2,1,0:T(8,128)(2,1)S(1)} %get-tuple-element.68), channel_id=1, source_target_pairs={{0,1},{1,0},{2,3},{3,2},{4,5},{5,4},{6,7},{7,6},{8,9},{9,8},{10,11... | collective-permute-start | bytes 221192 | tf_op jit(solution)/shard_map/ppermute | solution.py:441
  25.0 0.7 %collective-permute-start.6 = (bf16[2,144,128]{2,1,0:T(8,128)(2,1)S(1)}, bf16[2,144,128]{2,1,0:T(8,128)(2,1)S(1)}, u32[]{:S(2)}, u32[]{:S(2)}) collective-permute-start(bf16[2,144,128]{2,1,0:T(8,128)(2,1)S(1)} %get-tuple-element.69), channel_id=1, source_target_pairs={{0,2},{1,3},{2,0},{3,1},{4,6},{5,7},{6,4},{7,5},{8,10},{9,11},{10,... | collective-permute-start | bytes 221192 | tf_op jit(solution)/shard_map/ppermute | solution.py:441
  25.6 2.2 %collective-permute-start.4 = (bf16[2,144,128]{2,1,0:T(8,128)(2,1)S(1)}, bf16[2,144,128]{2,1,0:T(8,128)(2,1)S(1)}, u32[]{:S(2)}, u32[]{:S(2)}) collective-permute-start(bf16[2,144,128]{2,1,0:T(8,128)(2,1)S(1)} %get-tuple-element.67), channel_id=1, source_target_pairs={{0,3},{1,2},{2,1},{3,0},{4,7},{5,6},{6,5},{7,4},{8,11},{9,10},{10,... | collective-permute-start | bytes 221192 | tf_op jit(solution)/shard_map/ppermute | solution.py:441
  27.8 1.7 %inner_attention.5 = (bf16[2,1024,128]{2,1,0:T(8,128)(2,1)S(1)}, f32[2,1024,128]{2,1,0:T(8,128)S(1)}) custom-call(s32[2]{0:T(128)S(1)} %pad_add_fusion.m_ref, bf16[1024,1024]{1,0:T(8,128)(2,1)S(1)} %get-tuple-element.44.q_ref, bf16[8,1024,128]{2,1,0:T(8,128)(2,1)S(1)} %get-tuple-element.45.kf_ref, bf16[8,1024,128]{2,1,0:T(8,128)(2,1)S(1)} %get-tuple-element.46.vf_ref, ...), custom_call_target="tpu_custom_call" | custom-call | flops 268435456 | bytes 3145728 | tf_op jit(solution)/shard_map/inner_attention/pallas_call | solution.py:367
  29.6 0.0 collective-permute-done.5.refs_1_
  29.6 0.0 collective-permute-done.6.refs_2_
  29.6 2.5 %finish.2.refs_3_ = bf16[1024,1024]{1,0:T(8,128)(2,1)} custom-call(s32[2]{0:T(128)S(1)} %pad_add_fusion.m_ref, f32[1,1024]{1,0:T(1,128)S(1)} %bitcast.4, bf16[2,144,128]{2,1,0:T(8,128)(2,1)S(1)} %get-tuple-element.74.refs_0_, bf16[2,144,128]{2,1,0:T(8,128)(2,1)S(1)} %collective-permute-done.5.refs_1_, ...), custom_call_target="tpu_custom_call" | custom-call | flops 201326592 | bytes 6291456 | tf_op jit(solution)/shard_map/finish/pallas_call | solution.py:419
  32.1 0.0 collective-permute-done.4.refs_0_
  32.1 1.8 %finish.3 = bf16[1024,1024]{1,0:T(8,128)(2,1)} custom-call(s32[2]{0:T(128)S(1)} %pad_add_fusion.m_ref, f32[1,1024]{1,0:T(1,128)S(1)} %bitcast.5, bf16[2,144,128]{2,1,0:T(8,128)(2,1)S(1)} %collective-permute-done.4.refs_0_, bf16[2,1024,128]{2,1,0:T(8,128)(2,1)S(1)} %get-tuple-element.72.refs_1_, ...), custom_call_target="tpu_custom_call", output_to_operand_aliasing={{}: (5, {})} | custom-call | flops 67108864 | bytes 2097152 | tf_op jit(solution)/shard_map/finish/pallas_call | solution.py:419
  (1 shorter events, 0.0 us)
Async XLA Ops:
  6.3 7.2 %collective-permute-start = (bf16[2,160,128]{2,1,0:T(8,128)(2,1)S(1)}, bf16[2,160,128]{2,1,0:T(8,128)(2,1)S(1)}, u32[]{:S(2)}, u32[]{:S(2)}) collective-permute-start(bf16[2,160,128]{2,1,0:T(8,128)(2,1)S(1)} %get-tuple-element.83), channel_id=1, source_target_pairs={{0,1},{1,0},{2,3},{3,2},{4,5},{5,4},{6,7},{7,6},{8,9},{9,8},{10,11... | collective-permute-start | bytes 245768 | tf_op jit(solution)/shard_map/ppermute | solution.py:441
  9.4 5.1 %collective-permute-start.1 = (bf16[2,160,128]{2,1,0:T(8,128)(2,1)S(1)}, bf16[2,160,128]{2,1,0:T(8,128)(2,1)S(1)}, u32[]{:S(2)}, u32[]{:S(2)}) collective-permute-start(bf16[2,160,128]{2,1,0:T(8,128)(2,1)S(1)} %get-tuple-element.82), channel_id=1, source_target_pairs={{0,2},{1,3},{2,0},{3,1},{4,6},{5,7},{6,4},{7,5},{8,10},{9,11},{10,... | collective-permute-start | bytes 245768 | tf_op jit(solution)/shard_map/ppermute | solution.py:441
  10.9 5.3 %collective-permute-start.2 = (bf16[2,160,128]{2,1,0:T(8,128)(2,1)S(1)}, bf16[2,160,128]{2,1,0:T(8,128)(2,1)S(1)}, u32[]{:S(2)}, u32[]{:S(2)}) collective-permute-start(bf16[2,160,128]{2,1,0:T(8,128)(2,1)S(1)} %get-tuple-element.81), channel_id=1, source_target_pairs={{0,3},{1,2},{2,1},{3,0},{4,7},{5,6},{6,5},{7,4},{8,11},{9,10},{10,... | collective-permute-start | bytes 245768 | tf_op jit(solution)/shard_map/ppermute | solution.py:441
  17.1 6.1 %copy-start = (f32[1024]{0:T(1024)S(1)}, f32[1024]{0:T(1024)}, u32[]{:S(2)}) copy-start(f32[1024]{0:T(1024)} %param.9) | copy-start | bytes 12292
  17.1 6.1 %collective-permute-start.3 = (bf16[2,144,128]{2,1,0:T(8,128)(2,1)S(1)}, bf16[2,144,128]{2,1,0:T(8,128)(2,1)S(1)}, u32[]{:S(2)}, u32[]{:S(2)}) collective-permute-start(bf16[2,144,128]{2,1,0:T(8,128)(2,1)S(1)} %group_total.1), channel_id=1, source_target_pairs={{0,4},{1,5},{2,6},{3,7},{4,0},{5,1},{6,2},{7,3},{8,12},{9,13},{10,... | collective-permute-start | bytes 221192 | tf_op jit(solution)/shard_map/ppermute | solution.py:441
  24.3 5.3 %collective-permute-start.5 = (bf16[2,144,128]{2,1,0:T(8,128)(2,1)S(1)}, bf16[2,144,128]{2,1,0:T(8,128)(2,1)S(1)}, u32[]{:S(2)}, u32[]{:S(2)}) collective-permute-start(bf16[2,144,128]{2,1,0:T(8,128)(2,1)S(1)} %get-tuple-element.68), channel_id=1, source_target_pairs={{0,1},{1,0},{2,3},{3,2},{4,5},{5,4},{6,7},{7,6},{8,9},{9,8},{10,11... | collective-permute-start | bytes 221192 | tf_op jit(solution)/shard_map/ppermute | solution.py:441
  25.0 4.6 %collective-permute-start.6 = (bf16[2,144,128]{2,1,0:T(8,128)(2,1)S(1)}, bf16[2,144,128]{2,1,0:T(8,128)(2,1)S(1)}, u32[]{:S(2)}, u32[]{:S(2)}) collective-permute-start(bf16[2,144,128]{2,1,0:T(8,128)(2,1)S(1)} %get-tuple-element.69), channel_id=1, source_target_pairs={{0,2},{1,3},{2,0},{3,1},{4,6},{5,7},{6,4},{7,5},{8,10},{9,11},{10,... | collective-permute-start | bytes 221192 | tf_op jit(solution)/shard_map/ppermute | solution.py:441
  25.6 6.4 %collective-permute-start.4 = (bf16[2,144,128]{2,1,0:T(8,128)(2,1)S(1)}, bf16[2,144,128]{2,1,0:T(8,128)(2,1)S(1)}, u32[]{:S(2)}, u32[]{:S(2)}) collective-permute-start(bf16[2,144,128]{2,1,0:T(8,128)(2,1)S(1)} %get-tuple-element.67), channel_id=1, source_target_pairs={{0,3},{1,2},{2,1},{3,0},{4,7},{5,6},{6,5},{7,4},{8,11},{9,10},{10,... | collective-permute-start | bytes 221192 | tf_op jit(solution)/shard_map/ppermute | solution.py:441

commit v5 on v4

--- a/solution.py
+++ b/solution.py
@@ -21,6 +21,14 @@
 F32, BF16 = jnp.float32, jnp.bfloat16
 
 
+def member():
+    return lax.rem(lax.axis_index("ctx"), GROUP)
+
+
+def group():
+    return lax.div(lax.axis_index("ctx"), GROUP)
+
+
 def rows_iota(shape):
     return lax.broadcasted_iota(jnp.int32, shape, 0)
 
@@ -54,7 +62,7 @@
     return (taps[3:4] * at(0) + taps[2:3] * at(1)) + (taps[1:2] * at(2) + taps[0:1] * at(3))
 
 
-def state_kernel(m_ref, q_hbm, k_hbm, v_hbm, w_hbm, kf_ref, vf_ref, msg_ref, q_ref, w_ref, k_buf, v_buf, wide, k_sem, v_sem, sem):
+def state_kernel(q_hbm, k_hbm, v_hbm, w_hbm, kf_ref, vf_ref, msg_ref, q_ref, w_ref, k_buf, v_buf, wide, k_sem, v_sem, sem):
     heads, tokens = k_buf.shape[0:2]
 
     def fetch(source, target, semaphore, h):
@@ -112,7 +120,7 @@
                 vf_ref[h, rows] = vf
                 local = local + dot(kf_ref[h, rows], vf, ((0,), (0,)))
             per = heads // GROUP
-            place = (lax.div(h, per) ^ m_ref[0]) * per + lax.rem(h, per)
+            place = (lax.div(h, per) ^ member()) * per + lax.rem(h, per)
             msg_ref[place, 0:HDIM] = local.astype(BF16)
             mk = merged_rows(k_buf[h, 0:16], k_buf[h, tokens - 16 : tokens])
             mv = merged_rows(v_buf[h, 0:16], v_buf[h, tokens - 16 : tokens])
@@ -124,24 +132,23 @@
     for h in range(heads):
         cols = slice(h * HDIM, (h + 1) * HDIM)
         per = heads // GROUP
-        place = (h // per ^ m_ref[0]) * per + h % per
+        place = (h // per ^ member()) * per + h % per
         mq = merged_rows(q_ref[0:16, cols], q_ref[tokens - 16 : tokens, cols])
         msg_ref[place, HDIM + 16 : HDIM + 32] = jnp.concatenate([mq, mq], axis=0).astype(BF16)
 
 
 VMEM = pl.BlockSpec(memory_space=pltpu.VMEM)
-SMEM = pl.BlockSpec(memory_space=pltpu.SMEM)
 HBM = pl.BlockSpec(memory_space=pltpu.HBM)
 
 
-def block_states(m, queries, key_rows, value_rows, conv_weight):
+def block_states(queries, key_rows, value_rows, conv_weight):
     tokens, width = key_rows.shape
     heads = width // HDIM
     features = jax.ShapeDtypeStruct((heads, tokens, HDIM), BF16)
     arrays = [pltpu.with_memory_space_constraint(a, pltpu.HBM) for a in (queries, key_rows, value_rows, conv_weight)]
     return pl.pallas_call(
         state_kernel,
-        in_specs=[SMEM, HBM, HBM, HBM, HBM],
+        in_specs=[HBM, HBM, HBM, HBM],
         out_specs=[VMEM] * 5,
         out_shape=[
             features,
@@ -161,7 +168,7 @@
         compiler_params=pltpu.CompilerParams(vmem_limit_bytes=24 << 20),
         cost_estimate=pl.CostEstimate(flops=2 * tokens * width * HDIM, bytes_accessed=8 * tokens * width, transcendentals=tokens * width),
         name="block_states",
-    )(m, *arrays)
+    )(*arrays)
 
 
 def taps_of(w_ref, which, m, h, per):
@@ -187,25 +194,25 @@
     return edge_only(kf), edge_only(vf)
 
 
-def gather_packets(m_ref, packets, buf):
+def gather_packets(packets, buf):
     for j, packet in enumerate(packets):
-        buf[m_ref[0] ^ j] = packet[...]
-
-
-def gather_edges(m_ref, packets, buf):
+        buf[member() ^ j] = packet[...]
+
+
+def gather_edges(packets, buf):
     for j, packet in enumerate(packets):
-        buf[m_ref[0] ^ j] = packet[:, HDIM:]
-
-
-def total_kernel(has_tail, m_ref, *refs):
+        buf[member() ^ j] = packet[:, HDIM:]
+
+
+def total_kernel(has_tail, *refs):
     packets, refs = refs[:GROUP], refs[GROUP:]
     if has_tail:
         tail_ref, refs = refs[0], refs[1:]
     w_ref, out_ref, buf = refs
-    gather_edges(m_ref, packets, buf)
+    gather_edges(packets, buf)
     per = out_ref.shape[0]
     for h in range(per):
-        wk, wv = (taps_of(w_ref, which, m_ref[0], h, per) for which in (1, 2))
+        wk, wv = (taps_of(w_ref, which, member(), h, per) for which in (1, 2))
         before = tail_ref[h].astype(F32) if has_tail else jnp.zeros((AUX, HDIM), F32)
         kfs, vfs = [], []
         total = sum(packet[h, 0:HDIM].astype(F32) for packet in packets)
@@ -232,18 +239,18 @@
     return jnp.concatenate([tail, q, q], axis=0)
 
 
-def group_total(m, packets, tail, conv_weight):
+def group_total(packets, tail, conv_weight):
     heads = packets[0].shape[0]
     tails = [] if tail is None else [tail]
     return pl.pallas_call(
         functools.partial(total_kernel, tail is not None),
-        in_specs=[SMEM] + [VMEM] * (GROUP + len(tails) + 1),
+        in_specs=[VMEM] * (GROUP + len(tails) + 1),
         out_specs=VMEM,
         out_shape=jax.ShapeDtypeStruct((heads, HDIM + TAIL, HDIM), BF16),
         scratch_shapes=[pltpu.VMEM((GROUP, heads, AUX, HDIM), BF16)],
         compiler_params=pltpu.CompilerParams(vmem_limit_bytes=8 << 20),
         name="group_total",
-    )(m, *packets, *tails, conv_weight)
+    )(*packets, *tails, conv_weight)
 
 
 def edge_features(own, before, wq, wk, wv):
@@ -257,11 +264,11 @@
     return qf, dot(scores, vf, ((1,), (0,))), dot(kf, vf, ((0,), (0,)))
 
 
-def edges_kernel(m_ref, p0, p1, p2, p3, w_ref, qf_ref, inner_ref, before_ref, with_ref, first_ref, buf):
-    gather_packets(m_ref, (p0, p1, p2, p3), buf)
+def edges_kernel(p0, p1, p2, p3, w_ref, qf_ref, inner_ref, before_ref, with_ref, first_ref, buf):
+    gather_packets((p0, p1, p2, p3), buf)
     per = p0.shape[0]
     for h in range(per):
-        taps = [taps_of(w_ref, which, m_ref[0], h, per) for which in range(3)]
+        taps = [taps_of(w_ref, which, member(), h, per) for which in range(3)]
         first_ref[h] = buf[0, h, HDIM:]
         state = buf[0, h, 0:HDIM].astype(F32)
         for t in range(1, GROUP):
@@ -275,12 +282,12 @@
             state = state + buf[t, h, 0:HDIM].astype(F32)
 
 
-def member_edges(m, packets, conv_weight):
+def member_edges(packets, conv_weight):
     heads = packets[0].shape[0]
     later = GROUP - 1
     return pl.pallas_call(
         edges_kernel,
-        in_specs=[SMEM] + [VMEM] * (GROUP + 1),
+        in_specs=[VMEM] * (GROUP + 1),
         out_specs=[VMEM] * 5,
         out_shape=[
             jax.ShapeDtypeStruct((later, heads, 16, HDIM), BF16),
@@ -292,16 +299,16 @@
         scratch_shapes=[pltpu.VMEM((GROUP, heads, HDIM + AUX, HDIM), BF16)],
         compiler_params=pltpu.CompilerParams(vmem_limit_bytes=8 << 20),
         name="member_edges",
-    )(m, *packets, conv_weight)
-
-
-def prefix_kernel(m_ref, qf_ref, inner_ref, before_ref, with_ref, first_ref, x_ref, w_ref, gain_ref, o0, o1, o2, o3, out):
-    later = (m_ref[1] > 0).astype(F32)
+    )(*packets, conv_weight)
+
+
+def prefix_kernel(qf_ref, inner_ref, before_ref, with_ref, first_ref, x_ref, w_ref, gain_ref, o0, o1, o2, o3, out):
+    later = (group() > 0).astype(F32)
     blank = jnp.zeros((8, HDIM), F32)
     per = x_ref.shape[0]
     for h in range(per):
-        taps = [taps_of(w_ref, which, m_ref[0], h, per) for which in range(3)]
-        gain = gain_ref[:, pl.ds(pl.multiple_of((m_ref[0] * per + h) * HDIM, HDIM), HDIM)]
+        taps = [taps_of(w_ref, which, member(), h, per) for which in range(3)]
+        gain = gain_ref[:, pl.ds(pl.multiple_of((member() * per + h) * HDIM, HDIM), HDIM)]
         base = x_ref[h, 0:HDIM].astype(F32) * later
         tail = unpack_tail(x_ref[h, HDIM:].astype(F32) * later)
         qf, inner, first = edge_features(first_ref[h].astype(F32), tail, *taps)
@@ -318,30 +325,30 @@
             out[t, h, 0:HDIM] = shifted.astype(BF16)
             out[t, h, HDIM:] = jnp.concatenate([pltpu.roll(o[0:8], 5, 0), blank], axis=0).astype(BF16)
     for j, o_ref in enumerate((o0, o1, o2, o3)):
-        o_ref[...] = out[m_ref[0] ^ j]
-
-
-def member_prefixes(m, edges, incoming, conv_weight, gain):
+        o_ref[...] = out[member() ^ j]
+
+
+def member_prefixes(edges, incoming, conv_weight, gain):
     heads = incoming.shape[0]
     out = jax.ShapeDtypeStruct((heads, HDIM + FIX, HDIM), BF16)
     return pl.pallas_call(
         prefix_kernel,
-        in_specs=[SMEM] + [VMEM] * (len(edges) + 3),
+        in_specs=[VMEM] * (len(edges) + 3),
         out_specs=[VMEM] * GROUP,
         out_shape=[out] * GROUP,
         scratch_shapes=[pltpu.VMEM((GROUP, heads, HDIM + FIX, HDIM), BF16)],
         compiler_params=pltpu.CompilerParams(vmem_limit_bytes=8 << 20),
         name="member_prefixes",
-    )(m, *edges, incoming, conv_weight, gain)
-
-
-def inner_kernel(quarters, m_ref, q_ref, kf_ref, vf_ref, w_ref, qf_ref, inner_ref):
+    )(*edges, incoming, conv_weight, gain)
+
+
+def inner_kernel(quarters, q_ref, kf_ref, vf_ref, w_ref, qf_ref, inner_ref):
     heads, tokens = qf_ref.shape[0:2]
     per = heads // len(quarters)
     shape = (CHUNK, CHUNK)
     causal = rows_iota(shape) >= lax.broadcasted_iota(jnp.int32, shape, 1)
     for place in range(heads):
-        h = (m_ref[0] ^ quarters[place // per]) * per + place % per
+        h = (member() ^ quarters[place // per]) * per + place % per
         cols = pl.ds(pl.multiple_of(h * HDIM, HDIM), HDIM)
         wq = w_ref[0, :, cols] * 0.5
         state = None
@@ -361,12 +368,12 @@
                 state = new if state is None else state + new
 
 
-def inner_attention(quarters, m, queries, kf, vf, conv_weight):
+def inner_attention(quarters, queries, kf, vf, conv_weight):
     heads, tokens = kf.shape[0:2]
     count = heads // GROUP * len(quarters)
     return pl.pallas_call(
         functools.partial(inner_kernel, quarters),
-        in_specs=[SMEM] + [VMEM] * 4,
+        in_specs=[VMEM] * 4,
         out_specs=[VMEM] * 2,
         out_shape=[
             jax.ShapeDtypeStruct((count, tokens, HDIM), BF16),
@@ -379,10 +386,10 @@
             transcendentals=tokens * count * HDIM,
         ),
         name="inner_attention",
-    )(m, queries, kf, vf, conv_weight)
-
-
-def finish_kernel(quarters, places, aliased, m_ref, gain_ref, *refs):
+    )(queries, kf, vf, conv_weight)
+
+
+def finish_kernel(quarters, places, aliased, gain_ref, *refs):
     n = len(quarters)
     packets, qf_refs, inner_refs, refs = refs[0:n], refs[n : 2 * n], refs[2 * n : 3 * n], refs[3 * n + aliased :]
     out_hbm, out_buf, sem = refs
@@ -392,7 +399,7 @@
     there = rows_iota((FIX, HDIM)) < CONV - 1
     copies = []
     for i in range(n):
-        quarter = m_ref[0] ^ quarters[i]
+        quarter = member() ^ quarters[i]
         for c in range(PARTS):
             rows = slice(c * part, (c + 1) * part)
             for h in range(per):
@@ -411,17 +418,17 @@
         copy.wait()
 
 
-def finish(quarters, m, prefixes, pieces, places, gain, begun=None):
+def finish(quarters, prefixes, pieces, places, gain, begun=None):
     tokens = pieces[0][0].shape[1]
     width = gain.shape[1]
     n = len(quarters)
     others = [] if begun is None else [begun]
     return pl.pallas_call(
         functools.partial(finish_kernel, quarters, places, len(others)),
-        in_specs=[SMEM] + [VMEM] * (1 + 3 * n) + [HBM] * len(others),
+        in_specs=[VMEM] * (1 + 3 * n) + [HBM] * len(others),
         out_specs=HBM,
         out_shape=jax.ShapeDtypeStruct((tokens, width), BF16),
-        input_output_aliases={2 + 3 * n: 0} if others else {},
+        input_output_aliases={1 + 3 * n: 0} if others else {},
         scratch_shapes=[
             pltpu.VMEM((n, tokens, width // GROUP), BF16),
             pltpu.SemaphoreType.DMA((n, PARTS)),
@@ -433,7 +440,7 @@
             transcendentals=n * tokens * width // GROUP // HDIM,
         ),
         name="finish",
-    )(m, gain, *prefixes, *[p[0] for p in pieces], *[p[1] for p in pieces], *others)
+    )(gain, *prefixes, *[p[0] for p in pieces], *[p[1] for p in pieces], *others)
 
 
 def swapped(value, bits):
@@ -450,38 +457,36 @@
     width = queries.shape[1]
     heads = width // GROUP // HDIM
     groups = lax.axis_size("ctx") // GROUP
-    place = lax.axis_index("ctx")
-    m = jnp.stack([place % GROUP, place // GROUP]).astype(jnp.int32)
     gain = head_gain.reshape(1, width)
-    kf, vf, messages, queries, conv_weight = block_states(m, queries, key_rows, value_rows, conv_weight)
+    kf, vf, messages, queries, conv_weight = block_states(queries, key_rows, value_rows, conv_weight)
 
     def beside(quarters, arrays):
-        piece = inner_attention(quarters, m, queries, kf, vf, conv_weight)
+        piece = inner_attention(quarters, queries, kf, vf, conv_weight)
         return lax.optimization_barrier((arrays, piece))
 
     packets = [messages[0:heads]]
     packets += [swapped(messages[j * heads : (j + 1) * heads], j) for j in range(1, GROUP)]
     packets, piece01 = beside((0, 1), packets)
     if groups == 2:
-        incoming = swapped(group_total(m, packets, None, conv_weight), GROUP)
+        incoming = swapped(group_total(packets, None, conv_weight), GROUP)
     else:
-        last = jnp.stack(packets)[m[0] ^ (GROUP - 1)][:, HDIM:]
+        last = jnp.stack(packets)[member() ^ (GROUP - 1)][:, HDIM:]
         tail = to_next_group(last)
-        total = group_total(m, packets, tail, conv_weight)[:, 0:HDIM].astype(F32)
+        total = group_total(packets, tail, conv_weight)[:, 0:HDIM].astype(F32)
         tail = jnp.concatenate([tail[:, 21:24], tail[:, 3:16]], axis=1)
         prefix, passed = jnp.zeros_like(total), total
         for _ in range(groups - 1):
             prefix = to_next_group(passed)
             passed = prefix + total
         incoming = jnp.concatenate([prefix.astype(BF16), tail], axis=1)
-    edges = member_edges(m, packets, conv_weight)
+    edges = member_edges(packets, conv_weight)
     (incoming, edges), piece2 = beside((2,), (incoming, edges))
-    sends = member_prefixes(m, edges, incoming, conv_weight, gain)
+    sends = member_prefixes(edges, incoming, conv_weight, gain)
     near = [swapped(sends[j], j) for j in (1, 2)]
     far = swapped(sends[3], 3)
     near, piece3 = beside((3,), near)
-    out = finish((0, 1, 2), m, [sends[0]] + near, [piece01, piece01, piece2], (0, 1, 0), gain)
-    return finish((3,), m, [far], [piece3], (0,), gain, out)
+    out = finish((0, 1, 2), [sends[0]] + near, [piece01, piece01, piece2], (0, 1, 0), gain)
+    return finish((3,), [far], [piece3], (0,), gain, out)
 
 
 def solution(mesh):

time: 34 us -> 30.9 us (0.909)
  Pallas kernels: 19.5 us -> 14.5 us
  waiting for transfers between devices: 3.29 us -> 5.23 us
    pallas_call x6, Pallas kernels: 14.5 us -> 11.2 us  [the longest x1 5.64 us: block_states(): pl.pallas_call(state_kernel, in_specs=[HBM, HBM, HBM, HBM], out_specs=[VM...]
    ppermute x7, waiting for transfers between devices: 3.29 us -> 5.23 us  [swapped(): return lax.ppermute(value, 'ctx', [(s, s ^ bits) for s in range(count)])]
    pallas_call x2, Pallas kernels: 4.23 us -> 3.08 us  [finish(): pl.pallas_call(functools.partial(finish_kernel, quarters, places, len(oth...]
    pallas_call x1, Pallas kernels: 0.77 us -> 0.23 us  [group_total(): pl.pallas_call(functools.partial(total_kernel, tail is not None), in_spec...]
  transfers between devices with their start and end apart: 7 -> 7, of which waited for: 3 -> 4; matrix products, arithmetic and copies ran while one was open for 0% -> 0% of each run, Pallas kernels for 28% -> 22%
where the time goes in v5:
time: 30.9 us; the launch traced here: 30.7 us
  Pallas kernels  14.5 us (47%)
  starting transfers between devices  10.8 us (35%)
  waiting for transfers between devices  5.23 us (17%)
    ppermute x7, starting transfers between devices, swapped(): return lax.ppermute(value, 'ctx', [(s, s ^ bits) for s in range(count)])  10.8 us
    pallas_call x1, Pallas kernels, block_states(): pl.pallas_call(state_kernel, in_specs=[HBM, HBM, HBM, HBM], out_specs=[VM...  5.64 us
    ppermute x7, waiting for transfers between devices, swapped(): return lax.ppermute(value, 'ctx', [(s, s ^ bits) for s in range(count)])  5.23 us
    pallas_call x3, Pallas kernels, inner_attention(): pl.pallas_call(functools.partial(inner_kernel, quarters), in_specs=[VMEM]...  4.34 us
    pallas_call x2, Pallas kernels, finish(): pl.pallas_call(functools.partial(finish_kernel, quarters, places, len(oth...  3.08 us
    pallas_call x1, Pallas kernels, member_prefixes(): pl.pallas_call(prefix_kernel, in_specs=[VMEM] * (len(edges) + 3), out_spe...  0.62 us
  transfers between devices with their start and end apart: 7, of which 4 were waited for; matrix products, arithmetic and copies ran while one was open for 0% of the time, Pallas kernels for 22%

profile of v5, /device:TPU:0, one launch (start us, length us, event | category | flops | bytes accessed | tf_op | source)
XLA Modules:
  0.0 30.7 jit_solution(14568980873180768514)
XLA Ops:
  0.0 5.6 %block_states.1 = (bf16[8,1024,128]{2,1,0:T(8,128)(2,1)S(1)}, bf16[8,1024,128]{2,1,0:T(8,128)(2,1)S(1)}, bf16[8,160,128]{2,1,0:T(8,128)(2,1)S(1)}, bf16[1024,1024]{1,0:T(8,128)(2,1)S(1)}, f32[3,4,1024]{2,1,0:T(4,128)S(1)}) custom-call(bf16[1024,1024]{1,0:T(8,128)(2,1)} %q_hbm.1, bf16[1024,1024]{1,0:T(8,128)(2,1)} %k_hbm.1, bf16[1024,1024]{1,0:T(8,128)(2,1)} %v_hbm.1, ...), custom_call_target="tpu_custom_call" | custom-call | flops 268435456 | bytes 8388608 | tf_op jit(solution)/shard_map/block_states/pallas_call | solution.py:149
  5.7 3.0 %collective-permute-start = (bf16[2,160,128]{2,1,0:T(8,128)(2,1)S(1)}, bf16[2,160,128]{2,1,0:T(8,128)(2,1)S(1)}, u32[]{:S(2)}, u32[]{:S(2)}) collective-permute-start(bf16[2,160,128]{2,1,0:T(8,128)(2,1)S(1)} %get-tuple-element.83), channel_id=1, source_target_pairs={{0,1},{1,0},{2,3},{3,2},{4,5},{5,4},{6,7},{7,6},{8,9},{9,8},{10,11... | collective-permute-start | bytes 245768 | tf_op jit(solution)/shard_map/ppermute | solution.py:448
  8.7 1.6 %collective-permute-start.1 = (bf16[2,160,128]{2,1,0:T(8,128)(2,1)S(1)}, bf16[2,160,128]{2,1,0:T(8,128)(2,1)S(1)}, u32[]{:S(2)}, u32[]{:S(2)}) collective-permute-start(bf16[2,160,128]{2,1,0:T(8,128)(2,1)S(1)} %get-tuple-element.82), channel_id=1, source_target_pairs={{0,2},{1,3},{2,0},{3,1},{4,6},{5,7},{6,4},{7,5},{8,10},{9,11},{10,... | collective-permute-start | bytes 245768 | tf_op jit(solution)/shard_map/ppermute | solution.py:448
  10.3 0.0 collective-permute-start.2
  10.3 2.0 %inner_attention.3 = (bf16[4,1024,128]{2,1,0:T(8,128)(2,1)S(1)}, f32[4,1024,128]{2,1,0:T(8,128)S(1)}) custom-call(bf16[1024,1024]{1,0:T(8,128)(2,1)S(1)} %get-tuple-element.44.q_ref, bf16[8,1024,128]{2,1,0:T(8,128)(2,1)S(1)} %get-tuple-element.45.kf_ref, bf16[8,1024,128]{2,1,0:T(8,128)(2,1)S(1)} %get-tuple-element.46.vf_ref, ...), custom_call_target="tpu_custom_call" | custom-call | flops 536870912 | bytes 6291456 | tf_op jit(solution)/shard_map/inner_attention/pallas_call | solution.py:374
  12.3 0.0 collective-permute-done.refs_1_.p1
  12.3 1.6 %collective-permute-done.1.refs_2_.p2 = bf16[2,160,128]{2,1,0:T(8,128)(2,1)S(1)} collective-permute-done((bf16[2,160,128]{2,1,0:T(8,128)(2,1)S(1)}, bf16[2,160,128]{2,1,0:T(8,128)(2,1)S(1)}, u32[]{:S(2)}, u32[]{:S(2)}) %collective-permute-start.1) | collective-permute-done | bytes 81952 | tf_op jit(solution)/shard_map/ppermute | solution.py:448
  13.9 1.8 %collective-permute-done.2.refs_3_.p3 = bf16[2,160,128]{2,1,0:T(8,128)(2,1)S(1)} collective-permute-done((bf16[2,160,128]{2,1,0:T(8,128)(2,1)S(1)}, bf16[2,160,128]{2,1,0:T(8,128)(2,1)S(1)}, u32[]{:S(2)}, u32[]{:S(2)}) %collective-permute-start.2) | collective-permute-done | bytes 81952 | tf_op jit(solution)/shard_map/ppermute | solution.py:448
  15.6 0.2 group_total.1
  15.9 0.0 copy-start
  15.9 2.7 %collective-permute-start.3 = (bf16[2,144,128]{2,1,0:T(8,128)(2,1)S(1)}, bf16[2,144,128]{2,1,0:T(8,128)(2,1)S(1)}, u32[]{:S(2)}, u32[]{:S(2)}) collective-permute-start(bf16[2,144,128]{2,1,0:T(8,128)(2,1)S(1)} %group_total.1), channel_id=1, source_target_pairs={{0,4},{1,5},{2,6},{3,7},{4,0},{5,1},{6,2},{7,3},{8,12},{9,13},{10,... | collective-permute-start | bytes 221192 | tf_op jit(solution)/shard_map/ppermute | solution.py:448
  18.5 1.2 %inner_attention.4 = (bf16[2,1024,128]{2,1,0:T(8,128)(2,1)S(1)}, f32[2,1024,128]{2,1,0:T(8,128)S(1)}) custom-call(bf16[1024,1024]{1,0:T(8,128)(2,1)S(1)} %get-tuple-element.44.q_ref, bf16[8,1024,128]{2,1,0:T(8,128)(2,1)S(1)} %get-tuple-element.45.kf_ref, bf16[8,1024,128]{2,1,0:T(8,128)(2,1)S(1)} %get-tuple-element.46.vf_ref, ...), custom_call_target="tpu_custom_call" | custom-call | flops 268435456 | bytes 3145728 | tf_op jit(solution)/shard_map/inner_attention/pallas_call | solution.py:374
  19.7 0.6 %member_edges.1 = (bf16[3,2,16,128]{3,2,1,0:T(8,128)(2,1)S(1)}, f32[3,2,16,128]{3,2,1,0:T(8,128)S(1)}, f32[3,2,128,128]{3,2,1,0:T(8,128)S(1)}, f32[3,2,128,128]{3,2,1,0:T(8,128)S(1)}, bf16[2,32,128]{2,1,0:T(8,128)(2,1)S(1)}) custom-call(bf16[2,160,128]{2,1,0:T(8,128)(2,1)S(1)} %get-tuple-element.50.refs_0_.p0, ...), custom_call_target="tpu_custom_call" | custom-call | tf_op jit(solution)/shard_map/member_edges/pallas_call | solution.py:288
  20.3 1.6 %collective-permute-done.3.x_ref = bf16[2,144,128]{2,1,0:T(8,128)(2,1)S(1)} collective-permute-done((bf16[2,144,128]{2,1,0:T(8,128)(2,1)S(1)}, bf16[2,144,128]{2,1,0:T(8,128)(2,1)S(1)}, u32[]{:S(2)}, u32[]{:S(2)}) %collective-permute-start.3) | collective-permute-done | bytes 73760 | tf_op jit(solution)/shard_map/ppermute | solution.py:448
  21.9 0.0 copy-done
  21.9 0.6 %member_prefixes.1 = (bf16[2,144,128]{2,1,0:T(8,128)(2,1)S(1)}, bf16[2,144,128]{2,1,0:T(8,128)(2,1)S(1)}, bf16[2,144,128]{2,1,0:T(8,128)(2,1)S(1)}, bf16[2,144,128]{2,1,0:T(8,128)(2,1)S(1)}) custom-call(bf16[3,2,16,128]{3,2,1,0:T(8,128)(2,1)S(1)} %get-tuple-element.61.qf_ref, f32[3,2,16,128]{3,2,1,0:T(8,128)S(1)} %get-tuple-element.62.inner_ref, ...), custom_call_target="tpu_custom_call" | custom-call | tf_op jit(solution)/shard_map/member_prefixes/pallas_call | solution.py:334
  22.6 0.7 %collective-permute-start.5 = (bf16[2,144,128]{2,1,0:T(8,128)(2,1)S(1)}, bf16[2,144,128]{2,1,0:T(8,128)(2,1)S(1)}, u32[]{:S(2)}, u32[]{:S(2)}) collective-permute-start(bf16[2,144,128]{2,1,0:T(8,128)(2,1)S(1)} %get-tuple-element.68), channel_id=1, source_target_pairs={{0,1},{1,0},{2,3},{3,2},{4,5},{5,4},{6,7},{7,6},{8,9},{9,8},{10,11... | collective-permute-start | bytes 221192 | tf_op jit(solution)/shard_map/ppermute | solution.py:448
  23.2 0.5 %collective-permute-start.6 = (bf16[2,144,128]{2,1,0:T(8,128)(2,1)S(1)}, bf16[2,144,128]{2,1,0:T(8,128)(2,1)S(1)}, u32[]{:S(2)}, u32[]{:S(2)}) collective-permute-start(bf16[2,144,128]{2,1,0:T(8,128)(2,1)S(1)} %get-tuple-element.69), channel_id=1, source_target_pairs={{0,2},{1,3},{2,0},{3,1},{4,6},{5,7},{6,4},{7,5},{8,10},{9,11},{10,... | collective-permute-start | bytes 221192 | tf_op jit(solution)/shard_map/ppermute | solution.py:448
  23.8 2.3 %collective-permute-start.4 = (bf16[2,144,128]{2,1,0:T(8,128)(2,1)S(1)}, bf16[2,144,128]{2,1,0:T(8,128)(2,1)S(1)}, u32[]{:S(2)}, u32[]{:S(2)}) collective-permute-start(bf16[2,144,128]{2,1,0:T(8,128)(2,1)S(1)} %get-tuple-element.67), channel_id=1, source_target_pairs={{0,3},{1,2},{2,1},{3,0},{4,7},{5,6},{6,5},{7,4},{8,11},{9,10},{10,... | collective-permute-start | bytes 221192 | tf_op jit(solution)/shard_map/ppermute | solution.py:448
  26.1 1.2 %inner_attention.5 = (bf16[2,1024,128]{2,1,0:T(8,128)(2,1)S(1)}, f32[2,1024,128]{2,1,0:T(8,128)S(1)}) custom-call(bf16[1024,1024]{1,0:T(8,128)(2,1)S(1)} %get-tuple-element.44.q_ref, bf16[8,1024,128]{2,1,0:T(8,128)(2,1)S(1)} %get-tuple-element.45.kf_ref, bf16[8,1024,128]{2,1,0:T(8,128)(2,1)S(1)} %get-tuple-element.46.vf_ref, ...), custom_call_target="tpu_custom_call" | custom-call | flops 268435456 | bytes 3145728 | tf_op jit(solution)/shard_map/inner_attention/pallas_call | solution.py:374
  27.3 0.0 collective-permute-done.5.refs_1_
  27.3 0.3 collective-permute-done.6.refs_2_
  27.6 1.9 %finish.2.refs_3_ = bf16[1024,1024]{1,0:T(8,128)(2,1)} custom-call(f32[1,1024]{1,0:T(1,128)S(1)} %bitcast.2, bf16[2,144,128]{2,1,0:T(8,128)(2,1)S(1)} %get-tuple-element.74.refs_0_, bf16[2,144,128]{2,1,0:T(8,128)(2,1)S(1)} %collective-permute-done.5.refs_1_, bf16[2,144,128]{2,1,0:T(8,128)(2,1)S(1)} %collective-permute-done.6.refs_2_, ...), custom_call_target="tpu_custom_call" | custom-call | flops 201326592 | bytes 6291456 | tf_op jit(solution)/shard_map/finish/pallas_call | solution.py:426
  29.5 0.0 collective-permute-done.4.refs_0_
  29.5 1.2 %finish.3 = bf16[1024,1024]{1,0:T(8,128)(2,1)} custom-call(f32[1,1024]{1,0:T(1,128)S(1)} %bitcast.3, bf16[2,144,128]{2,1,0:T(8,128)(2,1)S(1)} %collective-permute-done.4.refs_0_, bf16[2,1024,128]{2,1,0:T(8,128)(2,1)S(1)} %get-tuple-element.72.refs_1_, f32[2,1024,128]{2,1,0:T(8,128)S(1)} %get-tuple-element.73.refs_2_, ...), custom_call_target="tpu_custom_call", output_to_operand_aliasing={{}: (4, {})} | custom-call | flops 67108864 | bytes 2097152 | tf_op jit(solution)/shard_map/finish/pallas_call | solution.py:426
  (1 shorter events, 0.0 us)
Async XLA Ops:
  5.7 6.6 %collective-permute-start = (bf16[2,160,128]{2,1,0:T(8,128)(2,1)S(1)}, bf16[2,160,128]{2,1,0:T(8,128)(2,1)S(1)}, u32[]{:S(2)}, u32[]{:S(2)}) collective-permute-start(bf16[2,160,128]{2,1,0:T(8,128)(2,1)S(1)} %get-tuple-element.83), channel_id=1, source_target_pairs={{0,1},{1,0},{2,3},{3,2},{4,5},{5,4},{6,7},{7,6},{8,9},{9,8},{10,11... | collective-permute-start | bytes 245768 | tf_op jit(solution)/shard_map/ppermute | solution.py:448
  8.7 5.1 %collective-permute-start.1 = (bf16[2,160,128]{2,1,0:T(8,128)(2,1)S(1)}, bf16[2,160,128]{2,1,0:T(8,128)(2,1)S(1)}, u32[]{:S(2)}, u32[]{:S(2)}) collective-permute-start(bf16[2,160,128]{2,1,0:T(8,128)(2,1)S(1)} %get-tuple-element.82), channel_id=1, source_target_pairs={{0,2},{1,3},{2,0},{3,1},{4,6},{5,7},{6,4},{7,5},{8,10},{9,11},{10,... | collective-permute-start | bytes 245768 | tf_op jit(solution)/shard_map/ppermute | solution.py:448
  10.3 5.3 %collective-permute-start.2 = (bf16[2,160,128]{2,1,0:T(8,128)(2,1)S(1)}, bf16[2,160,128]{2,1,0:T(8,128)(2,1)S(1)}, u32[]{:S(2)}, u32[]{:S(2)}) collective-permute-start(bf16[2,160,128]{2,1,0:T(8,128)(2,1)S(1)} %get-tuple-element.81), channel_id=1, source_target_pairs={{0,3},{1,2},{2,1},{3,0},{4,7},{5,6},{6,5},{7,4},{8,11},{9,10},{10,... | collective-permute-start | bytes 245768 | tf_op jit(solution)/shard_map/ppermute | solution.py:448
  15.9 6.1 %copy-start = (f32[1024]{0:T(1024)S(1)}, f32[1024]{0:T(1024)}, u32[]{:S(2)}) copy-start(f32[1024]{0:T(1024)} %param.9) | copy-start | bytes 12292
  15.9 6.1 %collective-permute-start.3 = (bf16[2,144,128]{2,1,0:T(8,128)(2,1)S(1)}, bf16[2,144,128]{2,1,0:T(8,128)(2,1)S(1)}, u32[]{:S(2)}, u32[]{:S(2)}) collective-permute-start(bf16[2,144,128]{2,1,0:T(8,128)(2,1)S(1)} %group_total.1), channel_id=1, source_target_pairs={{0,4},{1,5},{2,6},{3,7},{4,0},{5,1},{6,2},{7,3},{8,12},{9,13},{10,... | collective-permute-start | bytes 221192 | tf_op jit(solution)/shard_map/ppermute | solution.py:448
  22.6 4.7 %collective-permute-start.5 = (bf16[2,144,128]{2,1,0:T(8,128)(2,1)S(1)}, bf16[2,144,128]{2,1,0:T(8,128)(2,1)S(1)}, u32[]{:S(2)}, u32[]{:S(2)}) collective-permute-start(bf16[2,144,128]{2,1,0:T(8,128)(2,1)S(1)} %get-tuple-element.68), channel_id=1, source_target_pairs={{0,1},{1,0},{2,3},{3,2},{4,5},{5,4},{6,7},{7,6},{8,9},{9,8},{10,11... | collective-permute-start | bytes 221192 | tf_op jit(solution)/shard_map/ppermute | solution.py:448
  23.2 4.4 %collective-permute-start.6 = (bf16[2,144,128]{2,1,0:T(8,128)(2,1)S(1)}, bf16[2,144,128]{2,1,0:T(8,128)(2,1)S(1)}, u32[]{:S(2)}, u32[]{:S(2)}) collective-permute-start(bf16[2,144,128]{2,1,0:T(8,128)(2,1)S(1)} %get-tuple-element.69), channel_id=1, source_target_pairs={{0,2},{1,3},{2,0},{3,1},{4,6},{5,7},{6,4},{7,5},{8,10},{9,11},{10,... | collective-permute-start | bytes 221192 | tf_op jit(solution)/shard_map/ppermute | solution.py:448
  23.8 5.7 %collective-permute-start.4 = (bf16[2,144,128]{2,1,0:T(8,128)(2,1)S(1)}, bf16[2,144,128]{2,1,0:T(8,128)(2,1)S(1)}, u32[]{:S(2)}, u32[]{:S(2)}) collective-permute-start(bf16[2,144,128]{2,1,0:T(8,128)(2,1)S(1)} %get-tuple-element.67), channel_id=1, source_target_pairs={{0,3},{1,2},{2,1},{3,0},{4,7},{5,6},{6,5},{7,4},{8,11},{9,10},{10,... | collective-permute-start | bytes 221192 | tf_op jit(solution)/shard_map/ppermute | solution.py:448

commit v6 on v5

--- a/solution.py
+++ b/solution.py
@@ -10,9 +10,10 @@
 HDIM = 128
 CONV = 4
 GROUP = 4
-ROWS = 256
+ROWS = 64
 CHUNK = 256
 PARTS = 4
+AHEAD = 2
 PAIR = 2
 AUX = 32
 TAIL = 16
@@ -63,21 +64,22 @@
 
 
 def state_kernel(q_hbm, k_hbm, v_hbm, w_hbm, kf_ref, vf_ref, msg_ref, q_ref, w_ref, k_buf, v_buf, wide, k_sem, v_sem, sem):
-    heads, tokens = k_buf.shape[0:2]
-
-    def fetch(source, target, semaphore, h):
-        cols = pl.ds(pl.multiple_of(h * HDIM, HDIM), HDIM)
-        return pltpu.make_async_copy(source.at[:, cols], target.at[h], semaphore.at[h])
-
-    def fetch_pair(first):
-        for source, target, semaphore in ((k_hbm, k_buf, k_sem), (v_hbm, v_buf, v_sem)):
-            for u in range(PAIR):
-                fetch(source, target, semaphore, first + u).start()
+    pairs, tokens = k_buf.shape[0:2]
+    heads = pairs * PAIR
+
+    def fetch(source, target, semaphore, i):
+        cols = pl.ds(pl.multiple_of(i * PAIR * HDIM, PAIR * HDIM), PAIR * HDIM)
+        return pltpu.make_async_copy(source.at[:, cols], target.at[i], semaphore.at[i])
+
+    def fetch_pair(i):
+        fetch(k_hbm, k_buf, k_sem, i).start()
+        fetch(v_hbm, v_buf, v_sem, i).start()
 
     fetch_taps = pltpu.make_async_copy(w_hbm, w_ref, sem.at[0])
     fetch_queries = pltpu.make_async_copy(q_hbm, q_ref, sem.at[1])
     fetch_taps.start()
-    fetch_pair(0)
+    for i in range(AHEAD):
+        fetch_pair(i)
     for u in range(PAIR):
         for a in range(2):
             wide[u, a, 0:8] = jnp.zeros((8, HDIM), F32)
@@ -86,28 +88,26 @@
     def some_heads(i, carry):
         first = i * PAIR
 
-        @pl.when(first + PAIR < heads)
+        @pl.when(i + AHEAD < pairs)
         def _():
-            fetch_pair(first + PAIR)
-
-        @pl.when(first + 2 * PAIR == heads)
+            fetch_pair(i + AHEAD)
+
+        @pl.when(i + 2 == pairs)
         def _():
             fetch_queries.start()
 
-        for u in range(PAIR):
-            fetch(k_hbm, k_buf, k_sem, first + u).wait()
+        fetch(k_hbm, k_buf, k_sem, i).wait()
         for u in range(PAIR):
             h = first + u
             wk = w_ref[1, :, pl.ds(pl.multiple_of(h * HDIM, HDIM), HDIM)] * 0.5
             for start in range(0, tokens, ROWS):
                 rows = slice(start, start + ROWS)
-                wide[u, 0, start + 8 : start + 8 + ROWS] = k_buf[h, rows].astype(F32)
+                wide[u, 0, start + 8 : start + 8 + ROWS] = k_buf[i, rows, u * HDIM : (u + 1) * HDIM].astype(F32)
                 kf = silu_of_twice(conv_from(wide.at[u, 0], rows, wk))
                 if start == 0:
                     kf = jnp.where(rows_iota(kf.shape) < CONV - 1, 0.0, kf)
                 kf_ref[h, rows] = kf.astype(BF16)
-        for u in range(PAIR):
-            fetch(v_hbm, v_buf, v_sem, first + u).wait()
+        fetch(v_hbm, v_buf, v_sem, i).wait()
         for u in range(PAIR):
             h = first + u
             cols = pl.ds(pl.multiple_of(h * HDIM, HDIM), HDIM)
@@ -115,15 +115,16 @@
             local = jnp.zeros((HDIM, HDIM), F32)
             for start in range(0, tokens, ROWS):
                 rows = slice(start, start + ROWS)
-                wide[u, 1, start + 8 : start + 8 + ROWS] = v_buf[h, rows].astype(F32)
+                wide[u, 1, start + 8 : start + 8 + ROWS] = v_buf[i, rows, u * HDIM : (u + 1) * HDIM].astype(F32)
                 vf = conv_from(wide.at[u, 1], rows, wv).astype(BF16)
                 vf_ref[h, rows] = vf
                 local = local + dot(kf_ref[h, rows], vf, ((0,), (0,)))
             per = heads // GROUP
             place = (lax.div(h, per) ^ member()) * per + lax.rem(h, per)
             msg_ref[place, 0:HDIM] = local.astype(BF16)
-            mk = merged_rows(k_buf[h, 0:16], k_buf[h, tokens - 16 : tokens])
-            mv = merged_rows(v_buf[h, 0:16], v_buf[h, tokens - 16 : tokens])
+            own = slice(u * HDIM, (u + 1) * HDIM)
+            mk = merged_rows(k_buf[i, 0:16, own], k_buf[i, tokens - 16 : tokens, own])
+            mv = merged_rows(v_buf[i, 0:16, own], v_buf[i, tokens - 16 : tokens, own])
             msg_ref[place, HDIM : HDIM + 16] = jnp.concatenate([mk, mv], axis=0).astype(BF16)
         return carry
 
@@ -158,11 +159,11 @@
             jax.ShapeDtypeStruct(conv_weight.shape, F32),
         ],
         scratch_shapes=[
-            pltpu.VMEM((heads, tokens, HDIM), BF16),
-            pltpu.VMEM((heads, tokens, HDIM), BF16),
+            pltpu.VMEM((heads // PAIR, tokens, PAIR * HDIM), BF16),
+            pltpu.VMEM((heads // PAIR, tokens, PAIR * HDIM), BF16),
             pltpu.VMEM((PAIR, 2, tokens + 8, HDIM), F32),
-            pltpu.SemaphoreType.DMA((heads,)),
-            pltpu.SemaphoreType.DMA((heads,)),
+            pltpu.SemaphoreType.DMA((heads // PAIR,)),
+            pltpu.SemaphoreType.DMA((heads // PAIR,)),
             pltpu.SemaphoreType.DMA((2,)),
         ],
         compiler_params=pltpu.CompilerParams(vmem_limit_bytes=24 << 20),
@@ -464,9 +465,9 @@
         piece = inner_attention(quarters, queries, kf, vf, conv_weight)
         return lax.optimization_barrier((arrays, piece))
 
-    packets = [messages[0:heads]]
-    packets += [swapped(messages[j * heads : (j + 1) * heads], j) for j in range(1, GROUP)]
+    packets = [swapped(messages[j * heads : (j + 1) * heads], j) for j in (3, 2, 1)]
     packets, piece01 = beside((0, 1), packets)
+    packets = [messages[0:heads]] + packets[::-1]
     if groups == 2:
         incoming = swapped(group_total(packets, None, conv_weight), GROUP)
     else:

time: 30.9 us -> 29.5 us (0.955)
  waiting for transfers between devices: 5.23 us -> 4.32 us
  Pallas kernels: 14.5 us -> 14 us
    ppermute x7, waiting for transfers between devices: 5.23 us -> 4.32 us  [swapped(): return lax.ppermute(value, 'ctx', [(s, s ^ bits) for s in range(count)])]
    pallas_call x1, Pallas kernels: 5.64 us -> 5.15 us  [block_states(): pl.pallas_call(state_kernel, in_specs=[HBM, HBM, HBM, HBM], out_specs=[VM...]
  transfers between devices with their start and end apart: 7 -> 7, of which waited for: 4 -> 7; matrix products, arithmetic and copies ran while one was open for 0% -> 0% of each run, Pallas kernels for 22% -> 23%
where the time goes in v6:
time: 29.5 us; the launch traced here: 29.4 us
  Pallas kernels  14 us (47%)
  starting transfers between devices  10.9 us (37%)
  waiting for transfers between devices  4.32 us (15%)
    ppermute x7, starting transfers between devices, swapped(): return lax.ppermute(value, 'ctx', [(s, s ^ bits) for s in range(count)])  10.9 us
    pallas_call x1, Pallas kernels, block_states(): pl.pallas_call(state_kernel, in_specs=[HBM, HBM, HBM, HBM], out_specs=[VM...  5.15 us
    pallas_call x3, Pallas kernels, inner_attention(): pl.pallas_call(functools.partial(inner_kernel, quarters), in_specs=[VMEM]...  4.34 us
    ppermute x7, waiting for transfers between devices, swapped(): return lax.ppermute(value, 'ctx', [(s, s ^ bits) for s in range(count)])  4.32 us
    pallas_call x2, Pallas kernels, finish(): pl.pallas_call(functools.partial(finish_kernel, quarters, places, len(oth...  3.08 us
    pallas_call x1, Pallas kernels, member_prefixes(): pl.pallas_call(prefix_kernel, in_specs=[VMEM] * (len(edges) + 3), out_spe...  0.62 us
    pallas_call x1, Pallas kernels, member_edges(): pl.pallas_call(edges_kernel, in_specs=[VMEM] * (GROUP + 1), out_specs=[VM...  0.61 us
  transfers between devices with their start and end apart: 7, of which 7 were waited for; matrix products, arithmetic and copies ran while one was open for 0% of the time, Pallas kernels for 23%

profile of v6, /device:TPU:0, one launch (start us, length us, event | category | flops | bytes accessed | tf_op | source)
XLA Modules:
  0.0 29.4 jit_solution(10922455712065265726)
XLA Ops:
  0.0 5.2 %block_states.1 = (bf16[8,1024,128]{2,1,0:T(8,128)(2,1)S(1)}, bf16[8,1024,128]{2,1,0:T(8,128)(2,1)S(1)}, bf16[8,160,128]{2,1,0:T(8,128)(2,1)S(1)}, bf16[1024,1024]{1,0:T(8,128)(2,1)S(1)}, f32[3,4,1024]{2,1,0:T(4,128)S(1)}) custom-call(bf16[1024,1024]{1,0:T(8,128)(2,1)} %q_hbm.1, bf16[1024,1024]{1,0:T(8,128)(2,1)} %k_hbm.1, bf16[1024,1024]{1,0:T(8,128)(2,1)} %v_hbm.1, ...), custom_call_target="tpu_custom_call" | custom-call | flops 268435456 | bytes 8388608 | tf_op jit(solution)/shard_map/block_states/pallas_call | solution.py:150
  5.2 4.0 %collective-permute-start = (bf16[2,160,128]{2,1,0:T(8,128)(2,1)S(1)}, bf16[2,160,128]{2,1,0:T(8,128)(2,1)S(1)}, u32[]{:S(2)}, u32[]{:S(2)}) collective-permute-start(bf16[2,160,128]{2,1,0:T(8,128)(2,1)S(1)} %get-tuple-element.81), channel_id=1, source_target_pairs={{0,3},{1,2},{2,1},{3,0},{4,7},{5,6},{6,5},{7,4},{8,11},{9,10},{10,... | collective-permute-start | bytes 245768 | tf_op jit(solution)/shard_map/ppermute | solution.py:449
  9.2 0.4 %collective-permute-start.1 = (bf16[2,160,128]{2,1,0:T(8,128)(2,1)S(1)}, bf16[2,160,128]{2,1,0:T(8,128)(2,1)S(1)}, u32[]{:S(2)}, u32[]{:S(2)}) collective-permute-start(bf16[2,160,128]{2,1,0:T(8,128)(2,1)S(1)} %get-tuple-element.80), channel_id=1, source_target_pairs={{0,2},{1,3},{2,0},{3,1},{4,6},{5,7},{6,4},{7,5},{8,10},{9,11},{10,... | collective-permute-start | bytes 245768 | tf_op jit(solution)/shard_map/ppermute | solution.py:449
  9.7 0.2 collective-permute-start.2
  9.9 2.0 %inner_attention.3 = (bf16[4,1024,128]{2,1,0:T(8,128)(2,1)S(1)}, f32[4,1024,128]{2,1,0:T(8,128)S(1)}) custom-call(bf16[1024,1024]{1,0:T(8,128)(2,1)S(1)} %get-tuple-element.43.q_ref, bf16[8,1024,128]{2,1,0:T(8,128)(2,1)S(1)} %get-tuple-element.44.kf_ref, bf16[8,1024,128]{2,1,0:T(8,128)(2,1)S(1)} %get-tuple-element.45.vf_ref, ...), custom_call_target="tpu_custom_call" | custom-call | flops 536870912 | bytes 6291456 | tf_op jit(solution)/shard_map/inner_attention/pallas_call | solution.py:375
  11.9 0.2 collective-permute-done.refs_3_.p3
  12.1 1.8 %collective-permute-done.1.refs_2_.p2 = bf16[2,160,128]{2,1,0:T(8,128)(2,1)S(1)} collective-permute-done((bf16[2,160,128]{2,1,0:T(8,128)(2,1)S(1)}, bf16[2,160,128]{2,1,0:T(8,128)(2,1)S(1)}, u32[]{:S(2)}, u32[]{:S(2)}) %collective-permute-start.1) | collective-permute-done | bytes 81952 | tf_op jit(solution)/shard_map/ppermute | solution.py:449
  13.9 0.3 collective-permute-done.2.refs_1_.p1
  14.1 0.2 group_total.1
  14.4 0.0 copy-start
  14.4 2.7 %collective-permute-start.3 = (bf16[2,144,128]{2,1,0:T(8,128)(2,1)S(1)}, bf16[2,144,128]{2,1,0:T(8,128)(2,1)S(1)}, u32[]{:S(2)}, u32[]{:S(2)}) collective-permute-start(bf16[2,144,128]{2,1,0:T(8,128)(2,1)S(1)} %group_total.1), channel_id=1, source_target_pairs={{0,4},{1,5},{2,6},{3,7},{4,0},{5,1},{6,2},{7,3},{8,12},{9,13},{10,... | collective-permute-start | bytes 221192 | tf_op jit(solution)/shard_map/ppermute | solution.py:449
  17.0 1.2 %inner_attention.4 = (bf16[2,1024,128]{2,1,0:T(8,128)(2,1)S(1)}, f32[2,1024,128]{2,1,0:T(8,128)S(1)}) custom-call(bf16[1024,1024]{1,0:T(8,128)(2,1)S(1)} %get-tuple-element.43.q_ref, bf16[8,1024,128]{2,1,0:T(8,128)(2,1)S(1)} %get-tuple-element.44.kf_ref, bf16[8,1024,128]{2,1,0:T(8,128)(2,1)S(1)} %get-tuple-element.45.vf_ref, ...), custom_call_target="tpu_custom_call" | custom-call | flops 268435456 | bytes 3145728 | tf_op jit(solution)/shard_map/inner_attention/pallas_call | solution.py:375
  18.2 0.6 %member_edges.1 = (bf16[3,2,16,128]{3,2,1,0:T(8,128)(2,1)S(1)}, f32[3,2,16,128]{3,2,1,0:T(8,128)S(1)}, f32[3,2,128,128]{3,2,1,0:T(8,128)S(1)}, f32[3,2,128,128]{3,2,1,0:T(8,128)S(1)}, bf16[2,32,128]{2,1,0:T(8,128)(2,1)S(1)}) custom-call(bf16[2,160,128]{2,1,0:T(8,128)(2,1)S(1)} %get-tuple-element.82.refs_0_.p0, ...), custom_call_target="tpu_custom_call" | custom-call | tf_op jit(solution)/shard_map/member_edges/pallas_call | solution.py:289
  18.8 0.9 %collective-permute-done.3.x_ref = bf16[2,144,128]{2,1,0:T(8,128)(2,1)S(1)} collective-permute-done((bf16[2,144,128]{2,1,0:T(8,128)(2,1)S(1)}, bf16[2,144,128]{2,1,0:T(8,128)(2,1)S(1)}, u32[]{:S(2)}, u32[]{:S(2)}) %collective-permute-start.3) | collective-permute-done | bytes 73760 | tf_op jit(solution)/shard_map/ppermute | solution.py:449
  19.7 0.0 copy-done
  19.7 0.6 %member_prefixes.1 = (bf16[2,144,128]{2,1,0:T(8,128)(2,1)S(1)}, bf16[2,144,128]{2,1,0:T(8,128)(2,1)S(1)}, bf16[2,144,128]{2,1,0:T(8,128)(2,1)S(1)}, bf16[2,144,128]{2,1,0:T(8,128)(2,1)S(1)}) custom-call(bf16[3,2,16,128]{3,2,1,0:T(8,128)(2,1)S(1)} %get-tuple-element.59.qf_ref, f32[3,2,16,128]{3,2,1,0:T(8,128)S(1)} %get-tuple-element.60.inner_ref, ...), custom_call_target="tpu_custom_call" | custom-call | tf_op jit(solution)/shard_map/member_prefixes/pallas_call | solution.py:335
  20.3 1.1 %collective-permute-start.5 = (bf16[2,144,128]{2,1,0:T(8,128)(2,1)S(1)}, bf16[2,144,128]{2,1,0:T(8,128)(2,1)S(1)}, u32[]{:S(2)}, u32[]{:S(2)}) collective-permute-start(bf16[2,144,128]{2,1,0:T(8,128)(2,1)S(1)} %get-tuple-element.66), channel_id=1, source_target_pairs={{0,1},{1,0},{2,3},{3,2},{4,5},{5,4},{6,7},{7,6},{8,9},{9,8},{10,11... | collective-permute-start | bytes 221192 | tf_op jit(solution)/shard_map/ppermute | solution.py:449
  21.4 1.5 %collective-permute-start.6 = (bf16[2,144,128]{2,1,0:T(8,128)(2,1)S(1)}, bf16[2,144,128]{2,1,0:T(8,128)(2,1)S(1)}, u32[]{:S(2)}, u32[]{:S(2)}) collective-permute-start(bf16[2,144,128]{2,1,0:T(8,128)(2,1)S(1)} %get-tuple-element.67), channel_id=1, source_target_pairs={{0,2},{1,3},{2,0},{3,1},{4,6},{5,7},{6,4},{7,5},{8,10},{9,11},{10,... | collective-permute-start | bytes 221192 | tf_op jit(solution)/shard_map/ppermute | solution.py:449
  22.9 1.0 %collective-permute-start.4 = (bf16[2,144,128]{2,1,0:T(8,128)(2,1)S(1)}, bf16[2,144,128]{2,1,0:T(8,128)(2,1)S(1)}, u32[]{:S(2)}, u32[]{:S(2)}) collective-permute-start(bf16[2,144,128]{2,1,0:T(8,128)(2,1)S(1)} %get-tuple-element.65), channel_id=1, source_target_pairs={{0,3},{1,2},{2,1},{3,0},{4,7},{5,6},{6,5},{7,4},{8,11},{9,10},{10,... | collective-permute-start | bytes 221192 | tf_op jit(solution)/shard_map/ppermute | solution.py:449
  23.9 1.2 %inner_attention.5 = (bf16[2,1024,128]{2,1,0:T(8,128)(2,1)S(1)}, f32[2,1024,128]{2,1,0:T(8,128)S(1)}) custom-call(bf16[1024,1024]{1,0:T(8,128)(2,1)S(1)} %get-tuple-element.43.q_ref, bf16[8,1024,128]{2,1,0:T(8,128)(2,1)S(1)} %get-tuple-element.44.kf_ref, bf16[8,1024,128]{2,1,0:T(8,128)(2,1)S(1)} %get-tuple-element.45.vf_ref, ...), custom_call_target="tpu_custom_call" | custom-call | flops 268435456 | bytes 3145728 | tf_op jit(solution)/shard_map/inner_attention/pallas_call | solution.py:375
  25.1 0.5 %collective-permute-done.5.refs_1_ = bf16[2,144,128]{2,1,0:T(8,128)(2,1)S(1)} collective-permute-done((bf16[2,144,128]{2,1,0:T(8,128)(2,1)S(1)}, bf16[2,144,128]{2,1,0:T(8,128)(2,1)S(1)}, u32[]{:S(2)}, u32[]{:S(2)}) %collective-permute-start.5) | collective-permute-done | bytes 73760 | tf_op jit(solution)/shard_map/ppermute | solution.py:449
  25.5 0.3 collective-permute-done.6.refs_2_
  25.8 1.9 %finish.2.refs_3_ = bf16[1024,1024]{1,0:T(8,128)(2,1)} custom-call(f32[1,1024]{1,0:T(1,128)S(1)} %bitcast.2, bf16[2,144,128]{2,1,0:T(8,128)(2,1)S(1)} %get-tuple-element.72.refs_0_, bf16[2,144,128]{2,1,0:T(8,128)(2,1)S(1)} %collective-permute-done.5.refs_1_, bf16[2,144,128]{2,1,0:T(8,128)(2,1)S(1)} %collective-permute-done.6.refs_2_, ...), custom_call_target="tpu_custom_call" | custom-call | flops 201326592 | bytes 6291456 | tf_op jit(solution)/shard_map/finish/pallas_call | solution.py:427
  27.7 0.5 %collective-permute-done.4.refs_0_ = bf16[2,144,128]{2,1,0:T(8,128)(2,1)S(1)} collective-permute-done((bf16[2,144,128]{2,1,0:T(8,128)(2,1)S(1)}, bf16[2,144,128]{2,1,0:T(8,128)(2,1)S(1)}, u32[]{:S(2)}, u32[]{:S(2)}) %collective-permute-start.4) | collective-permute-done | bytes 73760 | tf_op jit(solution)/shard_map/ppermute | solution.py:449
  28.2 1.2 %finish.3 = bf16[1024,1024]{1,0:T(8,128)(2,1)} custom-call(f32[1,1024]{1,0:T(1,128)S(1)} %bitcast.3, bf16[2,144,128]{2,1,0:T(8,128)(2,1)S(1)} %collective-permute-done.4.refs_0_, bf16[2,1024,128]{2,1,0:T(8,128)(2,1)S(1)} %get-tuple-element.70.refs_1_, f32[2,1024,128]{2,1,0:T(8,128)S(1)} %get-tuple-element.71.refs_2_, ...), custom_call_target="tpu_custom_call", output_to_operand_aliasing={{}: (4, {})} | custom-call | flops 67108864 | bytes 2097152 | tf_op jit(solution)/shard_map/finish/pallas_call | solution.py:427
  (1 shorter events, 0.0 us)
Async XLA Ops:
  5.2 6.9 %collective-permute-start = (bf16[2,160,128]{2,1,0:T(8,128)(2,1)S(1)}, bf16[2,160,128]{2,1,0:T(8,128)(2,1)S(1)}, u32[]{:S(2)}, u32[]{:S(2)}) collective-permute-start(bf16[2,160,128]{2,1,0:T(8,128)(2,1)S(1)} %get-tuple-element.81), channel_id=1, source_target_pairs={{0,3},{1,2},{2,1},{3,0},{4,7},{5,6},{6,5},{7,4},{8,11},{9,10},{10,... | collective-permute-start | bytes 245768 | tf_op jit(solution)/shard_map/ppermute | solution.py:449
  9.2 4.6 %collective-permute-start.1 = (bf16[2,160,128]{2,1,0:T(8,128)(2,1)S(1)}, bf16[2,160,128]{2,1,0:T(8,128)(2,1)S(1)}, u32[]{:S(2)}, u32[]{:S(2)}) collective-permute-start(bf16[2,160,128]{2,1,0:T(8,128)(2,1)S(1)} %get-tuple-element.80), channel_id=1, source_target_pairs={{0,2},{1,3},{2,0},{3,1},{4,6},{5,7},{6,4},{7,5},{8,10},{9,11},{10,... | collective-permute-start | bytes 245768 | tf_op jit(solution)/shard_map/ppermute | solution.py:449
  9.7 4.4 %collective-permute-start.2 = (bf16[2,160,128]{2,1,0:T(8,128)(2,1)S(1)}, bf16[2,160,128]{2,1,0:T(8,128)(2,1)S(1)}, u32[]{:S(2)}, u32[]{:S(2)}) collective-permute-start(bf16[2,160,128]{2,1,0:T(8,128)(2,1)S(1)} %get-tuple-element.79), channel_id=1, source_target_pairs={{0,1},{1,0},{2,3},{3,2},{4,5},{5,4},{6,7},{7,6},{8,9},{9,8},{10,11... | collective-permute-start | bytes 245768 | tf_op jit(solution)/shard_map/ppermute | solution.py:449
  14.4 5.3 %copy-start = (f32[1024]{0:T(1024)S(1)}, f32[1024]{0:T(1024)}, u32[]{:S(2)}) copy-start(f32[1024]{0:T(1024)} %param.9) | copy-start | bytes 12292
  14.4 5.3 %collective-permute-start.3 = (bf16[2,144,128]{2,1,0:T(8,128)(2,1)S(1)}, bf16[2,144,128]{2,1,0:T(8,128)(2,1)S(1)}, u32[]{:S(2)}, u32[]{:S(2)}) collective-permute-start(bf16[2,144,128]{2,1,0:T(8,128)(2,1)S(1)} %group_total.1), channel_id=1, source_target_pairs={{0,4},{1,5},{2,6},{3,7},{4,0},{5,1},{6,2},{7,3},{8,12},{9,13},{10,... | collective-permute-start | bytes 221192 | tf_op jit(solution)/shard_map/ppermute | solution.py:449
  20.3 5.2 %collective-permute-start.5 = (bf16[2,144,128]{2,1,0:T(8,128)(2,1)S(1)}, bf16[2,144,128]{2,1,0:T(8,128)(2,1)S(1)}, u32[]{:S(2)}, u32[]{:S(2)}) collective-permute-start(bf16[2,144,128]{2,1,0:T(8,128)(2,1)S(1)} %get-tuple-element.66), channel_id=1, source_target_pairs={{0,1},{1,0},{2,3},{3,2},{4,5},{5,4},{6,7},{7,6},{8,9},{9,8},{10,11... | collective-permute-start | bytes 221192 | tf_op jit(solution)/shard_map/ppermute | solution.py:449
  21.4 4.4 %collective-permute-start.6 = (bf16[2,144,128]{2,1,0:T(8,128)(2,1)S(1)}, bf16[2,144,128]{2,1,0:T(8,128)(2,1)S(1)}, u32[]{:S(2)}, u32[]{:S(2)}) collective-permute-start(bf16[2,144,128]{2,1,0:T(8,128)(2,1)S(1)} %get-tuple-element.67), channel_id=1, source_target_pairs={{0,2},{1,3},{2,0},{3,1},{4,6},{5,7},{6,4},{7,5},{8,10},{9,11},{10,... | collective-permute-start | bytes 221192 | tf_op jit(solution)/shard_map/ppermute | solution.py:449
  22.9 5.3 %collective-permute-start.4 = (bf16[2,144,128]{2,1,0:T(8,128)(2,1)S(1)}, bf16[2,144,128]{2,1,0:T(8,128)(2,1)S(1)}, u32[]{:S(2)}, u32[]{:S(2)}) collective-permute-start(bf16[2,144,128]{2,1,0:T(8,128)(2,1)S(1)} %get-tuple-element.65), channel_id=1, source_target_pairs={{0,3},{1,2},{2,1},{3,0},{4,7},{5,6},{6,5},{7,4},{8,11},{9,10},{10,... | collective-permute-start | bytes 221192 | tf_op jit(solution)/shard_map/ppermute | solution.py:449

commit v7 on v6

--- a/solution.py
+++ b/solution.py
@@ -13,8 +13,8 @@
 ROWS = 64
 CHUNK = 256
 PARTS = 4
-AHEAD = 2
-PAIR = 2
+AHEAD = 1
+PAIR = 4
 AUX = 32
 TAIL = 16
 FIX = 16
@@ -466,7 +466,7 @@
         return lax.optimization_barrier((arrays, piece))
 
     packets = [swapped(messages[j * heads : (j + 1) * heads], j) for j in (3, 2, 1)]
-    packets, piece01 = beside((0, 1), packets)
+    packets, piece_a = beside((0, 3), packets)
     packets = [messages[0:heads]] + packets[::-1]
     if groups == 2:
         incoming = swapped(group_total(packets, None, conv_weight), GROUP)
@@ -481,13 +481,13 @@
             passed = prefix + total
         incoming = jnp.concatenate([prefix.astype(BF16), tail], axis=1)
     edges = member_edges(packets, conv_weight)
-    (incoming, edges), piece2 = beside((2,), (incoming, edges))
+    (incoming, edges), piece_b = beside((2,), (incoming, edges))
     sends = member_prefixes(edges, incoming, conv_weight, gain)
-    near = [swapped(sends[j], j) for j in (1, 2)]
-    far = swapped(sends[3], 3)
-    near, piece3 = beside((3,), near)
-    out = finish((0, 1, 2), [sends[0]] + near, [piece01, piece01, piece2], (0, 1, 0), gain)
-    return finish((3,), [far], [piece3], (0,), gain, out)
+    first = [swapped(sends[j], j) for j in (3,)]
+    last = [swapped(sends[j], j) for j in (2, 1)]
+    first, piece_c = beside((1,), first)
+    out = finish((0, 3), [sends[0]] + first, [piece_a, piece_a], (0, 1, ), gain)
+    return finish((2, 1), last, [piece_b, piece_c], (0, 0, ), gain, out)
 
 
 def solution(mesh):

time: 29.5 us -> 28.8 us (0.976)
  waiting for transfers between devices: 4.32 us -> 3.83 us
    ppermute x7, waiting for transfers between devices: 4.32 us -> 3.83 us  [swapped(): return lax.ppermute(value, 'ctx', [(s, s ^ bits) for s in range(count)])]
  transfers between devices with their start and end apart: 7 -> 7, of which waited for: 7 -> 5; matrix products, arithmetic and copies ran while one was open for 0% -> 0% of each run, Pallas kernels for 23% -> 22%
where the time goes in v7:
time: 28.8 us; the launch traced here: 28.7 us
  Pallas kernels  13.8 us (48%)
  starting transfers between devices  10.9 us (38%)
  waiting for transfers between devices  3.83 us (13%)
    ppermute x7, starting transfers between devices, swapped(): return lax.ppermute(value, 'ctx', [(s, s ^ bits) for s in range(count)])  10.9 us
    pallas_call x1, Pallas kernels, block_states(): pl.pallas_call(state_kernel, in_specs=[HBM, HBM, HBM, HBM], out_specs=[VM...  5.01 us
    pallas_call x3, Pallas kernels, inner_attention(): pl.pallas_call(functools.partial(inner_kernel, quarters), in_specs=[VMEM]...  4.31 us
    ppermute x7, waiting for transfers between devices, swapped(): return lax.ppermute(value, 'ctx', [(s, s ^ bits) for s in range(count)])  3.83 us
    pallas_call x2, Pallas kernels, finish(): pl.pallas_call(functools.partial(finish_kernel, quarters, places, len(oth...  3.05 us
    pallas_call x1, Pallas kernels, member_prefixes(): pl.pallas_call(prefix_kernel, in_specs=[VMEM] * (len(edges) + 3), out_spe...  0.62 us
    pallas_call x1, Pallas kernels, member_edges(): pl.pallas_call(edges_kernel, in_specs=[VMEM] * (GROUP + 1), out_specs=[VM...  0.61 us
  transfers between devices with their start and end apart: 7, of which 5 were waited for; matrix products, arithmetic and copies ran while one was open for 0% of the time, Pallas kernels for 22%

profile of v7, /device:TPU:0, one launch (start us, length us, event | category | flops | bytes accessed | tf_op | source)
XLA Modules:
  0.0 28.7 jit_solution(8378876082528850213)
XLA Ops:
  0.0 5.0 %block_states.1 = (bf16[8,1024,128]{2,1,0:T(8,128)(2,1)S(1)}, bf16[8,1024,128]{2,1,0:T(8,128)(2,1)S(1)}, bf16[8,160,128]{2,1,0:T(8,128)(2,1)S(1)}, bf16[1024,1024]{1,0:T(8,128)(2,1)S(1)}, f32[3,4,1024]{2,1,0:T(4,128)S(1)}) custom-call(bf16[1024,1024]{1,0:T(8,128)(2,1)} %q_hbm.1, bf16[1024,1024]{1,0:T(8,128)(2,1)} %k_hbm.1, bf16[1024,1024]{1,0:T(8,128)(2,1)} %v_hbm.1, ...), custom_call_target="tpu_custom_call" | custom-call | flops 268435456 | bytes 8388608 | tf_op jit(solution)/shard_map/block_states/pallas_call | solution.py:150
  5.0 4.0 %collective-permute-start = (bf16[2,160,128]{2,1,0:T(8,128)(2,1)S(1)}, bf16[2,160,128]{2,1,0:T(8,128)(2,1)S(1)}, u32[]{:S(2)}, u32[]{:S(2)}) collective-permute-start(bf16[2,160,128]{2,1,0:T(8,128)(2,1)S(1)} %get-tuple-element.79), channel_id=1, source_target_pairs={{0,3},{1,2},{2,1},{3,0},{4,7},{5,6},{6,5},{7,4},{8,11},{9,10},{10,... | collective-permute-start | bytes 245768 | tf_op jit(solution)/shard_map/ppermute | solution.py:449
  9.1 0.4 %collective-permute-start.1 = (bf16[2,160,128]{2,1,0:T(8,128)(2,1)S(1)}, bf16[2,160,128]{2,1,0:T(8,128)(2,1)S(1)}, u32[]{:S(2)}, u32[]{:S(2)}) collective-permute-start(bf16[2,160,128]{2,1,0:T(8,128)(2,1)S(1)} %get-tuple-element.78), channel_id=1, source_target_pairs={{0,2},{1,3},{2,0},{3,1},{4,6},{5,7},{6,4},{7,5},{8,10},{9,11},{10,... | collective-permute-start | bytes 245768 | tf_op jit(solution)/shard_map/ppermute | solution.py:449
  9.5 0.2 collective-permute-start.2
  9.7 2.0 %inner_attention.3 = (bf16[4,1024,128]{2,1,0:T(8,128)(2,1)S(1)}, f32[4,1024,128]{2,1,0:T(8,128)S(1)}) custom-call(bf16[1024,1024]{1,0:T(8,128)(2,1)S(1)} %get-tuple-element.42.q_ref, bf16[8,1024,128]{2,1,0:T(8,128)(2,1)S(1)} %get-tuple-element.43.kf_ref, bf16[8,1024,128]{2,1,0:T(8,128)(2,1)S(1)} %get-tuple-element.44.vf_ref, ...), custom_call_target="tpu_custom_call" | custom-call | flops 536870912 | bytes 6291456 | tf_op jit(solution)/shard_map/inner_attention/pallas_call | solution.py:375
  11.7 0.2 collective-permute-done.refs_3_.p3
  12.0 1.8 %collective-permute-done.1.refs_2_.p2 = bf16[2,160,128]{2,1,0:T(8,128)(2,1)S(1)} collective-permute-done((bf16[2,160,128]{2,1,0:T(8,128)(2,1)S(1)}, bf16[2,160,128]{2,1,0:T(8,128)(2,1)S(1)}, u32[]{:S(2)}, u32[]{:S(2)}) %collective-permute-start.1) | collective-permute-done | bytes 81952 | tf_op jit(solution)/shard_map/ppermute | solution.py:449
  13.7 0.3 collective-permute-done.2.refs_1_.p1
  14.0 0.2 group_total.1
  14.2 0.0 copy-start
  14.2 2.7 %collective-permute-start.3 = (bf16[2,144,128]{2,1,0:T(8,128)(2,1)S(1)}, bf16[2,144,128]{2,1,0:T(8,128)(2,1)S(1)}, u32[]{:S(2)}, u32[]{:S(2)}) collective-permute-start(bf16[2,144,128]{2,1,0:T(8,128)(2,1)S(1)} %group_total.1), channel_id=1, source_target_pairs={{0,4},{1,5},{2,6},{3,7},{4,0},{5,1},{6,2},{7,3},{8,12},{9,13},{10,... | collective-permute-start | bytes 221192 | tf_op jit(solution)/shard_map/ppermute | solution.py:449
  16.9 1.2 %inner_attention.4 = (bf16[2,1024,128]{2,1,0:T(8,128)(2,1)S(1)}, f32[2,1024,128]{2,1,0:T(8,128)S(1)}) custom-call(bf16[1024,1024]{1,0:T(8,128)(2,1)S(1)} %get-tuple-element.42.q_ref, bf16[8,1024,128]{2,1,0:T(8,128)(2,1)S(1)} %get-tuple-element.43.kf_ref, bf16[8,1024,128]{2,1,0:T(8,128)(2,1)S(1)} %get-tuple-element.44.vf_ref, ...), custom_call_target="tpu_custom_call" | custom-call | flops 268435456 | bytes 3145728 | tf_op jit(solution)/shard_map/inner_attention/pallas_call | solution.py:375
  18.1 0.6 %member_edges.1 = (bf16[3,2,16,128]{3,2,1,0:T(8,128)(2,1)S(1)}, f32[3,2,16,128]{3,2,1,0:T(8,128)S(1)}, f32[3,2,128,128]{3,2,1,0:T(8,128)S(1)}, f32[3,2,128,128]{3,2,1,0:T(8,128)S(1)}, bf16[2,32,128]{2,1,0:T(8,128)(2,1)S(1)}) custom-call(bf16[2,160,128]{2,1,0:T(8,128)(2,1)S(1)} %get-tuple-element.80.refs_0_.p0, ...), custom_call_target="tpu_custom_call" | custom-call | tf_op jit(solution)/shard_map/member_edges/pallas_call | solution.py:289
  18.7 0.9 %collective-permute-done.3.x_ref = bf16[2,144,128]{2,1,0:T(8,128)(2,1)S(1)} collective-permute-done((bf16[2,144,128]{2,1,0:T(8,128)(2,1)S(1)}, bf16[2,144,128]{2,1,0:T(8,128)(2,1)S(1)}, u32[]{:S(2)}, u32[]{:S(2)}) %collective-permute-start.3) | collective-permute-done | bytes 73760 | tf_op jit(solution)/shard_map/ppermute | solution.py:449
  19.5 0.0 copy-done
  19.5 0.6 %member_prefixes.1 = (bf16[2,144,128]{2,1,0:T(8,128)(2,1)S(1)}, bf16[2,144,128]{2,1,0:T(8,128)(2,1)S(1)}, bf16[2,144,128]{2,1,0:T(8,128)(2,1)S(1)}, bf16[2,144,128]{2,1,0:T(8,128)(2,1)S(1)}) custom-call(bf16[3,2,16,128]{3,2,1,0:T(8,128)(2,1)S(1)} %get-tuple-element.58.qf_ref, f32[3,2,16,128]{3,2,1,0:T(8,128)S(1)} %get-tuple-element.59.inner_ref, ...), custom_call_target="tpu_custom_call" | custom-call | tf_op jit(solution)/shard_map/member_prefixes/pallas_call | solution.py:335
  20.2 2.0 %collective-permute-start.6 = (bf16[2,144,128]{2,1,0:T(8,128)(2,1)S(1)}, bf16[2,144,128]{2,1,0:T(8,128)(2,1)S(1)}, u32[]{:S(2)}, u32[]{:S(2)}) collective-permute-start(bf16[2,144,128]{2,1,0:T(8,128)(2,1)S(1)} %get-tuple-element.67), channel_id=1, source_target_pairs={{0,3},{1,2},{2,1},{3,0},{4,7},{5,6},{6,5},{7,4},{8,11},{9,10},{10,... | collective-permute-start | bytes 221192 | tf_op jit(solution)/shard_map/ppermute | solution.py:449
  22.2 0.6 %collective-permute-start.4 = (bf16[2,144,128]{2,1,0:T(8,128)(2,1)S(1)}, bf16[2,144,128]{2,1,0:T(8,128)(2,1)S(1)}, u32[]{:S(2)}, u32[]{:S(2)}) collective-permute-start(bf16[2,144,128]{2,1,0:T(8,128)(2,1)S(1)} %get-tuple-element.64), channel_id=1, source_target_pairs={{0,2},{1,3},{2,0},{3,1},{4,6},{5,7},{6,4},{7,5},{8,10},{9,11},{10,... | collective-permute-start | bytes 221192 | tf_op jit(solution)/shard_map/ppermute | solution.py:449
  22.8 1.0 %collective-permute-start.5 = (bf16[2,144,128]{2,1,0:T(8,128)(2,1)S(1)}, bf16[2,144,128]{2,1,0:T(8,128)(2,1)S(1)}, u32[]{:S(2)}, u32[]{:S(2)}) collective-permute-start(bf16[2,144,128]{2,1,0:T(8,128)(2,1)S(1)} %get-tuple-element.65), channel_id=1, source_target_pairs={{0,1},{1,0},{2,3},{3,2},{4,5},{5,4},{6,7},{7,6},{8,9},{9,8},{10,11... | collective-permute-start | bytes 221192 | tf_op jit(solution)/shard_map/ppermute | solution.py:449
  23.7 1.2 %inner_attention.5 = (bf16[2,1024,128]{2,1,0:T(8,128)(2,1)S(1)}, f32[2,1024,128]{2,1,0:T(8,128)S(1)}) custom-call(bf16[1024,1024]{1,0:T(8,128)(2,1)S(1)} %get-tuple-element.42.q_ref, bf16[8,1024,128]{2,1,0:T(8,128)(2,1)S(1)} %get-tuple-element.43.kf_ref, bf16[8,1024,128]{2,1,0:T(8,128)(2,1)S(1)} %get-tuple-element.44.vf_ref, ...), custom_call_target="tpu_custom_call" | custom-call | flops 268435456 | bytes 3145728 | tf_op jit(solution)/shard_map/inner_attention/pallas_call | solution.py:375
  24.9 0.7 %collective-permute-done.6.refs_1_ = bf16[2,144,128]{2,1,0:T(8,128)(2,1)S(1)} collective-permute-done((bf16[2,144,128]{2,1,0:T(8,128)(2,1)S(1)}, bf16[2,144,128]{2,1,0:T(8,128)(2,1)S(1)}, u32[]{:S(2)}, u32[]{:S(2)}) %collective-permute-start.6) | collective-permute-done | bytes 73760 | tf_op jit(solution)/shard_map/ppermute | solution.py:449
  25.6 1.5 %finish.2.refs_6_ = bf16[1024,1024]{1,0:T(8,128)(2,1)} custom-call(f32[1,1024]{1,0:T(1,128)S(1)} %bitcast.2, bf16[2,144,128]{2,1,0:T(8,128)(2,1)S(1)} %get-tuple-element.73.refs_0_, bf16[2,144,128]{2,1,0:T(8,128)(2,1)S(1)} %collective-permute-done.6.refs_1_, bf16[4,1024,128]{2,1,0:T(8,128)(2,1)S(1)} %get-tuple-element.75.refs_2_.refs_3_, ...), custom_call_target="tpu_custom_call" | custom-call | flops 134217728 | bytes 4194304 | tf_op jit(solution)/shard_map/finish/pallas_call | solution.py:427
  27.1 0.0 collective-permute-done.4.refs_0_
  27.1 0.0 collective-permute-done.5.refs_1_
  27.1 1.5 %finish.3 = bf16[1024,1024]{1,0:T(8,128)(2,1)} custom-call(f32[1,1024]{1,0:T(1,128)S(1)} %bitcast.3, bf16[2,144,128]{2,1,0:T(8,128)(2,1)S(1)} %collective-permute-done.4.refs_0_, bf16[2,144,128]{2,1,0:T(8,128)(2,1)S(1)} %collective-permute-done.5.refs_1_, bf16[2,1024,128]{2,1,0:T(8,128)(2,1)S(1)} %get-tuple-element.66.refs_2_, ...), custom_call_target="tpu_custom_call", output_to_operand_aliasing={{}: (7, {})} | custom-call | flops 134217728 | bytes 4194304 | tf_op jit(solution)/shard_map/finish/pallas_call | solution.py:427
  (1 shorter events, 0.0 us)
Async XLA Ops:
  5.0 6.9 %collective-permute-start = (bf16[2,160,128]{2,1,0:T(8,128)(2,1)S(1)}, bf16[2,160,128]{2,1,0:T(8,128)(2,1)S(1)}, u32[]{:S(2)}, u32[]{:S(2)}) collective-permute-start(bf16[2,160,128]{2,1,0:T(8,128)(2,1)S(1)} %get-tuple-element.79), channel_id=1, source_target_pairs={{0,3},{1,2},{2,1},{3,0},{4,7},{5,6},{6,5},{7,4},{8,11},{9,10},{10,... | collective-permute-start | bytes 245768 | tf_op jit(solution)/shard_map/ppermute | solution.py:449
  9.1 4.6 %collective-permute-start.1 = (bf16[2,160,128]{2,1,0:T(8,128)(2,1)S(1)}, bf16[2,160,128]{2,1,0:T(8,128)(2,1)S(1)}, u32[]{:S(2)}, u32[]{:S(2)}) collective-permute-start(bf16[2,160,128]{2,1,0:T(8,128)(2,1)S(1)} %get-tuple-element.78), channel_id=1, source_target_pairs={{0,2},{1,3},{2,0},{3,1},{4,6},{5,7},{6,4},{7,5},{8,10},{9,11},{10,... | collective-permute-start | bytes 245768 | tf_op jit(solution)/shard_map/ppermute | solution.py:449
  9.5 4.4 %collective-permute-start.2 = (bf16[2,160,128]{2,1,0:T(8,128)(2,1)S(1)}, bf16[2,160,128]{2,1,0:T(8,128)(2,1)S(1)}, u32[]{:S(2)}, u32[]{:S(2)}) collective-permute-start(bf16[2,160,128]{2,1,0:T(8,128)(2,1)S(1)} %get-tuple-element.77), channel_id=1, source_target_pairs={{0,1},{1,0},{2,3},{3,2},{4,5},{5,4},{6,7},{7,6},{8,9},{9,8},{10,11... | collective-permute-start | bytes 245768 | tf_op jit(solution)/shard_map/ppermute | solution.py:449
  14.2 5.3 %copy-start = (f32[1024]{0:T(1024)S(1)}, f32[1024]{0:T(1024)}, u32[]{:S(2)}) copy-start(f32[1024]{0:T(1024)} %param.9) | copy-start | bytes 12292
  14.2 5.3 %collective-permute-start.3 = (bf16[2,144,128]{2,1,0:T(8,128)(2,1)S(1)}, bf16[2,144,128]{2,1,0:T(8,128)(2,1)S(1)}, u32[]{:S(2)}, u32[]{:S(2)}) collective-permute-start(bf16[2,144,128]{2,1,0:T(8,128)(2,1)S(1)} %group_total.1), channel_id=1, source_target_pairs={{0,4},{1,5},{2,6},{3,7},{4,0},{5,1},{6,2},{7,3},{8,12},{9,13},{10,... | collective-permute-start | bytes 221192 | tf_op jit(solution)/shard_map/ppermute | solution.py:449
  20.2 5.4 %collective-permute-start.6 = (bf16[2,144,128]{2,1,0:T(8,128)(2,1)S(1)}, bf16[2,144,128]{2,1,0:T(8,128)(2,1)S(1)}, u32[]{:S(2)}, u32[]{:S(2)}) collective-permute-start(bf16[2,144,128]{2,1,0:T(8,128)(2,1)S(1)} %get-tuple-element.67), channel_id=1, source_target_pairs={{0,3},{1,2},{2,1},{3,0},{4,7},{5,6},{6,5},{7,4},{8,11},{9,10},{10,... | collective-permute-start | bytes 221192 | tf_op jit(solution)/shard_map/ppermute | solution.py:449
  22.2 4.9 %collective-permute-start.4 = (bf16[2,144,128]{2,1,0:T(8,128)(2,1)S(1)}, bf16[2,144,128]{2,1,0:T(8,128)(2,1)S(1)}, u32[]{:S(2)}, u32[]{:S(2)}) collective-permute-start(bf16[2,144,128]{2,1,0:T(8,128)(2,1)S(1)} %get-tuple-element.64), channel_id=1, source_target_pairs={{0,2},{1,3},{2,0},{3,1},{4,6},{5,7},{6,4},{7,5},{8,10},{9,11},{10,... | collective-permute-start | bytes 221192 | tf_op jit(solution)/shard_map/ppermute | solution.py:449
  22.8 4.4 %collective-permute-start.5 = (bf16[2,144,128]{2,1,0:T(8,128)(2,1)S(1)}, bf16[2,144,128]{2,1,0:T(8,128)(2,1)S(1)}, u32[]{:S(2)}, u32[]{:S(2)}) collective-permute-start(bf16[2,144,128]{2,1,0:T(8,128)(2,1)S(1)} %get-tuple-element.65), channel_id=1, source_target_pairs={{0,1},{1,0},{2,3},{3,2},{4,5},{5,4},{6,7},{7,6},{8,9},{9,8},{10,11... | collective-permute-start | bytes 221192 | tf_op jit(solution)/shard_map/ppermute | solution.py:449

commit v8 on v7

--- a/solution.py
+++ b/solution.py
@@ -13,8 +13,6 @@
 ROWS = 64
 CHUNK = 256
 PARTS = 4
-AHEAD = 1
-PAIR = 4
 AUX = 32
 TAIL = 16
 FIX = 16
@@ -63,113 +61,167 @@
     return (taps[3:4] * at(0) + taps[2:3] * at(1)) + (taps[1:2] * at(2) + taps[0:1] * at(3))
 
 
-def state_kernel(q_hbm, k_hbm, v_hbm, w_hbm, kf_ref, vf_ref, msg_ref, q_ref, w_ref, k_buf, v_buf, wide, k_sem, v_sem, sem):
-    pairs, tokens = k_buf.shape[0:2]
-    heads = pairs * PAIR
-
-    def fetch(source, target, semaphore, i):
-        cols = pl.ds(pl.multiple_of(i * PAIR * HDIM, PAIR * HDIM), PAIR * HDIM)
-        return pltpu.make_async_copy(source.at[:, cols], target.at[i], semaphore.at[i])
-
-    def fetch_pair(i):
-        fetch(k_hbm, k_buf, k_sem, i).start()
-        fetch(v_hbm, v_buf, v_sem, i).start()
-
+def heads_of(quarter, per):
+    return [pl.ds(pl.multiple_of((quarter * per + u) * HDIM, HDIM), HDIM) for u in range(per)]
+
+
+def key_features(n, quarter, k_ref, w_ref, kf_ref, wide):
+    tokens, per = k_ref.shape[1], k_ref.shape[2] // HDIM
+    for u, cols in enumerate(heads_of(quarter, per)):
+        wk = w_ref[1, :, cols] * 0.5
+        for start in range(0, tokens, ROWS):
+            rows = slice(start, start + ROWS)
+            wide[n, u, 0, start + 8 : start + 8 + ROWS] = k_ref[n, rows, u * HDIM : (u + 1) * HDIM].astype(F32)
+            kf = silu_of_twice(conv_from(wide.at[n, u, 0], rows, wk))
+            if start == 0:
+                kf = jnp.where(rows_iota(kf.shape) < CONV - 1, 0.0, kf)
+            kf_ref[n * per + u, rows] = kf.astype(BF16)
+
+
+def states(n, quarter, k_ref, v_ref, w_ref, kf_ref, vf_ref, msg_ref, wide):
+    tokens, per = v_ref.shape[1], v_ref.shape[2] // HDIM
+    for u, cols in enumerate(heads_of(quarter, per)):
+        own = slice(u * HDIM, (u + 1) * HDIM)
+        wv = w_ref[2, :, cols]
+        local = jnp.zeros((HDIM, HDIM), F32)
+        for start in range(0, tokens, ROWS):
+            rows = slice(start, start + ROWS)
+            wide[n, u, 1, start + 8 : start + 8 + ROWS] = v_ref[n, rows, own].astype(F32)
+            vf = conv_from(wide.at[n, u, 1], rows, wv).astype(BF16)
+            vf_ref[n * per + u, rows] = vf
+            local = local + dot(kf_ref[n * per + u, rows], vf, ((0,), (0,)))
+        msg_ref[n * per + u, 0:HDIM] = local.astype(BF16)
+        mk = merged_rows(k_ref[n, 0:16, own], k_ref[n, tokens - 16 : tokens, own])
+        mv = merged_rows(v_ref[n, 0:16, own], v_ref[n, tokens - 16 : tokens, own])
+        msg_ref[n * per + u, HDIM : HDIM + 16] = jnp.concatenate([mk, mv], axis=0).astype(BF16)
+
+
+def query_rows(n, quarter, per, q_ref, msg_ref):
+    tokens = q_ref.shape[0]
+    for u, cols in enumerate(heads_of(quarter, per)):
+        mq = merged_rows(q_ref[0:16, cols], q_ref[tokens - 16 : tokens, cols])
+        msg_ref[n * per + u, HDIM + 16 : HDIM + 32] = jnp.concatenate([mq, mq], axis=0).astype(BF16)
+
+
+def clear_above(wide):
+    for n in range(wide.shape[0]):
+        for u in range(wide.shape[1]):
+            for a in range(2):
+                wide[n, u, a, 0:8] = jnp.zeros((8, HDIM), F32)
+
+
+def early_kernel(quarters, q_hbm, k_hbm, v_hbm, w_hbm, kf_ref, vf_ref, msg_ref, k_rest, v_rest, q_ref, w_ref, k_buf, v_buf, wide, k_sem, v_sem, sem):
+    count, tokens, part = k_buf.shape
+    per = part // HDIM
+    mine = [member() ^ j for j in quarters]
+
+    def fetch(source, target, rest, semaphore, n):
+        cols = pl.ds(pl.multiple_of(mine[n] * part, part), part)
+        place = target.at[n] if n < count else rest.at[0]
+        return pltpu.make_async_copy(source.at[:, cols], place, semaphore.at[n])
+
+    fetch_k = [fetch(k_hbm, k_buf, k_rest, k_sem, n) for n in range(GROUP)]
+    fetch_v = [fetch(v_hbm, v_buf, v_rest, v_sem, n) for n in range(GROUP)]
     fetch_taps = pltpu.make_async_copy(w_hbm, w_ref, sem.at[0])
     fetch_queries = pltpu.make_async_copy(q_hbm, q_ref, sem.at[1])
-    fetch_taps.start()
-    for i in range(AHEAD):
-        fetch_pair(i)
-    for u in range(PAIR):
-        for a in range(2):
-            wide[u, a, 0:8] = jnp.zeros((8, HDIM), F32)
+
+    def keys(n):
+        key_features(n, mine[n], k_buf, w_ref, kf_ref, wide)
+
+    def values(n):
+        states(n, mine[n], k_buf, v_buf, w_ref, kf_ref, vf_ref, msg_ref, wide)
+
+    for copy in (fetch_taps, fetch_k[0], fetch_v[0], fetch_k[1]):
+        copy.start()
+    clear_above(wide)
     fetch_taps.wait()
-
-    def some_heads(i, carry):
-        first = i * PAIR
-
-        @pl.when(i + AHEAD < pairs)
-        def _():
-            fetch_pair(i + AHEAD)
-
-        @pl.when(i + 2 == pairs)
-        def _():
-            fetch_queries.start()
-
-        fetch(k_hbm, k_buf, k_sem, i).wait()
-        for u in range(PAIR):
-            h = first + u
-            wk = w_ref[1, :, pl.ds(pl.multiple_of(h * HDIM, HDIM), HDIM)] * 0.5
-            for start in range(0, tokens, ROWS):
-                rows = slice(start, start + ROWS)
-                wide[u, 0, start + 8 : start + 8 + ROWS] = k_buf[i, rows, u * HDIM : (u + 1) * HDIM].astype(F32)
-                kf = silu_of_twice(conv_from(wide.at[u, 0], rows, wk))
-                if start == 0:
-                    kf = jnp.where(rows_iota(kf.shape) < CONV - 1, 0.0, kf)
-                kf_ref[h, rows] = kf.astype(BF16)
-        fetch(v_hbm, v_buf, v_sem, i).wait()
-        for u in range(PAIR):
-            h = first + u
-            cols = pl.ds(pl.multiple_of(h * HDIM, HDIM), HDIM)
-            wv = w_ref[2, :, cols]
-            local = jnp.zeros((HDIM, HDIM), F32)
-            for start in range(0, tokens, ROWS):
-                rows = slice(start, start + ROWS)
-                wide[u, 1, start + 8 : start + 8 + ROWS] = v_buf[i, rows, u * HDIM : (u + 1) * HDIM].astype(F32)
-                vf = conv_from(wide.at[u, 1], rows, wv).astype(BF16)
-                vf_ref[h, rows] = vf
-                local = local + dot(kf_ref[h, rows], vf, ((0,), (0,)))
-            per = heads // GROUP
-            place = (lax.div(h, per) ^ member()) * per + lax.rem(h, per)
-            msg_ref[place, 0:HDIM] = local.astype(BF16)
-            own = slice(u * HDIM, (u + 1) * HDIM)
-            mk = merged_rows(k_buf[i, 0:16, own], k_buf[i, tokens - 16 : tokens, own])
-            mv = merged_rows(v_buf[i, 0:16, own], v_buf[i, tokens - 16 : tokens, own])
-            msg_ref[place, HDIM : HDIM + 16] = jnp.concatenate([mk, mv], axis=0).astype(BF16)
-        return carry
-
-    lax.fori_loop(0, heads // PAIR, some_heads, 0)
+    fetch_k[0].wait()
+    for copy in (fetch_v[1], fetch_k[2], fetch_v[2]):
+        copy.start()
+    keys(0)
+    fetch_v[0].wait()
+    fetch_k[1].wait()
+    for copy in (fetch_k[3], fetch_v[3], fetch_queries):
+        copy.start()
+    values(0)
+    keys(1)
+    fetch_v[1].wait()
+    fetch_k[2].wait()
+    values(1)
+    keys(2)
+    fetch_v[2].wait()
+    values(2)
     fetch_queries.wait()
-    for h in range(heads):
-        cols = slice(h * HDIM, (h + 1) * HDIM)
-        per = heads // GROUP
-        place = (h // per ^ member()) * per + h % per
-        mq = merged_rows(q_ref[0:16, cols], q_ref[tokens - 16 : tokens, cols])
-        msg_ref[place, HDIM + 16 : HDIM + 32] = jnp.concatenate([mq, mq], axis=0).astype(BF16)
+    for n in range(count):
+        query_rows(n, mine[n], per, q_ref, msg_ref)
+    fetch_k[3].wait()
+    fetch_v[3].wait()
+
+
+def own_kernel(k_ref, v_ref, q_ref, w_ref, kf_ref, vf_ref, msg_ref, wide):
+    per = k_ref.shape[2] // HDIM
+    clear_above(wide)
+    key_features(0, member(), k_ref, w_ref, kf_ref, wide)
+    states(0, member(), k_ref, v_ref, w_ref, kf_ref, vf_ref, msg_ref, wide)
+    query_rows(0, member(), per, q_ref, msg_ref)
 
 
 VMEM = pl.BlockSpec(memory_space=pltpu.VMEM)
 HBM = pl.BlockSpec(memory_space=pltpu.HBM)
 
 
-def block_states(queries, key_rows, value_rows, conv_weight):
+def state_cost(tokens, width):
+    return pl.CostEstimate(flops=2 * tokens * width * HDIM, bytes_accessed=8 * tokens * width, transcendentals=tokens * width)
+
+
+def early_states(quarters, queries, key_rows, value_rows, conv_weight):
     tokens, width = key_rows.shape
-    heads = width // HDIM
-    features = jax.ShapeDtypeStruct((heads, tokens, HDIM), BF16)
+    count, part = len(quarters) - 1, width // GROUP
+    per = part // HDIM
+    features = jax.ShapeDtypeStruct((count * per, tokens, HDIM), BF16)
+    rest = jax.ShapeDtypeStruct((1, tokens, part), BF16)
     arrays = [pltpu.with_memory_space_constraint(a, pltpu.HBM) for a in (queries, key_rows, value_rows, conv_weight)]
     return pl.pallas_call(
-        state_kernel,
-        in_specs=[HBM, HBM, HBM, HBM],
-        out_specs=[VMEM] * 5,
+        functools.partial(early_kernel, quarters),
+        in_specs=[HBM] * 4,
+        out_specs=[VMEM] * 7,
         out_shape=[
             features,
             features,
-            jax.ShapeDtypeStruct((heads, HDIM + AUX, HDIM), BF16),
+            jax.ShapeDtypeStruct((count * per, HDIM + AUX, HDIM), BF16),
+            rest,
+            rest,
             jax.ShapeDtypeStruct(queries.shape, BF16),
             jax.ShapeDtypeStruct(conv_weight.shape, F32),
         ],
         scratch_shapes=[
-            pltpu.VMEM((heads // PAIR, tokens, PAIR * HDIM), BF16),
-            pltpu.VMEM((heads // PAIR, tokens, PAIR * HDIM), BF16),
-            pltpu.VMEM((PAIR, 2, tokens + 8, HDIM), F32),
-            pltpu.SemaphoreType.DMA((heads // PAIR,)),
-            pltpu.SemaphoreType.DMA((heads // PAIR,)),
+            pltpu.VMEM((count, tokens, part), BF16),
+            pltpu.VMEM((count, tokens, part), BF16),
+            pltpu.VMEM((count, per, 2, tokens + 8, HDIM), F32),
+            pltpu.SemaphoreType.DMA((GROUP,)),
+            pltpu.SemaphoreType.DMA((GROUP,)),
             pltpu.SemaphoreType.DMA((2,)),
         ],
-        compiler_params=pltpu.CompilerParams(vmem_limit_bytes=24 << 20),
-        cost_estimate=pl.CostEstimate(flops=2 * tokens * width * HDIM, bytes_accessed=8 * tokens * width, transcendentals=tokens * width),
-        name="block_states",
+        compiler_params=pltpu.CompilerParams(vmem_limit_bytes=28 << 20),
+        cost_estimate=state_cost(tokens, width),
+        name="early_states",
     )(*arrays)
+
+
+def own_states(k_rest, v_rest, queries, conv_weight):
+    tokens, part = k_rest.shape[1:3]
+    per = part // HDIM
+    features = jax.ShapeDtypeStruct((per, tokens, HDIM), BF16)
+    return pl.pallas_call(
+        own_kernel,
+        in_specs=[VMEM] * 4,
+        out_specs=[VMEM] * 3,
+        out_shape=[features, features, jax.ShapeDtypeStruct((per, HDIM + AUX, HDIM), BF16)],
+        scratch_shapes=[pltpu.VMEM((1, per, 2, tokens + 8, HDIM), F32)],
+        compiler_params=pltpu.CompilerParams(vmem_limit_bytes=16 << 20),
+        cost_estimate=state_cost(tokens, part),
+        name="own_states",
+    )(k_rest, v_rest, queries, conv_weight)
 
 
 def taps_of(w_ref, which, m, h, per):
@@ -343,9 +395,11 @@
     )(*edges, incoming, conv_weight, gain)
 
 
-def inner_kernel(quarters, q_ref, kf_ref, vf_ref, w_ref, qf_ref, inner_ref):
+def inner_kernel(quarters, slots, q_ref, w_ref, *refs):
+    n = len(quarters)
+    kf_refs, vf_refs, (qf_ref, inner_ref) = refs[0:n], refs[n : 2 * n], refs[2 * n :]
     heads, tokens = qf_ref.shape[0:2]
-    per = heads // len(quarters)
+    per = heads // n
     shape = (CHUNK, CHUNK)
     causal = rows_iota(shape) >= lax.broadcasted_iota(jnp.int32, shape, 1)
     for place in range(heads):
@@ -358,7 +412,8 @@
             above = q_ref[start - 16 : start, cols] if start else None
             qf = (silu_of_twice(conv_rows(q_ref[rows, cols], above, wq)) * SCALE).astype(BF16)
             qf_ref[place, rows] = qf
-            kf, vf = kf_ref[h, rows], vf_ref[h, rows]
+            kept = slots[place // per] * per + place % per
+            kf, vf = kf_refs[place // per][kept, rows], vf_refs[place // per][kept, rows]
             scores = jnp.where(causal, dot(qf, kf, ((1,), (1,))), 0.0).astype(BF16)
             inner = dot(scores, vf, ((1,), (0,)))
             if state is not None:
@@ -369,12 +424,13 @@
                 state = new if state is None else state + new
 
 
-def inner_attention(quarters, queries, kf, vf, conv_weight):
-    heads, tokens = kf.shape[0:2]
-    count = heads // GROUP * len(quarters)
-    return pl.pallas_call(
-        functools.partial(inner_kernel, quarters),
-        in_specs=[VMEM] * 4,
+def inner_attention(quarters, queries, kept, conv_weight):
+    tokens, width = queries.shape
+    count = width // HDIM // GROUP * len(quarters)
+    kfs, vfs, slots = zip(*(kept[j] for j in quarters))
+    return pl.pallas_call(
+        functools.partial(inner_kernel, quarters, slots),
+        in_specs=[VMEM] * (2 + 2 * len(quarters)),
         out_specs=[VMEM] * 2,
         out_shape=[
             jax.ShapeDtypeStruct((count, tokens, HDIM), BF16),
@@ -387,7 +443,7 @@
             transcendentals=tokens * count * HDIM,
         ),
         name="inner_attention",
-    )(queries, kf, vf, conv_weight)
+    )(queries, conv_weight, *kfs, *vfs)
 
 
 def finish_kernel(quarters, places, aliased, gain_ref, *refs):
@@ -459,15 +515,21 @@
     heads = width // GROUP // HDIM
     groups = lax.axis_size("ctx") // GROUP
     gain = head_gain.reshape(1, width)
-    kf, vf, messages, queries, conv_weight = block_states(queries, key_rows, value_rows, conv_weight)
+    order = (3, 2, 1)
+    kf, vf, early, k_rest, v_rest, queries, conv_weight = early_states(
+        order + (0,), queries, key_rows, value_rows, conv_weight
+    )
+    kept = {j: (kf, vf, n) for n, j in enumerate(order)}
+    sent = [swapped(early[n * heads : (n + 1) * heads], j) for n, j in enumerate(order)]
+    kf, vf, own = own_states(k_rest, v_rest, queries, conv_weight)
+    kept[0] = (kf, vf, 0)
 
     def beside(quarters, arrays):
-        piece = inner_attention(quarters, queries, kf, vf, conv_weight)
+        piece = inner_attention(quarters, queries, kept, conv_weight)
         return lax.optimization_barrier((arrays, piece))
 
-    packets = [swapped(messages[j * heads : (j + 1) * heads], j) for j in (3, 2, 1)]
-    packets, piece_a = beside((0, 3), packets)
-    packets = [messages[0:heads]] + packets[::-1]
+    sent, piece_a = beside((0, 3), sent)
+    packets = [own] + sent[::-1]
     if groups == 2:
         incoming = swapped(group_total(packets, None, conv_weight), GROUP)
     else:

time: 28.8 us -> 28 us (0.972)
  waiting for transfers between devices: 3.83 us -> 2.62 us
  Pallas kernels: 13.8 us -> 14.3 us
    ppermute x7, waiting for transfers between devices: 3.83 us -> 2.62 us  [swapped(): return lax.ppermute(value, 'ctx', [(s, s ^ bits) for s in range(count)])]
    pallas_call x4 -> x5, Pallas kernels: 9.32 us -> 9.66 us  [the longest x3 4.35 us: inner_attention(): pl.pallas_call(functools.partial(inner_kernel, quarters, slots), in_specs...]
  transfers between devices with their start and end apart: 7 -> 7, of which waited for: 5 -> 4; matrix products, arithmetic and copies ran while one was open for 0% -> 0% of each run, Pallas kernels for 22% -> 28%
where the time goes in v8:
time: 28 us; the launch traced here: 27.9 us
  Pallas kernels  14.3 us (51%)
  starting transfers between devices  10.9 us (39%)
  waiting for transfers between devices  2.62 us (9%)
    ppermute x7, starting transfers between devices, swapped(): return lax.ppermute(value, 'ctx', [(s, s ^ bits) for s in range(count)])  10.9 us
    pallas_call x3, Pallas kernels, inner_attention(): pl.pallas_call(functools.partial(inner_kernel, quarters, slots), in_specs...  4.35 us
    pallas_call x1, Pallas kernels, early_states(): pl.pallas_call(functools.partial(early_kernel, quarters), in_specs=[HBM]...  4.14 us
    pallas_call x2, Pallas kernels, finish(): pl.pallas_call(functools.partial(finish_kernel, quarters, places, len(oth...  3.14 us
    ppermute x7, waiting for transfers between devices, swapped(): return lax.ppermute(value, 'ctx', [(s, s ^ bits) for s in range(count)])  2.62 us
    pallas_call x1, Pallas kernels, own_states(): pl.pallas_call(own_kernel, in_specs=[VMEM] * 4, out_specs=[VMEM] * 3, out...  1.18 us
    pallas_call x1, Pallas kernels, member_prefixes(): pl.pallas_call(prefix_kernel, in_specs=[VMEM] * (len(edges) + 3), out_spe...  0.62 us
    pallas_call x1, Pallas kernels, member_edges(): pl.pallas_call(edges_kernel, in_specs=[VMEM] * (GROUP + 1), out_specs=[VM...  0.61 us
  transfers between devices with their start and end apart: 7, of which 4 were waited for; matrix products, arithmetic and copies ran while one was open for 0% of the time, Pallas kernels for 28%

profile of v8, /device:TPU:0, one launch (start us, length us, event | category | flops | bytes accessed | tf_op | source)
XLA Modules:
  0.0 27.9 jit_solution(5494332255774596235)
XLA Ops:
  0.0 4.1 %early_states.1 = (bf16[6,1024,128]{2,1,0:T(8,128)(2,1)S(1)}, bf16[6,1024,128]{2,1,0:T(8,128)(2,1)S(1)}, bf16[6,160,128]{2,1,0:T(8,128)(2,1)S(1)}, bf16[1,1024,2...) custom-call(bf16[1024,1024]{1,0:T(8,128)(2,1)} %q_hbm.1, ...), custom_call_target="tpu_custom_call" | custom-call | flops 268435456 | bytes 8388608 | tf_op jit(solution)/shard_map/early_states/pallas_call | solution.py:184
  4.2 4.0 %collective-permute-start = (bf16[2,160,128]{2,1,0:T(8,128)(2,1)S(1)}, bf16[2,160,128]{2,1,0:T(8,128)(2,1)S(1)}, u32[]{:S(2)}, u32[]{:S(2)}) collective-permute-start(bf16[2,160,128]{2,1,0:T(8,128)(2,1)S(1)} %get-tuple-element.89), channel_id=1, source_target_pairs={{0,3},{1,2},{2,1},{3,0},{4,7},{5,6},{6,5},{7,4},{8,11},{9,10},{10,... | collective-permute-start | bytes 245768 | tf_op jit(solution)/shard_map/ppermute | solution.py:505
  8.2 0.5 %collective-permute-start.1 = (bf16[2,160,128]{2,1,0:T(8,128)(2,1)S(1)}, bf16[2,160,128]{2,1,0:T(8,128)(2,1)S(1)}, u32[]{:S(2)}, u32[]{:S(2)}) collective-permute-start(bf16[2,160,128]{2,1,0:T(8,128)(2,1)S(1)} %get-tuple-element.88), channel_id=1, source_target_pairs={{0,2},{1,3},{2,0},{3,1},{4,6},{5,7},{6,4},{7,5},{8,10},{9,11},{10,... | collective-permute-start | bytes 245768 | tf_op jit(solution)/shard_map/ppermute | solution.py:505
  8.7 0.2 collective-permute-start.2
  8.8 1.2 %own_states.1 = (bf16[2,1024,128]{2,1,0:T(8,128)(2,1)S(1)}, bf16[2,1024,128]{2,1,0:T(8,128)(2,1)S(1)}, bf16[2,160,128]{2,1,0:T(8,128)(2,1)S(1)}) custom-call(bf16[1,1024,256]{2,1,0:T(8,128)(2,1)S(1)} %get-tuple-element.46.k_ref, bf16[1,1024,256]{2,1,0:T(8,128)(2,1)S(1)} %get-tuple-element.47.v_ref, bf16[1024,1024]{1,0:T(8,128)(2,1)S(1)} %get-tuple-element.48.q_ref, ...), custom_call_target="tpu_custom_call" | custom-call | flops 67108864 | bytes 2097152 | tf_op jit(solution)/shard_map/own_states/pallas_call | solution.py:215
  10.0 2.0 %inner_attention.3 = (bf16[4,1024,128]{2,1,0:T(8,128)(2,1)S(1)}, f32[4,1024,128]{2,1,0:T(8,128)S(1)}) custom-call(bf16[1024,1024]{1,0:T(8,128)(2,1)S(1)} %get-tuple-element.48.q_ref, f32[3,4,1024]{2,1,0:T(4,128)S(1)} %get-tuple-element.49.w_ref.refs_4_, bf16[2,1024,128]{2,1,0:T(8,128)(2,1)S(1)} %get-tuple-element.52.refs_0_, ...), custom_call_target="tpu_custom_call" | custom-call | flops 536870912 | bytes 6291456 | tf_op jit(solution)/shard_map/inner_attention/pallas_call | solution.py:431
  12.0 0.0 collective-permute-done.refs_3_.p3
  12.0 0.8 %collective-permute-done.1.refs_2_.p2 = bf16[2,160,128]{2,1,0:T(8,128)(2,1)S(1)} collective-permute-done((bf16[2,160,128]{2,1,0:T(8,128)(2,1)S(1)}, bf16[2,160,128]{2,1,0:T(8,128)(2,1)S(1)}, u32[]{:S(2)}, u32[]{:S(2)}) %collective-permute-start.1) | collective-permute-done | bytes 81952 | tf_op jit(solution)/shard_map/ppermute | solution.py:505
  12.8 0.3 collective-permute-done.2.refs_1_.p1
  13.1 0.2 group_total.1
  13.3 0.0 copy-start
  13.3 2.7 %collective-permute-start.3 = (bf16[2,144,128]{2,1,0:T(8,128)(2,1)S(1)}, bf16[2,144,128]{2,1,0:T(8,128)(2,1)S(1)}, u32[]{:S(2)}, u32[]{:S(2)}) collective-permute-start(bf16[2,144,128]{2,1,0:T(8,128)(2,1)S(1)} %group_total.1), channel_id=1, source_target_pairs={{0,4},{1,5},{2,6},{3,7},{4,0},{5,1},{6,2},{7,3},{8,12},{9,13},{10,... | collective-permute-start | bytes 221192 | tf_op jit(solution)/shard_map/ppermute | solution.py:505
  16.0 1.2 %inner_attention.4 = (bf16[2,1024,128]{2,1,0:T(8,128)(2,1)S(1)}, f32[2,1024,128]{2,1,0:T(8,128)S(1)}) custom-call(bf16[1024,1024]{1,0:T(8,128)(2,1)S(1)} %get-tuple-element.48.q_ref, f32[3,4,1024]{2,1,0:T(4,128)S(1)} %get-tuple-element.49.w_ref.refs_4_, bf16[6,1024,128]{2,1,0:T(8,128)(2,1)S(1)} %get-tuple-element.53.refs_1_.refs_0_, ...), custom_call_target="tpu_custom_call" | custom-call | flops 268435456 | bytes 3145728 | tf_op jit(solution)/shard_map/inner_attention/pallas_call | solution.py:431
  17.2 0.6 %member_edges.1 = (bf16[3,2,16,128]{3,2,1,0:T(8,128)(2,1)S(1)}, f32[3,2,16,128]{3,2,1,0:T(8,128)S(1)}, f32[3,2,128,128]{3,2,1,0:T(8,128)S(1)}, f32[3,2,128,128]{3,2,1,0:T(8,128)S(1)}, bf16[2,32,128]{2,1,0:T(8,128)(2,1)S(1)}) custom-call(bf16[2,160,128]{2,1,0:T(8,128)(2,1)S(1)} %get-tuple-element.50.refs_0_.p0, ...), custom_call_target="tpu_custom_call" | custom-call | tf_op jit(solution)/shard_map/member_edges/pallas_call | solution.py:341
  17.8 0.9 %collective-permute-done.3.x_ref = bf16[2,144,128]{2,1,0:T(8,128)(2,1)S(1)} collective-permute-done((bf16[2,144,128]{2,1,0:T(8,128)(2,1)S(1)}, bf16[2,144,128]{2,1,0:T(8,128)(2,1)S(1)}, u32[]{:S(2)}, u32[]{:S(2)}) %collective-permute-start.3) | collective-permute-done | bytes 73760 | tf_op jit(solution)/shard_map/ppermute | solution.py:505
  18.7 0.0 copy-done
  18.7 0.6 %member_prefixes.1 = (bf16[2,144,128]{2,1,0:T(8,128)(2,1)S(1)}, bf16[2,144,128]{2,1,0:T(8,128)(2,1)S(1)}, bf16[2,144,128]{2,1,0:T(8,128)(2,1)S(1)}, bf16[2,144,128]{2,1,0:T(8,128)(2,1)S(1)}) custom-call(bf16[3,2,16,128]{3,2,1,0:T(8,128)(2,1)S(1)} %get-tuple-element.68.qf_ref, f32[3,2,16,128]{3,2,1,0:T(8,128)S(1)} %get-tuple-element.69.inner_ref, ...), custom_call_target="tpu_custom_call" | custom-call | tf_op jit(solution)/shard_map/member_prefixes/pallas_call | solution.py:387
  19.3 2.0 %collective-permute-start.6 = (bf16[2,144,128]{2,1,0:T(8,128)(2,1)S(1)}, bf16[2,144,128]{2,1,0:T(8,128)(2,1)S(1)}, u32[]{:S(2)}, u32[]{:S(2)}) collective-permute-start(bf16[2,144,128]{2,1,0:T(8,128)(2,1)S(1)} %get-tuple-element.77), channel_id=1, source_target_pairs={{0,3},{1,2},{2,1},{3,0},{4,7},{5,6},{6,5},{7,4},{8,11},{9,10},{10,... | collective-permute-start | bytes 221192 | tf_op jit(solution)/shard_map/ppermute | solution.py:505
  21.3 0.6 %collective-permute-start.4 = (bf16[2,144,128]{2,1,0:T(8,128)(2,1)S(1)}, bf16[2,144,128]{2,1,0:T(8,128)(2,1)S(1)}, u32[]{:S(2)}, u32[]{:S(2)}) collective-permute-start(bf16[2,144,128]{2,1,0:T(8,128)(2,1)S(1)} %get-tuple-element.74), channel_id=1, source_target_pairs={{0,2},{1,3},{2,0},{3,1},{4,6},{5,7},{6,4},{7,5},{8,10},{9,11},{10,... | collective-permute-start | bytes 221192 | tf_op jit(solution)/shard_map/ppermute | solution.py:505
  21.9 1.0 %collective-permute-start.5 = (bf16[2,144,128]{2,1,0:T(8,128)(2,1)S(1)}, bf16[2,144,128]{2,1,0:T(8,128)(2,1)S(1)}, u32[]{:S(2)}, u32[]{:S(2)}) collective-permute-start(bf16[2,144,128]{2,1,0:T(8,128)(2,1)S(1)} %get-tuple-element.75), channel_id=1, source_target_pairs={{0,1},{1,0},{2,3},{3,2},{4,5},{5,4},{6,7},{7,6},{8,9},{9,8},{10,11... | collective-permute-start | bytes 221192 | tf_op jit(solution)/shard_map/ppermute | solution.py:505
  22.8 1.2 %inner_attention.5 = (bf16[2,1024,128]{2,1,0:T(8,128)(2,1)S(1)}, f32[2,1024,128]{2,1,0:T(8,128)S(1)}) custom-call(bf16[1024,1024]{1,0:T(8,128)(2,1)S(1)} %get-tuple-element.48.q_ref, f32[3,4,1024]{2,1,0:T(4,128)S(1)} %get-tuple-element.49.w_ref.refs_4_, bf16[6,1024,128]{2,1,0:T(8,128)(2,1)S(1)} %get-tuple-element.53.refs_1_.refs_0_, ...), custom_call_target="tpu_custom_call" | custom-call | flops 268435456 | bytes 3145728 | tf_op jit(solution)/shard_map/inner_attention/pallas_call | solution.py:431
  24.0 0.7 %collective-permute-done.6.refs_1_ = bf16[2,144,128]{2,1,0:T(8,128)(2,1)S(1)} collective-permute-done((bf16[2,144,128]{2,1,0:T(8,128)(2,1)S(1)}, bf16[2,144,128]{2,1,0:T(8,128)(2,1)S(1)}, u32[]{:S(2)}, u32[]{:S(2)}) %collective-permute-start.6) | collective-permute-done | bytes 73760 | tf_op jit(solution)/shard_map/ppermute | solution.py:505
  24.7 1.6 %finish.2.refs_6_ = bf16[1024,1024]{1,0:T(8,128)(2,1)} custom-call(f32[1,1024]{1,0:T(1,128)S(1)} %bitcast.2, bf16[2,144,128]{2,1,0:T(8,128)(2,1)S(1)} %get-tuple-element.83.refs_0_, bf16[2,144,128]{2,1,0:T(8,128)(2,1)S(1)} %collective-permute-done.6.refs_1_, bf16[4,1024,128]{2,1,0:T(8,128)(2,1)S(1)} %get-tuple-element.85.refs_2_.refs_3_, ...), custom_call_target="tpu_custom_call" | custom-call | flops 134217728 | bytes 4194304 | tf_op jit(solution)/shard_map/finish/pallas_call | solution.py:483
  26.3 0.0 collective-permute-done.4.refs_0_
  26.3 0.0 collective-permute-done.5.refs_1_
  26.3 1.6 %finish.3 = bf16[1024,1024]{1,0:T(8,128)(2,1)} custom-call(f32[1,1024]{1,0:T(1,128)S(1)} %bitcast.3, bf16[2,144,128]{2,1,0:T(8,128)(2,1)S(1)} %collective-permute-done.4.refs_0_, bf16[2,144,128]{2,1,0:T(8,128)(2,1)S(1)} %collective-permute-done.5.refs_1_, bf16[2,1024,128]{2,1,0:T(8,128)(2,1)S(1)} %get-tuple-element.76.refs_2_, ...), custom_call_target="tpu_custom_call", output_to_operand_aliasing={{}: (7, {})} | custom-call | flops 134217728 | bytes 4194304 | tf_op jit(solution)/shard_map/finish/pallas_call | solution.py:483
  (1 shorter events, 0.0 us)
Async XLA Ops:
  4.2 7.9 %collective-permute-start = (bf16[2,160,128]{2,1,0:T(8,128)(2,1)S(1)}, bf16[2,160,128]{2,1,0:T(8,128)(2,1)S(1)}, u32[]{:S(2)}, u32[]{:S(2)}) collective-permute-start(bf16[2,160,128]{2,1,0:T(8,128)(2,1)S(1)} %get-tuple-element.89), channel_id=1, source_target_pairs={{0,3},{1,2},{2,1},{3,0},{4,7},{5,6},{6,5},{7,4},{8,11},{9,10},{10,... | collective-permute-start | bytes 245768 | tf_op jit(solution)/shard_map/ppermute | solution.py:505
  8.2 4.6 %collective-permute-start.1 = (bf16[2,160,128]{2,1,0:T(8,128)(2,1)S(1)}, bf16[2,160,128]{2,1,0:T(8,128)(2,1)S(1)}, u32[]{:S(2)}, u32[]{:S(2)}) collective-permute-start(bf16[2,160,128]{2,1,0:T(8,128)(2,1)S(1)} %get-tuple-element.88), channel_id=1, source_target_pairs={{0,2},{1,3},{2,0},{3,1},{4,6},{5,7},{6,4},{7,5},{8,10},{9,11},{10,... | collective-permute-start | bytes 245768 | tf_op jit(solution)/shard_map/ppermute | solution.py:505
  8.7 4.4 %collective-permute-start.2 = (bf16[2,160,128]{2,1,0:T(8,128)(2,1)S(1)}, bf16[2,160,128]{2,1,0:T(8,128)(2,1)S(1)}, u32[]{:S(2)}, u32[]{:S(2)}) collective-permute-start(bf16[2,160,128]{2,1,0:T(8,128)(2,1)S(1)} %get-tuple-element.87), channel_id=1, source_target_pairs={{0,1},{1,0},{2,3},{3,2},{4,5},{5,4},{6,7},{7,6},{8,9},{9,8},{10,11... | collective-permute-start | bytes 245768 | tf_op jit(solution)/shard_map/ppermute | solution.py:505
  13.3 5.3 %copy-start = (f32[1024]{0:T(1024)S(1)}, f32[1024]{0:T(1024)}, u32[]{:S(2)}) copy-start(f32[1024]{0:T(1024)} %param.9) | copy-start | bytes 12292
  13.3 5.3 %collective-permute-start.3 = (bf16[2,144,128]{2,1,0:T(8,128)(2,1)S(1)}, bf16[2,144,128]{2,1,0:T(8,128)(2,1)S(1)}, u32[]{:S(2)}, u32[]{:S(2)}) collective-permute-start(bf16[2,144,128]{2,1,0:T(8,128)(2,1)S(1)} %group_total.1), channel_id=1, source_target_pairs={{0,4},{1,5},{2,6},{3,7},{4,0},{5,1},{6,2},{7,3},{8,12},{9,13},{10,... | collective-permute-start | bytes 221192 | tf_op jit(solution)/shard_map/ppermute | solution.py:505
  19.3 5.4 %collective-permute-start.6 = (bf16[2,144,128]{2,1,0:T(8,128)(2,1)S(1)}, bf16[2,144,128]{2,1,0:T(8,128)(2,1)S(1)}, u32[]{:S(2)}, u32[]{:S(2)}) collective-permute-start(bf16[2,144,128]{2,1,0:T(8,128)(2,1)S(1)} %get-tuple-element.77), channel_id=1, source_target_pairs={{0,3},{1,2},{2,1},{3,0},{4,7},{5,6},{6,5},{7,4},{8,11},{9,10},{10,... | collective-permute-start | bytes 221192 | tf_op jit(solution)/shard_map/ppermute | solution.py:505
  21.3 5.0 %collective-permute-start.4 = (bf16[2,144,128]{2,1,0:T(8,128)(2,1)S(1)}, bf16[2,144,128]{2,1,0:T(8,128)(2,1)S(1)}, u32[]{:S(2)}, u32[]{:S(2)}) collective-permute-start(bf16[2,144,128]{2,1,0:T(8,128)(2,1)S(1)} %get-tuple-element.74), channel_id=1, source_target_pairs={{0,2},{1,3},{2,0},{3,1},{4,6},{5,7},{6,4},{7,5},{8,10},{9,11},{10,... | collective-permute-start | bytes 221192 | tf_op jit(solution)/shard_map/ppermute | solution.py:505
  21.9 4.5 %collective-permute-start.5 = (bf16[2,144,128]{2,1,0:T(8,128)(2,1)S(1)}, bf16[2,144,128]{2,1,0:T(8,128)(2,1)S(1)}, u32[]{:S(2)}, u32[]{:S(2)}) collective-permute-start(bf16[2,144,128]{2,1,0:T(8,128)(2,1)S(1)} %get-tuple-element.75), channel_id=1, source_target_pairs={{0,1},{1,0},{2,3},{3,2},{4,5},{5,4},{6,7},{7,6},{8,9},{9,8},{10,11... | collective-permute-start | bytes 221192 | tf_op jit(solution)/shard_map/ppermute | solution.py:505

commit v9 on v8

--- a/solution.py
+++ b/solution.py
@@ -528,8 +528,8 @@
         piece = inner_attention(quarters, queries, kept, conv_weight)
         return lax.optimization_barrier((arrays, piece))
 
-    sent, piece_a = beside((0, 3), sent)
-    packets = [own] + sent[::-1]
+    sent, piece_a = beside((0, 3), sent[::-1])
+    packets = [own] + sent
     if groups == 2:
         incoming = swapped(group_total(packets, None, conv_weight), GROUP)
     else:
@@ -543,13 +543,13 @@
             passed = prefix + total
         incoming = jnp.concatenate([prefix.astype(BF16), tail], axis=1)
     edges = member_edges(packets, conv_weight)
-    (incoming, edges), piece_b = beside((2,), (incoming, edges))
+    (incoming, edges), piece_b = beside((2, 1), (incoming, edges))
     sends = member_prefixes(edges, incoming, conv_weight, gain)
-    first = [swapped(sends[j], j) for j in (3,)]
-    last = [swapped(sends[j], j) for j in (2, 1)]
-    first, piece_c = beside((1,), first)
-    out = finish((0, 3), [sends[0]] + first, [piece_a, piece_a], (0, 1, ), gain)
-    return finish((2, 1), last, [piece_b, piece_c], (0, 0, ), gain, out)
+    out = finish((0,), [sends[0]], [piece_a], (0,), gain)
+    far, near = swapped(sends[3], 3), [swapped(sends[j], j) for j in (2, 1)]
+    far, out = lax.optimization_barrier((far, out))
+    out = finish((3,), [far], [piece_a], (1,), gain, out)
+    return finish((2, 1), near, [piece_b, piece_b], (0, 1), gain, out)
 
 
 def solution(mesh):

time: 28 us -> 27.9 us (level)
  waiting for transfers between devices: 2.62 us -> 2.07 us
  Pallas kernels: 14.3 us -> 14.7 us
    pallas_call x2 -> x3, Pallas kernels: 3.14 us -> 3.93 us  [finish(): pl.pallas_call(functools.partial(finish_kernel, quarters, places, len(oth...]
    ppermute x7, waiting for transfers between devices: 2.62 us -> 2.07 us  [swapped(): return lax.ppermute(value, 'ctx', [(s, s ^ bits) for s in range(count)])]
    pallas_call x3 -> x2, Pallas kernels: 4.35 us -> 3.97 us  [inner_attention(): pl.pallas_call(functools.partial(inner_kernel, quarters, slots), in_specs...]
  transfers between devices with their start and end apart: 7 -> 7, of which waited for: 4 -> 5; matrix products, arithmetic and copies ran while one was open for 0% -> 0% of each run, Pallas kernels for 28% -> 29%
where the time goes in v9:
time: 27.9 us; the launch traced here: 27.7 us
  Pallas kernels  14.7 us (53%)
  starting transfers between devices  10.9 us (39%)
  waiting for transfers between devices  2.07 us (7%)
    ppermute x7, starting transfers between devices, swapped(): return lax.ppermute(value, 'ctx', [(s, s ^ bits) for s in range(count)])  10.9 us
    pallas_call x1, Pallas kernels, early_states(): pl.pallas_call(functools.partial(early_kernel, quarters), in_specs=[HBM]...  4.14 us
    pallas_call x2, Pallas kernels, inner_attention(): pl.pallas_call(functools.partial(inner_kernel, quarters, slots), in_specs...  3.97 us
    pallas_call x3, Pallas kernels, finish(): pl.pallas_call(functools.partial(finish_kernel, quarters, places, len(oth...  3.93 us
    ppermute x7, waiting for transfers between devices, swapped(): return lax.ppermute(value, 'ctx', [(s, s ^ bits) for s in range(count)])  2.07 us
    pallas_call x1, Pallas kernels, own_states(): pl.pallas_call(own_kernel, in_specs=[VMEM] * 4, out_specs=[VMEM] * 3, out...  1.18 us
    pallas_call x1, Pallas kernels, member_prefixes(): pl.pallas_call(prefix_kernel, in_specs=[VMEM] * (len(edges) + 3), out_spe...  0.62 us
    pallas_call x1, Pallas kernels, member_edges(): pl.pallas_call(edges_kernel, in_specs=[VMEM] * (GROUP + 1), out_specs=[VM...  0.61 us
  transfers between devices with their start and end apart: 7, of which 5 were waited for; matrix products, arithmetic and copies ran while one was open for 0% of the time, Pallas kernels for 29%

profile of v9, /device:TPU:0, one launch (start us, length us, event | category | flops | bytes accessed | tf_op | source)
XLA Modules:
  0.0 27.7 jit_solution(12615475896582508866)
XLA Ops:
  0.0 4.1 %early_states.1 = (bf16[6,1024,128]{2,1,0:T(8,128)(2,1)S(1)}, bf16[6,1024,128]{2,1,0:T(8,128)(2,1)S(1)}, bf16[6,160,128]{2,1,0:T(8,128)(2,1)S(1)}, bf16[1,1024,2...) custom-call(bf16[1024,1024]{1,0:T(8,128)(2,1)} %q_hbm.1, ...), custom_call_target="tpu_custom_call" | custom-call | flops 268435456 | bytes 8388608 | tf_op jit(solution)/shard_map/early_states/pallas_call | solution.py:184
  4.2 4.0 %collective-permute-start.2 = (bf16[2,160,128]{2,1,0:T(8,128)(2,1)S(1)}, bf16[2,160,128]{2,1,0:T(8,128)(2,1)S(1)}, u32[]{:S(2)}, u32[]{:S(2)}) collective-permute-start(bf16[2,160,128]{2,1,0:T(8,128)(2,1)S(1)} %get-tuple-element.81), channel_id=1, source_target_pairs={{0,3},{1,2},{2,1},{3,0},{4,7},{5,6},{6,5},{7,4},{8,11},{9,10},{10,... | collective-permute-start | bytes 245768 | tf_op jit(solution)/shard_map/ppermute | solution.py:505
  8.2 0.5 %collective-permute-start.1 = (bf16[2,160,128]{2,1,0:T(8,128)(2,1)S(1)}, bf16[2,160,128]{2,1,0:T(8,128)(2,1)S(1)}, u32[]{:S(2)}, u32[]{:S(2)}) collective-permute-start(bf16[2,160,128]{2,1,0:T(8,128)(2,1)S(1)} %get-tuple-element.82), channel_id=1, source_target_pairs={{0,2},{1,3},{2,0},{3,1},{4,6},{5,7},{6,4},{7,5},{8,10},{9,11},{10,... | collective-permute-start | bytes 245768 | tf_op jit(solution)/shard_map/ppermute | solution.py:505
  8.7 0.2 collective-permute-start
  8.8 1.2 %own_states.1 = (bf16[2,1024,128]{2,1,0:T(8,128)(2,1)S(1)}, bf16[2,1024,128]{2,1,0:T(8,128)(2,1)S(1)}, bf16[2,160,128]{2,1,0:T(8,128)(2,1)S(1)}) custom-call(bf16[1,1024,256]{2,1,0:T(8,128)(2,1)S(1)} %get-tuple-element.43.k_ref, bf16[1,1024,256]{2,1,0:T(8,128)(2,1)S(1)} %get-tuple-element.44.v_ref, bf16[1024,1024]{1,0:T(8,128)(2,1)S(1)} %get-tuple-element.45.q_ref, ...), custom_call_target="tpu_custom_call" | custom-call | flops 67108864 | bytes 2097152 | tf_op jit(solution)/shard_map/own_states/pallas_call | solution.py:215
  10.0 2.0 %inner_attention.2 = (bf16[4,1024,128]{2,1,0:T(8,128)(2,1)S(1)}, f32[4,1024,128]{2,1,0:T(8,128)S(1)}) custom-call(bf16[1024,1024]{1,0:T(8,128)(2,1)S(1)} %get-tuple-element.45.q_ref, f32[3,4,1024]{2,1,0:T(4,128)S(1)} %get-tuple-element.46.w_ref.refs_4_, bf16[2,1024,128]{2,1,0:T(8,128)(2,1)S(1)} %get-tuple-element.49.refs_0_, ...), custom_call_target="tpu_custom_call" | custom-call | flops 536870912 | bytes 6291456 | tf_op jit(solution)/shard_map/inner_attention/pallas_call | solution.py:431
  12.0 0.0 collective-permute-done.2.refs_3_.p3
  12.0 0.8 %collective-permute-done.1.refs_2_.p2 = bf16[2,160,128]{2,1,0:T(8,128)(2,1)S(1)} collective-permute-done((bf16[2,160,128]{2,1,0:T(8,128)(2,1)S(1)}, bf16[2,160,128]{2,1,0:T(8,128)(2,1)S(1)}, u32[]{:S(2)}, u32[]{:S(2)}) %collective-permute-start.1) | collective-permute-done | bytes 81952 | tf_op jit(solution)/shard_map/ppermute | solution.py:505
  12.8 0.3 collective-permute-done.refs_1_.p1
  13.1 0.2 group_total.1
  13.3 0.0 copy-start
  13.3 2.7 %collective-permute-start.3 = (bf16[2,144,128]{2,1,0:T(8,128)(2,1)S(1)}, bf16[2,144,128]{2,1,0:T(8,128)(2,1)S(1)}, u32[]{:S(2)}, u32[]{:S(2)}) collective-permute-start(bf16[2,144,128]{2,1,0:T(8,128)(2,1)S(1)} %group_total.1), channel_id=1, source_target_pairs={{0,4},{1,5},{2,6},{3,7},{4,0},{5,1},{6,2},{7,3},{8,12},{9,13},{10,... | collective-permute-start | bytes 221192 | tf_op jit(solution)/shard_map/ppermute | solution.py:505
  16.0 2.0 %inner_attention.3 = (bf16[4,1024,128]{2,1,0:T(8,128)(2,1)S(1)}, f32[4,1024,128]{2,1,0:T(8,128)S(1)}) custom-call(bf16[1024,1024]{1,0:T(8,128)(2,1)S(1)} %get-tuple-element.45.q_ref, f32[3,4,1024]{2,1,0:T(4,128)S(1)} %get-tuple-element.46.w_ref.refs_4_, bf16[6,1024,128]{2,1,0:T(8,128)(2,1)S(1)} %get-tuple-element.50.refs_1_.refs_0_, ...), custom_call_target="tpu_custom_call" | custom-call | flops 536870912 | bytes 6291456 | tf_op jit(solution)/shard_map/inner_attention/pallas_call | solution.py:431
  18.0 0.6 %member_edges.1 = (bf16[3,2,16,128]{3,2,1,0:T(8,128)(2,1)S(1)}, f32[3,2,16,128]{3,2,1,0:T(8,128)S(1)}, f32[3,2,128,128]{3,2,1,0:T(8,128)S(1)}, f32[3,2,128,128]{3,2,1,0:T(8,128)S(1)}, bf16[2,32,128]{2,1,0:T(8,128)(2,1)S(1)}) custom-call(bf16[2,160,128]{2,1,0:T(8,128)(2,1)S(1)} %get-tuple-element.47.refs_0_.p0, ...), custom_call_target="tpu_custom_call" | custom-call | tf_op jit(solution)/shard_map/member_edges/pallas_call | solution.py:341
  18.6 0.1 collective-permute-done.3.x_ref
  18.7 0.0 copy-done
  18.7 0.6 %member_prefixes.1 = (bf16[2,144,128]{2,1,0:T(8,128)(2,1)S(1)}, bf16[2,144,128]{2,1,0:T(8,128)(2,1)S(1)}, bf16[2,144,128]{2,1,0:T(8,128)(2,1)S(1)}, bf16[2,144,128]{2,1,0:T(8,128)(2,1)S(1)}) custom-call(bf16[3,2,16,128]{3,2,1,0:T(8,128)(2,1)S(1)} %get-tuple-element.65.qf_ref, f32[3,2,16,128]{3,2,1,0:T(8,128)S(1)} %get-tuple-element.66.inner_ref, ...), custom_call_target="tpu_custom_call" | custom-call | tf_op jit(solution)/shard_map/member_prefixes/pallas_call | solution.py:387
  19.3 2.0 %collective-permute-start.6 = (bf16[2,144,128]{2,1,0:T(8,128)(2,1)S(1)}, bf16[2,144,128]{2,1,0:T(8,128)(2,1)S(1)}, u32[]{:S(2)}, u32[]{:S(2)}) collective-permute-start(bf16[2,144,128]{2,1,0:T(8,128)(2,1)S(1)} %get-tuple-element.75), channel_id=1, source_target_pairs={{0,3},{1,2},{2,1},{3,0},{4,7},{5,6},{6,5},{7,4},{8,11},{9,10},{10,... | collective-permute-start | bytes 221192 | tf_op jit(solution)/shard_map/ppermute | solution.py:505
  21.3 0.6 %collective-permute-start.4 = (bf16[2,144,128]{2,1,0:T(8,128)(2,1)S(1)}, bf16[2,144,128]{2,1,0:T(8,128)(2,1)S(1)}, u32[]{:S(2)}, u32[]{:S(2)}) collective-permute-start(bf16[2,144,128]{2,1,0:T(8,128)(2,1)S(1)} %get-tuple-element.71), channel_id=1, source_target_pairs={{0,2},{1,3},{2,0},{3,1},{4,6},{5,7},{6,4},{7,5},{8,10},{9,11},{10,... | collective-permute-start | bytes 221192 | tf_op jit(solution)/shard_map/ppermute | solution.py:505
  21.9 1.0 %collective-permute-start.5 = (bf16[2,144,128]{2,1,0:T(8,128)(2,1)S(1)}, bf16[2,144,128]{2,1,0:T(8,128)(2,1)S(1)}, u32[]{:S(2)}, u32[]{:S(2)}) collective-permute-start(bf16[2,144,128]{2,1,0:T(8,128)(2,1)S(1)} %get-tuple-element.72), channel_id=1, source_target_pairs={{0,1},{1,0},{2,3},{3,2},{4,5},{5,4},{6,7},{7,6},{8,9},{9,8},{10,11... | collective-permute-start | bytes 221192 | tf_op jit(solution)/shard_map/ppermute | solution.py:505
  22.8 1.2 %finish.3.refs_3_ = bf16[1024,1024]{1,0:T(8,128)(2,1)} custom-call(f32[1,1024]{1,0:T(1,128)S(1)} %bitcast.2, bf16[2,144,128]{2,1,0:T(8,128)(2,1)S(1)} %get-tuple-element.76.refs_0_, bf16[4,1024,128]{2,1,0:T(8,128)(2,1)S(1)} %get-tuple-element.77.refs_1_, f32[4,1024,128]{2,1,0:T(8,128)S(1)} %get-tuple-element.78.refs_2_), custom_call_target="tpu_custom_call" | custom-call | flops 67108864 | bytes 2097152 | tf_op jit(solution)/shard_map/finish/pallas_call | solution.py:483
  24.1 0.7 %collective-permute-done.6.refs_0_ = bf16[2,144,128]{2,1,0:T(8,128)(2,1)S(1)} collective-permute-done((bf16[2,144,128]{2,1,0:T(8,128)(2,1)S(1)}, bf16[2,144,128]{2,1,0:T(8,128)(2,1)S(1)}, u32[]{:S(2)}, u32[]{:S(2)}) %collective-permute-start.6) | collective-permute-done | bytes 73760 | tf_op jit(solution)/shard_map/ppermute | solution.py:505
  24.7 1.2 %finish.4.refs_6_ = bf16[1024,1024]{1,0:T(8,128)(2,1)} custom-call(f32[1,1024]{1,0:T(1,128)S(1)} %bitcast.3, bf16[2,144,128]{2,1,0:T(8,128)(2,1)S(1)} %collective-permute-done.6.refs_0_, bf16[4,1024,128]{2,1,0:T(8,128)(2,1)S(1)} %get-tuple-element.77.refs_1_, f32[4,1024,128]{2,1,0:T(8,128)S(1)} %get-tuple-element.78.refs_2_, ...), custom_call_target="tpu_custom_call", output_to_operand_aliasing={{}: (4, {})} | custom-call | flops 67108864 | bytes 2097152 | tf_op jit(solution)/shard_map/finish/pallas_call | solution.py:483
  25.9 0.0 collective-permute-done.4.refs_0_
  25.9 0.3 collective-permute-done.5.refs_1_
  26.2 1.5 %finish.5 = bf16[1024,1024]{1,0:T(8,128)(2,1)} custom-call(f32[1,1024]{1,0:T(1,128)S(1)} %bitcast.4, bf16[2,144,128]{2,1,0:T(8,128)(2,1)S(1)} %collective-permute-done.4.refs_0_, bf16[2,144,128]{2,1,0:T(8,128)(2,1)S(1)} %collective-permute-done.5.refs_1_, ...), custom_call_target="tpu_custom_call", output_to_operand_aliasing={{}: (7, {})} | custom-call | flops 134217728 | bytes 4194304 | tf_op jit(solution)/shard_map/finish/pallas_call | solution.py:483
  (1 shorter events, 0.0 us)
Async XLA Ops:
  4.2 7.9 %collective-permute-start.2 = (bf16[2,160,128]{2,1,0:T(8,128)(2,1)S(1)}, bf16[2,160,128]{2,1,0:T(8,128)(2,1)S(1)}, u32[]{:S(2)}, u32[]{:S(2)}) collective-permute-start(bf16[2,160,128]{2,1,0:T(8,128)(2,1)S(1)} %get-tuple-element.81), channel_id=1, source_target_pairs={{0,3},{1,2},{2,1},{3,0},{4,7},{5,6},{6,5},{7,4},{8,11},{9,10},{10,... | collective-permute-start | bytes 245768 | tf_op jit(solution)/shard_map/ppermute | solution.py:505
  8.2 4.6 %collective-permute-start.1 = (bf16[2,160,128]{2,1,0:T(8,128)(2,1)S(1)}, bf16[2,160,128]{2,1,0:T(8,128)(2,1)S(1)}, u32[]{:S(2)}, u32[]{:S(2)}) collective-permute-start(bf16[2,160,128]{2,1,0:T(8,128)(2,1)S(1)} %get-tuple-element.82), channel_id=1, source_target_pairs={{0,2},{1,3},{2,0},{3,1},{4,6},{5,7},{6,4},{7,5},{8,10},{9,11},{10,... | collective-permute-start | bytes 245768 | tf_op jit(solution)/shard_map/ppermute | solution.py:505
  8.7 4.4 %collective-permute-start = (bf16[2,160,128]{2,1,0:T(8,128)(2,1)S(1)}, bf16[2,160,128]{2,1,0:T(8,128)(2,1)S(1)}, u32[]{:S(2)}, u32[]{:S(2)}) collective-permute-start(bf16[2,160,128]{2,1,0:T(8,128)(2,1)S(1)} %get-tuple-element.83), channel_id=1, source_target_pairs={{0,1},{1,0},{2,3},{3,2},{4,5},{5,4},{6,7},{7,6},{8,9},{9,8},{10,11... | collective-permute-start | bytes 245768 | tf_op jit(solution)/shard_map/ppermute | solution.py:505
  13.3 5.3 %copy-start = (f32[1024]{0:T(1024)S(1)}, f32[1024]{0:T(1024)}, u32[]{:S(2)}) copy-start(f32[1024]{0:T(1024)} %param.9) | copy-start | bytes 12292
  13.3 5.3 %collective-permute-start.3 = (bf16[2,144,128]{2,1,0:T(8,128)(2,1)S(1)}, bf16[2,144,128]{2,1,0:T(8,128)(2,1)S(1)}, u32[]{:S(2)}, u32[]{:S(2)}) collective-permute-start(bf16[2,144,128]{2,1,0:T(8,128)(2,1)S(1)} %group_total.1), channel_id=1, source_target_pairs={{0,4},{1,5},{2,6},{3,7},{4,0},{5,1},{6,2},{7,3},{8,12},{9,13},{10,... | collective-permute-start | bytes 221192 | tf_op jit(solution)/shard_map/ppermute | solution.py:505
  19.3 5.4 %collective-permute-start.6 = (bf16[2,144,128]{2,1,0:T(8,128)(2,1)S(1)}, bf16[2,144,128]{2,1,0:T(8,128)(2,1)S(1)}, u32[]{:S(2)}, u32[]{:S(2)}) collective-permute-start(bf16[2,144,128]{2,1,0:T(8,128)(2,1)S(1)} %get-tuple-element.75), channel_id=1, source_target_pairs={{0,3},{1,2},{2,1},{3,0},{4,7},{5,6},{6,5},{7,4},{8,11},{9,10},{10,... | collective-permute-start | bytes 221192 | tf_op jit(solution)/shard_map/ppermute | solution.py:505
  21.3 4.6 %collective-permute-start.4 = (bf16[2,144,128]{2,1,0:T(8,128)(2,1)S(1)}, bf16[2,144,128]{2,1,0:T(8,128)(2,1)S(1)}, u32[]{:S(2)}, u32[]{:S(2)}) collective-permute-start(bf16[2,144,128]{2,1,0:T(8,128)(2,1)S(1)} %get-tuple-element.71), channel_id=1, source_target_pairs={{0,2},{1,3},{2,0},{3,1},{4,6},{5,7},{6,4},{7,5},{8,10},{9,11},{10,... | collective-permute-start | bytes 221192 | tf_op jit(solution)/shard_map/ppermute | solution.py:505
  21.9 4.4 %collective-permute-start.5 = (bf16[2,144,128]{2,1,0:T(8,128)(2,1)S(1)}, bf16[2,144,128]{2,1,0:T(8,128)(2,1)S(1)}, u32[]{:S(2)}, u32[]{:S(2)}) collective-permute-start(bf16[2,144,128]{2,1,0:T(8,128)(2,1)S(1)} %get-tuple-element.72), channel_id=1, source_target_pairs={{0,1},{1,0},{2,3},{3,2},{4,5},{5,4},{6,7},{7,6},{8,9},{9,8},{10,11... | collective-permute-start | bytes 221192 | tf_op jit(solution)/shard_map/ppermute | solution.py:505

commit v10 on v9

--- a/solution.py
+++ b/solution.py
@@ -310,11 +310,13 @@
     kf, vf = edge_kv(own, before, wk, wv)
     qf = silu_of_twice(edge_rows(own[16:24], before[16:24], wq * 0.5)) * SCALE
     blank = jnp.zeros((8, HDIM), F32)
-    qf, kf, vf = (jnp.concatenate([a, blank], axis=0).astype(BF16) for a in (edge_only(qf), kf, vf))
-    scores = dot(qf, kf, ((1,), (1,)))
-    causal = rows_iota(scores.shape) >= lax.broadcasted_iota(jnp.int32, scores.shape, 1)
-    scores = jnp.where(causal, scores, 0.0).astype(BF16)
-    return qf, dot(scores, vf, ((1,), (0,))), dot(kf, vf, ((0,), (0,)))
+    qf, kf, vf = (a.astype(BF16).astype(F32) for a in (edge_only(qf), kf, vf))
+    inner = blank
+    for back in range(CONV - 1):
+        scores = jnp.sum(qf * pltpu.roll(kf, back, 0), axis=1, keepdims=True)
+        inner = inner + scores.astype(BF16).astype(F32) * pltpu.roll(vf, back, 0)
+    qf, kf, vf = (jnp.concatenate([a, blank], axis=0).astype(BF16) for a in (qf, kf, vf))
+    return qf, jnp.concatenate([inner, blank], axis=0), dot(kf, vf, ((0,), (0,)))
 
 
 def edges_kernel(p0, p1, p2, p3, w_ref, qf_ref, inner_ref, before_ref, with_ref, first_ref, buf):
@@ -355,13 +357,12 @@
     )(*packets, conv_weight)
 
 
-def prefix_kernel(qf_ref, inner_ref, before_ref, with_ref, first_ref, x_ref, w_ref, gain_ref, o0, o1, o2, o3, out):
+def prefix_kernel(qf_ref, inner_ref, before_ref, with_ref, first_ref, x_ref, w_ref, o0, o1, o2, o3, out):
     later = (group() > 0).astype(F32)
     blank = jnp.zeros((8, HDIM), F32)
     per = x_ref.shape[0]
     for h in range(per):
         taps = [taps_of(w_ref, which, member(), h, per) for which in range(3)]
-        gain = gain_ref[:, pl.ds(pl.multiple_of((member() * per + h) * HDIM, HDIM), HDIM)]
         base = x_ref[h, 0:HDIM].astype(F32) * later
         tail = unpack_tail(x_ref[h, HDIM:].astype(F32) * later)
         qf, inner, first = edge_features(first_ref[h].astype(F32), tail, *taps)
@@ -374,25 +375,24 @@
                 prefix = base + before_ref[t - 1, h]
                 shifted = base + with_ref[t - 1, h]
             o = inner + dot(qf, prefix.astype(BF16), ((1,), (0,)))
-            o = o * lax.rsqrt(jnp.mean(o * o, axis=1, keepdims=True) + 1e-06) * gain
             out[t, h, 0:HDIM] = shifted.astype(BF16)
             out[t, h, HDIM:] = jnp.concatenate([pltpu.roll(o[0:8], 5, 0), blank], axis=0).astype(BF16)
     for j, o_ref in enumerate((o0, o1, o2, o3)):
         o_ref[...] = out[member() ^ j]
 
 
-def member_prefixes(edges, incoming, conv_weight, gain):
+def member_prefixes(edges, incoming, conv_weight):
     heads = incoming.shape[0]
     out = jax.ShapeDtypeStruct((heads, HDIM + FIX, HDIM), BF16)
     return pl.pallas_call(
         prefix_kernel,
-        in_specs=[VMEM] * (len(edges) + 3),
+        in_specs=[VMEM] * (len(edges) + 2),
         out_specs=[VMEM] * GROUP,
         out_shape=[out] * GROUP,
         scratch_shapes=[pltpu.VMEM((GROUP, heads, HDIM + FIX, HDIM), BF16)],
         compiler_params=pltpu.CompilerParams(vmem_limit_bytes=8 << 20),
         name="member_prefixes",
-    )(*edges, incoming, conv_weight, gain)
+    )(*edges, incoming, conv_weight)
 
 
 def inner_kernel(quarters, slots, q_ref, w_ref, *refs):
@@ -463,10 +463,10 @@
                 place = places[i] * per + h
                 gain = gain_ref[:, pl.ds(pl.multiple_of((quarter * per + h) * HDIM, HDIM), HDIM)]
                 o = inner_refs[i][place, rows] + dot(qf_refs[i][place, rows], packets[i][h, 0:HDIM], ((1,), (0,)))
-                o = o * lax.rsqrt(jnp.mean(o * o, axis=1, keepdims=True) + 1e-06) * gain
                 if c == 0:
                     fixed = packets[i][h, HDIM:].astype(F32)
                     o = jnp.concatenate([jnp.where(there, fixed, o[0:FIX]), o[FIX:]], axis=0)
+                o = o * lax.rsqrt(jnp.mean(o * o, axis=1, keepdims=True) + 1e-06) * gain
                 out_buf[i, rows, h * HDIM : (h + 1) * HDIM] = o.astype(BF16)
             cols = pl.ds(pl.multiple_of(quarter * per * HDIM, per * HDIM), per * HDIM)
             copies.append(pltpu.make_async_copy(out_buf.at[i, rows], out_hbm.at[rows, cols], sem.at[i, c]))
@@ -544,7 +544,7 @@
         incoming = jnp.concatenate([prefix.astype(BF16), tail], axis=1)
     edges = member_edges(packets, conv_weight)
     (incoming, edges), piece_b = beside((2, 1), (incoming, edges))
-    sends = member_prefixes(edges, incoming, conv_weight, gain)
+    sends = member_prefixes(edges, incoming, conv_weight)
     out = finish((0,), [sends[0]], [piece_a], (0,), gain)
     far, near = swapped(sends[3], 3), [swapped(sends[j], j) for j in (2, 1)]
     far, out = lax.optimization_barrier((far, out))

time: 27.9 us -> 27.8 us (level)
  Pallas kernels: 14.7 us -> 14.3 us
  waiting for transfers between devices: 2.07 us -> 2.37 us
    pallas_call x1, Pallas kernels: 0.61 us -> 0.31 us  [member_edges(): pl.pallas_call(edges_kernel, in_specs=[VMEM] * (GROUP + 1), out_specs=[VM...]
    ppermute x7, waiting for transfers between devices: 2.07 us -> 2.37 us  [swapped(): return lax.ppermute(value, 'ctx', [(s, s ^ bits) for s in range(count)])]
  transfers between devices with their start and end apart: 7 -> 7, of which waited for: 5 -> 5; matrix products, arithmetic and copies ran while one was open for 0% -> 0% of each run, Pallas kernels for 29% -> 28%
where the time goes in v10:
time: 27.8 us; the launch traced here: 27.7 us
  Pallas kernels  14.3 us (51%)
  starting transfers between devices  10.9 us (39%)
  waiting for transfers between devices  2.37 us (9%)
    ppermute x7, starting transfers between devices, swapped(): return lax.ppermute(value, 'ctx', [(s, s ^ bits) for s in range(count)])  10.9 us
    pallas_call x1, Pallas kernels, early_states(): pl.pallas_call(functools.partial(early_kernel, quarters), in_specs=[HBM]...  4.14 us
    pallas_call x2, Pallas kernels, inner_attention(): pl.pallas_call(functools.partial(inner_kernel, quarters, slots), in_specs...  3.97 us
    pallas_call x3, Pallas kernels, finish(): pl.pallas_call(functools.partial(finish_kernel, quarters, places, len(oth...  3.93 us
    ppermute x7, waiting for transfers between devices, swapped(): return lax.ppermute(value, 'ctx', [(s, s ^ bits) for s in range(count)])  2.37 us
    pallas_call x1, Pallas kernels, own_states(): pl.pallas_call(own_kernel, in_specs=[VMEM] * 4, out_specs=[VMEM] * 3, out...  1.18 us
  transfers between devices with their start and end apart: 7, of which 5 were waited for; matrix products, arithmetic and copies ran while one was open for 0% of the time, Pallas kernels for 28%

profile of v10, /device:TPU:0, one launch (start us, length us, event | category | flops | bytes accessed | tf_op | source)
XLA Modules:
  0.0 27.7 jit_solution(12782385675635125752)
XLA Ops:
  0.0 4.1 %early_states.1 = (bf16[6,1024,128]{2,1,0:T(8,128)(2,1)S(1)}, bf16[6,1024,128]{2,1,0:T(8,128)(2,1)S(1)}, bf16[6,160,128]{2,1,0:T(8,128)(2,1)S(1)}, bf16[1,1024,2...) custom-call(bf16[1024,1024]{1,0:T(8,128)(2,1)} %q_hbm.1, ...), custom_call_target="tpu_custom_call" | custom-call | flops 268435456 | bytes 8388608 | tf_op jit(solution)/shard_map/early_states/pallas_call | solution.py:184
  4.2 4.0 %collective-permute-start.2 = (bf16[2,160,128]{2,1,0:T(8,128)(2,1)S(1)}, bf16[2,160,128]{2,1,0:T(8,128)(2,1)S(1)}, u32[]{:S(2)}, u32[]{:S(2)}) collective-permute-start(bf16[2,160,128]{2,1,0:T(8,128)(2,1)S(1)} %get-tuple-element.81), channel_id=1, source_target_pairs={{0,3},{1,2},{2,1},{3,0},{4,7},{5,6},{6,5},{7,4},{8,11},{9,10},{10,... | collective-permute-start | bytes 245768 | tf_op jit(solution)/shard_map/ppermute | solution.py:505
  8.2 0.5 %collective-permute-start.1 = (bf16[2,160,128]{2,1,0:T(8,128)(2,1)S(1)}, bf16[2,160,128]{2,1,0:T(8,128)(2,1)S(1)}, u32[]{:S(2)}, u32[]{:S(2)}) collective-permute-start(bf16[2,160,128]{2,1,0:T(8,128)(2,1)S(1)} %get-tuple-element.82), channel_id=1, source_target_pairs={{0,2},{1,3},{2,0},{3,1},{4,6},{5,7},{6,4},{7,5},{8,10},{9,11},{10,... | collective-permute-start | bytes 245768 | tf_op jit(solution)/shard_map/ppermute | solution.py:505
  8.7 0.2 collective-permute-start
  8.8 1.2 %own_states.1 = (bf16[2,1024,128]{2,1,0:T(8,128)(2,1)S(1)}, bf16[2,1024,128]{2,1,0:T(8,128)(2,1)S(1)}, bf16[2,160,128]{2,1,0:T(8,128)(2,1)S(1)}) custom-call(bf16[1,1024,256]{2,1,0:T(8,128)(2,1)S(1)} %get-tuple-element.43.k_ref, bf16[1,1024,256]{2,1,0:T(8,128)(2,1)S(1)} %get-tuple-element.44.v_ref, bf16[1024,1024]{1,0:T(8,128)(2,1)S(1)} %get-tuple-element.45.q_ref, ...), custom_call_target="tpu_custom_call" | custom-call | flops 67108864 | bytes 2097152 | tf_op jit(solution)/shard_map/own_states/pallas_call | solution.py:215
  10.0 2.0 %inner_attention.2 = (bf16[4,1024,128]{2,1,0:T(8,128)(2,1)S(1)}, f32[4,1024,128]{2,1,0:T(8,128)S(1)}) custom-call(bf16[1024,1024]{1,0:T(8,128)(2,1)S(1)} %get-tuple-element.45.q_ref, f32[3,4,1024]{2,1,0:T(4,128)S(1)} %get-tuple-element.46.w_ref.refs_4_, bf16[2,1024,128]{2,1,0:T(8,128)(2,1)S(1)} %get-tuple-element.49.refs_0_, ...), custom_call_target="tpu_custom_call" | custom-call | flops 536870912 | bytes 6291456 | tf_op jit(solution)/shard_map/inner_attention/pallas_call | solution.py:431
  12.0 0.0 collective-permute-done.2.refs_3_.p3
  12.0 0.8 %collective-permute-done.1.refs_2_.p2 = bf16[2,160,128]{2,1,0:T(8,128)(2,1)S(1)} collective-permute-done((bf16[2,160,128]{2,1,0:T(8,128)(2,1)S(1)}, bf16[2,160,128]{2,1,0:T(8,128)(2,1)S(1)}, u32[]{:S(2)}, u32[]{:S(2)}) %collective-permute-start.1) | collective-permute-done | bytes 81952 | tf_op jit(solution)/shard_map/ppermute | solution.py:505
  12.8 0.3 collective-permute-done.refs_1_.p1
  13.1 0.2 group_total.1
  13.3 0.0 copy-start
  13.3 2.7 %collective-permute-start.3 = (bf16[2,144,128]{2,1,0:T(8,128)(2,1)S(1)}, bf16[2,144,128]{2,1,0:T(8,128)(2,1)S(1)}, u32[]{:S(2)}, u32[]{:S(2)}) collective-permute-start(bf16[2,144,128]{2,1,0:T(8,128)(2,1)S(1)} %group_total.1), channel_id=1, source_target_pairs={{0,4},{1,5},{2,6},{3,7},{4,0},{5,1},{6,2},{7,3},{8,12},{9,13},{10,... | collective-permute-start | bytes 221192 | tf_op jit(solution)/shard_map/ppermute | solution.py:505
  16.0 2.0 %inner_attention.3 = (bf16[4,1024,128]{2,1,0:T(8,128)(2,1)S(1)}, f32[4,1024,128]{2,1,0:T(8,128)S(1)}) custom-call(bf16[1024,1024]{1,0:T(8,128)(2,1)S(1)} %get-tuple-element.45.q_ref, f32[3,4,1024]{2,1,0:T(4,128)S(1)} %get-tuple-element.46.w_ref.refs_4_, bf16[6,1024,128]{2,1,0:T(8,128)(2,1)S(1)} %get-tuple-element.50.refs_1_.refs_0_, ...), custom_call_target="tpu_custom_call" | custom-call | flops 536870912 | bytes 6291456 | tf_op jit(solution)/shard_map/inner_attention/pallas_call | solution.py:431
  18.0 0.3 %member_edges.1 = (bf16[3,2,16,128]{3,2,1,0:T(8,128)(2,1)S(1)}, f32[3,2,16,128]{3,2,1,0:T(8,128)S(1)}, f32[3,2,128,128]{3,2,1,0:T(8,128)S(1)}, f32[3,2,128,128]{3,2,1,0:T(8,128)S(1)}, bf16[2,32,128]{2,1,0:T(8,128)(2,1)S(1)}) custom-call(bf16[2,160,128]{2,1,0:T(8,128)(2,1)S(1)} %get-tuple-element.47.refs_0_.p0, ...), custom_call_target="tpu_custom_call" | custom-call | tf_op jit(solution)/shard_map/member_edges/pallas_call | solution.py:343
  18.3 0.4 %collective-permute-done.3.x_ref = bf16[2,144,128]{2,1,0:T(8,128)(2,1)S(1)} collective-permute-done((bf16[2,144,128]{2,1,0:T(8,128)(2,1)S(1)}, bf16[2,144,128]{2,1,0:T(8,128)(2,1)S(1)}, u32[]{:S(2)}, u32[]{:S(2)}) %collective-permute-start.3) | collective-permute-done | bytes 73760 | tf_op jit(solution)/shard_map/ppermute | solution.py:505
  18.7 0.5 %member_prefixes.1 = (bf16[2,144,128]{2,1,0:T(8,128)(2,1)S(1)}, bf16[2,144,128]{2,1,0:T(8,128)(2,1)S(1)}, bf16[2,144,128]{2,1,0:T(8,128)(2,1)S(1)}, bf16[2,144,128]{2,1,0:T(8,128)(2,1)S(1)}) custom-call(bf16[3,2,16,128]{3,2,1,0:T(8,128)(2,1)S(1)} %get-tuple-element.65.qf_ref, f32[3,2,16,128]{3,2,1,0:T(8,128)S(1)} %get-tuple-element.66.inner_ref, ...), custom_call_target="tpu_custom_call" | custom-call | tf_op jit(solution)/shard_map/member_prefixes/pallas_call | solution.py:387
  19.2 2.0 %collective-permute-start.6 = (bf16[2,144,128]{2,1,0:T(8,128)(2,1)S(1)}, bf16[2,144,128]{2,1,0:T(8,128)(2,1)S(1)}, u32[]{:S(2)}, u32[]{:S(2)}) collective-permute-start(bf16[2,144,128]{2,1,0:T(8,128)(2,1)S(1)} %get-tuple-element.75), channel_id=1, source_target_pairs={{0,3},{1,2},{2,1},{3,0},{4,7},{5,6},{6,5},{7,4},{8,11},{9,10},{10,... | collective-permute-start | bytes 221192 | tf_op jit(solution)/shard_map/ppermute | solution.py:505
  21.2 0.6 %collective-permute-start.4 = (bf16[2,144,128]{2,1,0:T(8,128)(2,1)S(1)}, bf16[2,144,128]{2,1,0:T(8,128)(2,1)S(1)}, u32[]{:S(2)}, u32[]{:S(2)}) collective-permute-start(bf16[2,144,128]{2,1,0:T(8,128)(2,1)S(1)} %get-tuple-element.71), channel_id=1, source_target_pairs={{0,2},{1,3},{2,0},{3,1},{4,6},{5,7},{6,4},{7,5},{8,10},{9,11},{10,... | collective-permute-start | bytes 221192 | tf_op jit(solution)/shard_map/ppermute | solution.py:505
  21.8 1.0 %collective-permute-start.5 = (bf16[2,144,128]{2,1,0:T(8,128)(2,1)S(1)}, bf16[2,144,128]{2,1,0:T(8,128)(2,1)S(1)}, u32[]{:S(2)}, u32[]{:S(2)}) collective-permute-start(bf16[2,144,128]{2,1,0:T(8,128)(2,1)S(1)} %get-tuple-element.72), channel_id=1, source_target_pairs={{0,1},{1,0},{2,3},{3,2},{4,5},{5,4},{6,7},{7,6},{8,9},{9,8},{10,11... | collective-permute-start | bytes 221192 | tf_op jit(solution)/shard_map/ppermute | solution.py:505
  22.8 0.0 copy-done
  22.8 1.2 %finish.3.refs_3_ = bf16[1024,1024]{1,0:T(8,128)(2,1)} custom-call(f32[1,1024]{1,0:T(1,128)S(1)} %bitcast.1, bf16[2,144,128]{2,1,0:T(8,128)(2,1)S(1)} %get-tuple-element.76.refs_0_, bf16[4,1024,128]{2,1,0:T(8,128)(2,1)S(1)} %get-tuple-element.77.refs_1_, f32[4,1024,128]{2,1,0:T(8,128)S(1)} %get-tuple-element.78.refs_2_), custom_call_target="tpu_custom_call" | custom-call | flops 67108864 | bytes 2097152 | tf_op jit(solution)/shard_map/finish/pallas_call | solution.py:483
  24.0 0.7 %collective-permute-done.6.refs_0_ = bf16[2,144,128]{2,1,0:T(8,128)(2,1)S(1)} collective-permute-done((bf16[2,144,128]{2,1,0:T(8,128)(2,1)S(1)}, bf16[2,144,128]{2,1,0:T(8,128)(2,1)S(1)}, u32[]{:S(2)}, u32[]{:S(2)}) %collective-permute-start.6) | collective-permute-done | bytes 73760 | tf_op jit(solution)/shard_map/ppermute | solution.py:505
  24.6 1.2 %finish.4.refs_6_ = bf16[1024,1024]{1,0:T(8,128)(2,1)} custom-call(f32[1,1024]{1,0:T(1,128)S(1)} %bitcast.2, bf16[2,144,128]{2,1,0:T(8,128)(2,1)S(1)} %collective-permute-done.6.refs_0_, bf16[4,1024,128]{2,1,0:T(8,128)(2,1)S(1)} %get-tuple-element.77.refs_1_, f32[4,1024,128]{2,1,0:T(8,128)S(1)} %get-tuple-element.78.refs_2_, ...), custom_call_target="tpu_custom_call", output_to_operand_aliasing={{}: (4, {})} | custom-call | flops 67108864 | bytes 2097152 | tf_op jit(solution)/shard_map/finish/pallas_call | solution.py:483
  25.8 0.0 collective-permute-done.4.refs_0_
  25.9 0.3 %collective-permute-done.5.refs_1_ = bf16[2,144,128]{2,1,0:T(8,128)(2,1)S(1)} collective-permute-done((bf16[2,144,128]{2,1,0:T(8,128)(2,1)S(1)}, bf16[2,144,128]{2,1,0:T(8,128)(2,1)S(1)}, u32[]{:S(2)}, u32[]{:S(2)}) %collective-permute-start.5) | collective-permute-done | bytes 73760 | tf_op jit(solution)/shard_map/ppermute | solution.py:505
  26.1 1.5 %finish.5 = bf16[1024,1024]{1,0:T(8,128)(2,1)} custom-call(f32[1,1024]{1,0:T(1,128)S(1)} %bitcast.3, bf16[2,144,128]{2,1,0:T(8,128)(2,1)S(1)} %collective-permute-done.4.refs_0_, bf16[2,144,128]{2,1,0:T(8,128)(2,1)S(1)} %collective-permute-done.5.refs_1_, ...), custom_call_target="tpu_custom_call", output_to_operand_aliasing={{}: (7, {})} | custom-call | flops 134217728 | bytes 4194304 | tf_op jit(solution)/shard_map/finish/pallas_call | solution.py:483
  (1 shorter events, 0.0 us)
Async XLA Ops:
  4.2 7.9 %collective-permute-start.2 = (bf16[2,160,128]{2,1,0:T(8,128)(2,1)S(1)}, bf16[2,160,128]{2,1,0:T(8,128)(2,1)S(1)}, u32[]{:S(2)}, u32[]{:S(2)}) collective-permute-start(bf16[2,160,128]{2,1,0:T(8,128)(2,1)S(1)} %get-tuple-element.81), channel_id=1, source_target_pairs={{0,3},{1,2},{2,1},{3,0},{4,7},{5,6},{6,5},{7,4},{8,11},{9,10},{10,... | collective-permute-start | bytes 245768 | tf_op jit(solution)/shard_map/ppermute | solution.py:505
  8.2 4.6 %collective-permute-start.1 = (bf16[2,160,128]{2,1,0:T(8,128)(2,1)S(1)}, bf16[2,160,128]{2,1,0:T(8,128)(2,1)S(1)}, u32[]{:S(2)}, u32[]{:S(2)}) collective-permute-start(bf16[2,160,128]{2,1,0:T(8,128)(2,1)S(1)} %get-tuple-element.82), channel_id=1, source_target_pairs={{0,2},{1,3},{2,0},{3,1},{4,6},{5,7},{6,4},{7,5},{8,10},{9,11},{10,... | collective-permute-start | bytes 245768 | tf_op jit(solution)/shard_map/ppermute | solution.py:505
  8.7 4.4 %collective-permute-start = (bf16[2,160,128]{2,1,0:T(8,128)(2,1)S(1)}, bf16[2,160,128]{2,1,0:T(8,128)(2,1)S(1)}, u32[]{:S(2)}, u32[]{:S(2)}) collective-permute-start(bf16[2,160,128]{2,1,0:T(8,128)(2,1)S(1)} %get-tuple-element.83), channel_id=1, source_target_pairs={{0,1},{1,0},{2,3},{3,2},{4,5},{5,4},{6,7},{7,6},{8,9},{9,8},{10,11... | collective-permute-start | bytes 245768 | tf_op jit(solution)/shard_map/ppermute | solution.py:505
  13.3 9.4 %copy-start = (f32[1024]{0:T(1024)S(1)}, f32[1024]{0:T(1024)}, u32[]{:S(2)}) copy-start(f32[1024]{0:T(1024)} %param.9) | copy-start | bytes 12292
  13.3 5.3 %collective-permute-start.3 = (bf16[2,144,128]{2,1,0:T(8,128)(2,1)S(1)}, bf16[2,144,128]{2,1,0:T(8,128)(2,1)S(1)}, u32[]{:S(2)}, u32[]{:S(2)}) collective-permute-start(bf16[2,144,128]{2,1,0:T(8,128)(2,1)S(1)} %group_total.1), channel_id=1, source_target_pairs={{0,4},{1,5},{2,6},{3,7},{4,0},{5,1},{6,2},{7,3},{8,12},{9,13},{10,... | collective-permute-start | bytes 221192 | tf_op jit(solution)/shard_map/ppermute | solution.py:505
  19.2 5.4 %collective-permute-start.6 = (bf16[2,144,128]{2,1,0:T(8,128)(2,1)S(1)}, bf16[2,144,128]{2,1,0:T(8,128)(2,1)S(1)}, u32[]{:S(2)}, u32[]{:S(2)}) collective-permute-start(bf16[2,144,128]{2,1,0:T(8,128)(2,1)S(1)} %get-tuple-element.75), channel_id=1, source_target_pairs={{0,3},{1,2},{2,1},{3,0},{4,7},{5,6},{6,5},{7,4},{8,11},{9,10},{10,... | collective-permute-start | bytes 221192 | tf_op jit(solution)/shard_map/ppermute | solution.py:505
  21.2 4.6 %collective-permute-start.4 = (bf16[2,144,128]{2,1,0:T(8,128)(2,1)S(1)}, bf16[2,144,128]{2,1,0:T(8,128)(2,1)S(1)}, u32[]{:S(2)}, u32[]{:S(2)}) collective-permute-start(bf16[2,144,128]{2,1,0:T(8,128)(2,1)S(1)} %get-tuple-element.71), channel_id=1, source_target_pairs={{0,2},{1,3},{2,0},{3,1},{4,6},{5,7},{6,4},{7,5},{8,10},{9,11},{10,... | collective-permute-start | bytes 221192 | tf_op jit(solution)/shard_map/ppermute | solution.py:505
  21.8 4.4 %collective-permute-start.5 = (bf16[2,144,128]{2,1,0:T(8,128)(2,1)S(1)}, bf16[2,144,128]{2,1,0:T(8,128)(2,1)S(1)}, u32[]{:S(2)}, u32[]{:S(2)}) collective-permute-start(bf16[2,144,128]{2,1,0:T(8,128)(2,1)S(1)} %get-tuple-element.72), channel_id=1, source_target_pairs={{0,1},{1,0},{2,3},{3,2},{4,5},{5,4},{6,7},{7,6},{8,9},{9,8},{10,11... | collective-permute-start | bytes 221192 | tf_op jit(solution)/shard_map/ppermute | solution.py:505

commit v11 on v10

--- a/solution.py
+++ b/solution.py
@@ -12,7 +12,7 @@
 GROUP = 4
 ROWS = 64
 CHUNK = 256
-PARTS = 4
+PARTS = 2
 AUX = 32
 TAIL = 16
 FIX = 16

time: 27.8 us -> 27.8 us (level)
  transfers between devices with their start and end apart: 7 -> 7, of which waited for: 5 -> 5; matrix products, arithmetic and copies ran while one was open for 0% -> 0% of each run, Pallas kernels for 28% -> 29%
where the time goes in v11:
time: 27.8 us; the launch traced here: 27.7 us
  Pallas kernels  14.4 us (52%)
  starting transfers between devices  10.9 us (39%)
  waiting for transfers between devices  2.31 us (8%)
    ppermute x7, starting transfers between devices, swapped(): return lax.ppermute(value, 'ctx', [(s, s ^ bits) for s in range(count)])  10.9 us
    pallas_call x1, Pallas kernels, early_states(): pl.pallas_call(functools.partial(early_kernel, quarters), in_specs=[HBM]...  4.14 us
    pallas_call x3, Pallas kernels, finish(): pl.pallas_call(functools.partial(finish_kernel, quarters, places, len(oth...  3.99 us
    pallas_call x2, Pallas kernels, inner_attention(): pl.pallas_call(functools.partial(inner_kernel, quarters, slots), in_specs...  3.97 us
    ppermute x7, waiting for transfers between devices, swapped(): return lax.ppermute(value, 'ctx', [(s, s ^ bits) for s in range(count)])  2.31 us
    pallas_call x1, Pallas kernels, own_states(): pl.pallas_call(own_kernel, in_specs=[VMEM] * 4, out_specs=[VMEM] * 3, out...  1.18 us
  transfers between devices with their start and end apart: 7, of which 5 were waited for; matrix products, arithmetic and copies ran while one was open for 0% of the time, Pallas kernels for 29%

profile of v11, /device:TPU:0, one launch (start us, length us, event | category | flops | bytes accessed | tf_op | source)
XLA Modules:
  0.0 27.7 jit_solution(11358122921008452261)
XLA Ops:
  0.0 4.1 %early_states.1 = (bf16[6,1024,128]{2,1,0:T(8,128)(2,1)S(1)}, bf16[6,1024,128]{2,1,0:T(8,128)(2,1)S(1)}, bf16[6,160,128]{2,1,0:T(8,128)(2,1)S(1)}, bf16[1,1024,2...) custom-call(bf16[1024,1024]{1,0:T(8,128)(2,1)} %q_hbm.1, ...), custom_call_target="tpu_custom_call" | custom-call | flops 268435456 | bytes 8388608 | tf_op jit(solution)/shard_map/early_states/pallas_call | solution.py:184
  4.2 4.0 %collective-permute-start.2 = (bf16[2,160,128]{2,1,0:T(8,128)(2,1)S(1)}, bf16[2,160,128]{2,1,0:T(8,128)(2,1)S(1)}, u32[]{:S(2)}, u32[]{:S(2)}) collective-permute-start(bf16[2,160,128]{2,1,0:T(8,128)(2,1)S(1)} %get-tuple-element.81), channel_id=1, source_target_pairs={{0,3},{1,2},{2,1},{3,0},{4,7},{5,6},{6,5},{7,4},{8,11},{9,10},{10,... | collective-permute-start | bytes 245768 | tf_op jit(solution)/shard_map/ppermute | solution.py:505
  8.2 0.5 %collective-permute-start.1 = (bf16[2,160,128]{2,1,0:T(8,128)(2,1)S(1)}, bf16[2,160,128]{2,1,0:T(8,128)(2,1)S(1)}, u32[]{:S(2)}, u32[]{:S(2)}) collective-permute-start(bf16[2,160,128]{2,1,0:T(8,128)(2,1)S(1)} %get-tuple-element.82), channel_id=1, source_target_pairs={{0,2},{1,3},{2,0},{3,1},{4,6},{5,7},{6,4},{7,5},{8,10},{9,11},{10,... | collective-permute-start | bytes 245768 | tf_op jit(solution)/shard_map/ppermute | solution.py:505
  8.7 0.2 collective-permute-start
  8.8 1.2 %own_states.1 = (bf16[2,1024,128]{2,1,0:T(8,128)(2,1)S(1)}, bf16[2,1024,128]{2,1,0:T(8,128)(2,1)S(1)}, bf16[2,160,128]{2,1,0:T(8,128)(2,1)S(1)}) custom-call(bf16[1,1024,256]{2,1,0:T(8,128)(2,1)S(1)} %get-tuple-element.43.k_ref, bf16[1,1024,256]{2,1,0:T(8,128)(2,1)S(1)} %get-tuple-element.44.v_ref, bf16[1024,1024]{1,0:T(8,128)(2,1)S(1)} %get-tuple-element.45.q_ref, ...), custom_call_target="tpu_custom_call" | custom-call | flops 67108864 | bytes 2097152 | tf_op jit(solution)/shard_map/own_states/pallas_call | solution.py:215
  10.0 2.0 %inner_attention.2 = (bf16[4,1024,128]{2,1,0:T(8,128)(2,1)S(1)}, f32[4,1024,128]{2,1,0:T(8,128)S(1)}) custom-call(bf16[1024,1024]{1,0:T(8,128)(2,1)S(1)} %get-tuple-element.45.q_ref, f32[3,4,1024]{2,1,0:T(4,128)S(1)} %get-tuple-element.46.w_ref.refs_4_, bf16[2,1024,128]{2,1,0:T(8,128)(2,1)S(1)} %get-tuple-element.49.refs_0_, ...), custom_call_target="tpu_custom_call" | custom-call | flops 536870912 | bytes 6291456 | tf_op jit(solution)/shard_map/inner_attention/pallas_call | solution.py:431
  12.0 0.0 collective-permute-done.2.refs_3_.p3
  12.0 0.8 %collective-permute-done.1.refs_2_.p2 = bf16[2,160,128]{2,1,0:T(8,128)(2,1)S(1)} collective-permute-done((bf16[2,160,128]{2,1,0:T(8,128)(2,1)S(1)}, bf16[2,160,128]{2,1,0:T(8,128)(2,1)S(1)}, u32[]{:S(2)}, u32[]{:S(2)}) %collective-permute-start.1) | collective-permute-done | bytes 81952 | tf_op jit(solution)/shard_map/ppermute | solution.py:505
  12.8 0.3 collective-permute-done.refs_1_.p1
  13.1 0.2 group_total.1
  13.3 0.0 copy-start
  13.3 2.7 %collective-permute-start.3 = (bf16[2,144,128]{2,1,0:T(8,128)(2,1)S(1)}, bf16[2,144,128]{2,1,0:T(8,128)(2,1)S(1)}, u32[]{:S(2)}, u32[]{:S(2)}) collective-permute-start(bf16[2,144,128]{2,1,0:T(8,128)(2,1)S(1)} %group_total.1), channel_id=1, source_target_pairs={{0,4},{1,5},{2,6},{3,7},{4,0},{5,1},{6,2},{7,3},{8,12},{9,13},{10,... | collective-permute-start | bytes 221192 | tf_op jit(solution)/shard_map/ppermute | solution.py:505
  16.0 2.0 %inner_attention.3 = (bf16[4,1024,128]{2,1,0:T(8,128)(2,1)S(1)}, f32[4,1024,128]{2,1,0:T(8,128)S(1)}) custom-call(bf16[1024,1024]{1,0:T(8,128)(2,1)S(1)} %get-tuple-element.45.q_ref, f32[3,4,1024]{2,1,0:T(4,128)S(1)} %get-tuple-element.46.w_ref.refs_4_, bf16[6,1024,128]{2,1,0:T(8,128)(2,1)S(1)} %get-tuple-element.50.refs_1_.refs_0_, ...), custom_call_target="tpu_custom_call" | custom-call | flops 536870912 | bytes 6291456 | tf_op jit(solution)/shard_map/inner_attention/pallas_call | solution.py:431
  18.0 0.3 %member_edges.1 = (bf16[3,2,16,128]{3,2,1,0:T(8,128)(2,1)S(1)}, f32[3,2,16,128]{3,2,1,0:T(8,128)S(1)}, f32[3,2,128,128]{3,2,1,0:T(8,128)S(1)}, f32[3,2,128,128]{3,2,1,0:T(8,128)S(1)}, bf16[2,32,128]{2,1,0:T(8,128)(2,1)S(1)}) custom-call(bf16[2,160,128]{2,1,0:T(8,128)(2,1)S(1)} %get-tuple-element.47.refs_0_.p0, ...), custom_call_target="tpu_custom_call" | custom-call | tf_op jit(solution)/shard_map/member_edges/pallas_call | solution.py:343
  18.3 0.4 %collective-permute-done.3.x_ref = bf16[2,144,128]{2,1,0:T(8,128)(2,1)S(1)} collective-permute-done((bf16[2,144,128]{2,1,0:T(8,128)(2,1)S(1)}, bf16[2,144,128]{2,1,0:T(8,128)(2,1)S(1)}, u32[]{:S(2)}, u32[]{:S(2)}) %collective-permute-start.3) | collective-permute-done | bytes 73760 | tf_op jit(solution)/shard_map/ppermute | solution.py:505
  18.7 0.5 %member_prefixes.1 = (bf16[2,144,128]{2,1,0:T(8,128)(2,1)S(1)}, bf16[2,144,128]{2,1,0:T(8,128)(2,1)S(1)}, bf16[2,144,128]{2,1,0:T(8,128)(2,1)S(1)}, bf16[2,144,128]{2,1,0:T(8,128)(2,1)S(1)}) custom-call(bf16[3,2,16,128]{3,2,1,0:T(8,128)(2,1)S(1)} %get-tuple-element.65.qf_ref, f32[3,2,16,128]{3,2,1,0:T(8,128)S(1)} %get-tuple-element.66.inner_ref, ...), custom_call_target="tpu_custom_call" | custom-call | tf_op jit(solution)/shard_map/member_prefixes/pallas_call | solution.py:387
  19.2 2.0 %collective-permute-start.6 = (bf16[2,144,128]{2,1,0:T(8,128)(2,1)S(1)}, bf16[2,144,128]{2,1,0:T(8,128)(2,1)S(1)}, u32[]{:S(2)}, u32[]{:S(2)}) collective-permute-start(bf16[2,144,128]{2,1,0:T(8,128)(2,1)S(1)} %get-tuple-element.75), channel_id=1, source_target_pairs={{0,3},{1,2},{2,1},{3,0},{4,7},{5,6},{6,5},{7,4},{8,11},{9,10},{10,... | collective-permute-start | bytes 221192 | tf_op jit(solution)/shard_map/ppermute | solution.py:505
  21.2 0.6 %collective-permute-start.4 = (bf16[2,144,128]{2,1,0:T(8,128)(2,1)S(1)}, bf16[2,144,128]{2,1,0:T(8,128)(2,1)S(1)}, u32[]{:S(2)}, u32[]{:S(2)}) collective-permute-start(bf16[2,144,128]{2,1,0:T(8,128)(2,1)S(1)} %get-tuple-element.71), channel_id=1, source_target_pairs={{0,2},{1,3},{2,0},{3,1},{4,6},{5,7},{6,4},{7,5},{8,10},{9,11},{10,... | collective-permute-start | bytes 221192 | tf_op jit(solution)/shard_map/ppermute | solution.py:505
  21.8 1.0 %collective-permute-start.5 = (bf16[2,144,128]{2,1,0:T(8,128)(2,1)S(1)}, bf16[2,144,128]{2,1,0:T(8,128)(2,1)S(1)}, u32[]{:S(2)}, u32[]{:S(2)}) collective-permute-start(bf16[2,144,128]{2,1,0:T(8,128)(2,1)S(1)} %get-tuple-element.72), channel_id=1, source_target_pairs={{0,1},{1,0},{2,3},{3,2},{4,5},{5,4},{6,7},{7,6},{8,9},{9,8},{10,11... | collective-permute-start | bytes 221192 | tf_op jit(solution)/shard_map/ppermute | solution.py:505
  22.8 0.0 copy-done
  22.8 1.2 %finish.3.refs_3_ = bf16[1024,1024]{1,0:T(8,128)(2,1)} custom-call(f32[1,1024]{1,0:T(1,128)S(1)} %bitcast.1, bf16[2,144,128]{2,1,0:T(8,128)(2,1)S(1)} %get-tuple-element.76.refs_0_, bf16[4,1024,128]{2,1,0:T(8,128)(2,1)S(1)} %get-tuple-element.77.refs_1_, f32[4,1024,128]{2,1,0:T(8,128)S(1)} %get-tuple-element.78.refs_2_), custom_call_target="tpu_custom_call" | custom-call | flops 67108864 | bytes 2097152 | tf_op jit(solution)/shard_map/finish/pallas_call | solution.py:483
  24.0 0.6 %collective-permute-done.6.refs_0_ = bf16[2,144,128]{2,1,0:T(8,128)(2,1)S(1)} collective-permute-done((bf16[2,144,128]{2,1,0:T(8,128)(2,1)S(1)}, bf16[2,144,128]{2,1,0:T(8,128)(2,1)S(1)}, u32[]{:S(2)}, u32[]{:S(2)}) %collective-permute-start.6) | collective-permute-done | bytes 73760 | tf_op jit(solution)/shard_map/ppermute | solution.py:505
  24.6 1.2 %finish.4.refs_6_ = bf16[1024,1024]{1,0:T(8,128)(2,1)} custom-call(f32[1,1024]{1,0:T(1,128)S(1)} %bitcast.2, bf16[2,144,128]{2,1,0:T(8,128)(2,1)S(1)} %collective-permute-done.6.refs_0_, bf16[4,1024,128]{2,1,0:T(8,128)(2,1)S(1)} %get-tuple-element.77.refs_1_, f32[4,1024,128]{2,1,0:T(8,128)S(1)} %get-tuple-element.78.refs_2_, ...), custom_call_target="tpu_custom_call", output_to_operand_aliasing={{}: (4, {})} | custom-call | flops 67108864 | bytes 2097152 | tf_op jit(solution)/shard_map/finish/pallas_call | solution.py:483
  25.9 0.0 collective-permute-done.4.refs_0_
  25.9 0.2 collective-permute-done.5.refs_1_
  26.1 1.5 %finish.5 = bf16[1024,1024]{1,0:T(8,128)(2,1)} custom-call(f32[1,1024]{1,0:T(1,128)S(1)} %bitcast.3, bf16[2,144,128]{2,1,0:T(8,128)(2,1)S(1)} %collective-permute-done.4.refs_0_, bf16[2,144,128]{2,1,0:T(8,128)(2,1)S(1)} %collective-permute-done.5.refs_1_, ...), custom_call_target="tpu_custom_call", output_to_operand_aliasing={{}: (7, {})} | custom-call | flops 134217728 | bytes 4194304 | tf_op jit(solution)/shard_map/finish/pallas_call | solution.py:483
  (1 shorter events, 0.0 us)
Async XLA Ops:
  4.2 7.9 %collective-permute-start.2 = (bf16[2,160,128]{2,1,0:T(8,128)(2,1)S(1)}, bf16[2,160,128]{2,1,0:T(8,128)(2,1)S(1)}, u32[]{:S(2)}, u32[]{:S(2)}) collective-permute-start(bf16[2,160,128]{2,1,0:T(8,128)(2,1)S(1)} %get-tuple-element.81), channel_id=1, source_target_pairs={{0,3},{1,2},{2,1},{3,0},{4,7},{5,6},{6,5},{7,4},{8,11},{9,10},{10,... | collective-permute-start | bytes 245768 | tf_op jit(solution)/shard_map/ppermute | solution.py:505
  8.2 4.6 %collective-permute-start.1 = (bf16[2,160,128]{2,1,0:T(8,128)(2,1)S(1)}, bf16[2,160,128]{2,1,0:T(8,128)(2,1)S(1)}, u32[]{:S(2)}, u32[]{:S(2)}) collective-permute-start(bf16[2,160,128]{2,1,0:T(8,128)(2,1)S(1)} %get-tuple-element.82), channel_id=1, source_target_pairs={{0,2},{1,3},{2,0},{3,1},{4,6},{5,7},{6,4},{7,5},{8,10},{9,11},{10,... | collective-permute-start | bytes 245768 | tf_op jit(solution)/shard_map/ppermute | solution.py:505
  8.7 4.4 %collective-permute-start = (bf16[2,160,128]{2,1,0:T(8,128)(2,1)S(1)}, bf16[2,160,128]{2,1,0:T(8,128)(2,1)S(1)}, u32[]{:S(2)}, u32[]{:S(2)}) collective-permute-start(bf16[2,160,128]{2,1,0:T(8,128)(2,1)S(1)} %get-tuple-element.83), channel_id=1, source_target_pairs={{0,1},{1,0},{2,3},{3,2},{4,5},{5,4},{6,7},{7,6},{8,9},{9,8},{10,11... | collective-permute-start | bytes 245768 | tf_op jit(solution)/shard_map/ppermute | solution.py:505
  13.3 9.4 %copy-start = (f32[1024]{0:T(1024)S(1)}, f32[1024]{0:T(1024)}, u32[]{:S(2)}) copy-start(f32[1024]{0:T(1024)} %param.9) | copy-start | bytes 12292
  13.3 5.3 %collective-permute-start.3 = (bf16[2,144,128]{2,1,0:T(8,128)(2,1)S(1)}, bf16[2,144,128]{2,1,0:T(8,128)(2,1)S(1)}, u32[]{:S(2)}, u32[]{:S(2)}) collective-permute-start(bf16[2,144,128]{2,1,0:T(8,128)(2,1)S(1)} %group_total.1), channel_id=1, source_target_pairs={{0,4},{1,5},{2,6},{3,7},{4,0},{5,1},{6,2},{7,3},{8,12},{9,13},{10,... | collective-permute-start | bytes 221192 | tf_op jit(solution)/shard_map/ppermute | solution.py:505
  19.2 5.4 %collective-permute-start.6 = (bf16[2,144,128]{2,1,0:T(8,128)(2,1)S(1)}, bf16[2,144,128]{2,1,0:T(8,128)(2,1)S(1)}, u32[]{:S(2)}, u32[]{:S(2)}) collective-permute-start(bf16[2,144,128]{2,1,0:T(8,128)(2,1)S(1)} %get-tuple-element.75), channel_id=1, source_target_pairs={{0,3},{1,2},{2,1},{3,0},{4,7},{5,6},{6,5},{7,4},{8,11},{9,10},{10,... | collective-permute-start | bytes 221192 | tf_op jit(solution)/shard_map/ppermute | solution.py:505
  21.2 4.6 %collective-permute-start.4 = (bf16[2,144,128]{2,1,0:T(8,128)(2,1)S(1)}, bf16[2,144,128]{2,1,0:T(8,128)(2,1)S(1)}, u32[]{:S(2)}, u32[]{:S(2)}) collective-permute-start(bf16[2,144,128]{2,1,0:T(8,128)(2,1)S(1)} %get-tuple-element.71), channel_id=1, source_target_pairs={{0,2},{1,3},{2,0},{3,1},{4,6},{5,7},{6,4},{7,5},{8,10},{9,11},{10,... | collective-permute-start | bytes 221192 | tf_op jit(solution)/shard_map/ppermute | solution.py:505
  21.8 4.4 %collective-permute-start.5 = (bf16[2,144,128]{2,1,0:T(8,128)(2,1)S(1)}, bf16[2,144,128]{2,1,0:T(8,128)(2,1)S(1)}, u32[]{:S(2)}, u32[]{:S(2)}) collective-permute-start(bf16[2,144,128]{2,1,0:T(8,128)(2,1)S(1)} %get-tuple-element.72), channel_id=1, source_target_pairs={{0,1},{1,0},{2,3},{3,2},{4,5},{5,4},{6,7},{7,6},{8,9},{9,8},{10,11... | collective-permute-start | bytes 221192 | tf_op jit(solution)/shard_map/ppermute | solution.py:505

commit v12 on v10

--- a/solution.py
+++ b/solution.py
@@ -545,10 +545,8 @@
     edges = member_edges(packets, conv_weight)
     (incoming, edges), piece_b = beside((2, 1), (incoming, edges))
     sends = member_prefixes(edges, incoming, conv_weight)
-    out = finish((0,), [sends[0]], [piece_a], (0,), gain)
     far, near = swapped(sends[3], 3), [swapped(sends[j], j) for j in (2, 1)]
-    far, out = lax.optimization_barrier((far, out))
-    out = finish((3,), [far], [piece_a], (1,), gain, out)
+    out = finish((0, 3), [sends[0], far], [piece_a, piece_a], (0, 1), gain)
     return finish((2, 1), near, [piece_b, piece_b], (0, 1), gain, out)
 
 

time: 27.8 us -> 27.9 us (level)
  waiting for transfers between devices: 2.37 us -> 3.25 us
  Pallas kernels: 14.3 us -> 13.5 us
    ppermute x7, waiting for transfers between devices: 2.37 us -> 3.25 us  [swapped(): return lax.ppermute(value, 'ctx', [(s, s ^ bits) for s in range(count)])]
    pallas_call x3 -> x2, Pallas kernels: 3.93 us -> 3.1 us  [finish(): pl.pallas_call(functools.partial(finish_kernel, quarters, places, len(oth...]
  transfers between devices with their start and end apart: 7 -> 7, of which waited for: 5 -> 4; matrix products, arithmetic and copies ran while one was open for 0% -> 0% of each run, Pallas kernels for 28% -> 25%
where the time goes in v12:
time: 27.9 us; the launch traced here: 27.8 us
  Pallas kernels  13.5 us (48%)
  starting transfers between devices  10.9 us (39%)
  waiting for transfers between devices  3.25 us (12%)
    ppermute x7, starting transfers between devices, swapped(): return lax.ppermute(value, 'ctx', [(s, s ^ bits) for s in range(count)])  10.9 us
    pallas_call x1, Pallas kernels, early_states(): pl.pallas_call(functools.partial(early_kernel, quarters), in_specs=[HBM]...  4.14 us
    pallas_call x2, Pallas kernels, inner_attention(): pl.pallas_call(functools.partial(inner_kernel, quarters, slots), in_specs...  4 us
    ppermute x7, waiting for transfers between devices, swapped(): return lax.ppermute(value, 'ctx', [(s, s ^ bits) for s in range(count)])  3.25 us
    pallas_call x2, Pallas kernels, finish(): pl.pallas_call(functools.partial(finish_kernel, quarters, places, len(oth...  3.1 us
    pallas_call x1, Pallas kernels, own_states(): pl.pallas_call(own_kernel, in_specs=[VMEM] * 4, out_specs=[VMEM] * 3, out...  1.2 us
  transfers between devices with their start and end apart: 7, of which 4 were waited for; matrix products, arithmetic and copies ran while one was open for 0% of the time, Pallas kernels for 25%

profile of v12, /device:TPU:0, one launch (start us, length us, event | category | flops | bytes accessed | tf_op | source)
XLA Modules:
  0.0 27.8 jit_solution(2304304436174064554)
XLA Ops:
  0.0 4.1 %early_states.1 = (bf16[6,1024,128]{2,1,0:T(8,128)(2,1)S(1)}, bf16[6,1024,128]{2,1,0:T(8,128)(2,1)S(1)}, bf16[6,160,128]{2,1,0:T(8,128)(2,1)S(1)}, bf16[1,1024,2...) custom-call(bf16[1024,1024]{1,0:T(8,128)(2,1)} %q_hbm.1, ...), custom_call_target="tpu_custom_call" | custom-call | flops 268435456 | bytes 8388608 | tf_op jit(solution)/shard_map/early_states/pallas_call | solution.py:184
  4.2 4.0 %collective-permute-start.2 = (bf16[2,160,128]{2,1,0:T(8,128)(2,1)S(1)}, bf16[2,160,128]{2,1,0:T(8,128)(2,1)S(1)}, u32[]{:S(2)}, u32[]{:S(2)}) collective-permute-start(bf16[2,160,128]{2,1,0:T(8,128)(2,1)S(1)} %get-tuple-element.77), channel_id=1, source_target_pairs={{0,3},{1,2},{2,1},{3,0},{4,7},{5,6},{6,5},{7,4},{8,11},{9,10},{10,... | collective-permute-start | bytes 245768 | tf_op jit(solution)/shard_map/ppermute | solution.py:505
  8.2 0.5 %collective-permute-start.1 = (bf16[2,160,128]{2,1,0:T(8,128)(2,1)S(1)}, bf16[2,160,128]{2,1,0:T(8,128)(2,1)S(1)}, u32[]{:S(2)}, u32[]{:S(2)}) collective-permute-start(bf16[2,160,128]{2,1,0:T(8,128)(2,1)S(1)} %get-tuple-element.78), channel_id=1, source_target_pairs={{0,2},{1,3},{2,0},{3,1},{4,6},{5,7},{6,4},{7,5},{8,10},{9,11},{10,... | collective-permute-start | bytes 245768 | tf_op jit(solution)/shard_map/ppermute | solution.py:505
  8.7 0.2 collective-permute-start
  8.8 1.2 %own_states.1 = (bf16[2,1024,128]{2,1,0:T(8,128)(2,1)S(1)}, bf16[2,1024,128]{2,1,0:T(8,128)(2,1)S(1)}, bf16[2,160,128]{2,1,0:T(8,128)(2,1)S(1)}) custom-call(bf16[1,1024,256]{2,1,0:T(8,128)(2,1)S(1)} %get-tuple-element.41.k_ref, bf16[1,1024,256]{2,1,0:T(8,128)(2,1)S(1)} %get-tuple-element.42.v_ref, bf16[1024,1024]{1,0:T(8,128)(2,1)S(1)} %get-tuple-element.43.q_ref, ...), custom_call_target="tpu_custom_call" | custom-call | flops 67108864 | bytes 2097152 | tf_op jit(solution)/shard_map/own_states/pallas_call | solution.py:215
  10.1 2.0 %inner_attention.2 = (bf16[4,1024,128]{2,1,0:T(8,128)(2,1)S(1)}, f32[4,1024,128]{2,1,0:T(8,128)S(1)}) custom-call(bf16[1024,1024]{1,0:T(8,128)(2,1)S(1)} %get-tuple-element.43.q_ref, f32[3,4,1024]{2,1,0:T(4,128)S(1)} %get-tuple-element.44.w_ref.refs_4_, bf16[2,1024,128]{2,1,0:T(8,128)(2,1)S(1)} %get-tuple-element.47.refs_0_, ...), custom_call_target="tpu_custom_call" | custom-call | flops 536870912 | bytes 6291456 | tf_op jit(solution)/shard_map/inner_attention/pallas_call | solution.py:431
  12.1 0.0 collective-permute-done.2.refs_3_.p3
  12.1 0.7 %collective-permute-done.1.refs_2_.p2 = bf16[2,160,128]{2,1,0:T(8,128)(2,1)S(1)} collective-permute-done((bf16[2,160,128]{2,1,0:T(8,128)(2,1)S(1)}, bf16[2,160,128]{2,1,0:T(8,128)(2,1)S(1)}, u32[]{:S(2)}, u32[]{:S(2)}) %collective-permute-start.1) | collective-permute-done | bytes 81952 | tf_op jit(solution)/shard_map/ppermute | solution.py:505
  12.8 0.3 collective-permute-done.refs_1_.p1
  13.1 0.2 group_total.1
  13.3 0.0 copy-start
  13.3 2.7 %collective-permute-start.3 = (bf16[2,144,128]{2,1,0:T(8,128)(2,1)S(1)}, bf16[2,144,128]{2,1,0:T(8,128)(2,1)S(1)}, u32[]{:S(2)}, u32[]{:S(2)}) collective-permute-start(bf16[2,144,128]{2,1,0:T(8,128)(2,1)S(1)} %group_total.1), channel_id=1, source_target_pairs={{0,4},{1,5},{2,6},{3,7},{4,0},{5,1},{6,2},{7,3},{8,12},{9,13},{10,... | collective-permute-start | bytes 221192 | tf_op jit(solution)/shard_map/ppermute | solution.py:505
  16.0 2.0 %inner_attention.3 = (bf16[4,1024,128]{2,1,0:T(8,128)(2,1)S(1)}, f32[4,1024,128]{2,1,0:T(8,128)S(1)}) custom-call(bf16[1024,1024]{1,0:T(8,128)(2,1)S(1)} %get-tuple-element.43.q_ref, f32[3,4,1024]{2,1,0:T(4,128)S(1)} %get-tuple-element.44.w_ref.refs_4_, bf16[6,1024,128]{2,1,0:T(8,128)(2,1)S(1)} %get-tuple-element.48.refs_1_.refs_0_, ...), custom_call_target="tpu_custom_call" | custom-call | flops 536870912 | bytes 6291456 | tf_op jit(solution)/shard_map/inner_attention/pallas_call | solution.py:431
  18.0 0.3 %member_edges.1 = (bf16[3,2,16,128]{3,2,1,0:T(8,128)(2,1)S(1)}, f32[3,2,16,128]{3,2,1,0:T(8,128)S(1)}, f32[3,2,128,128]{3,2,1,0:T(8,128)S(1)}, f32[3,2,128,128]{3,2,1,0:T(8,128)S(1)}, bf16[2,32,128]{2,1,0:T(8,128)(2,1)S(1)}) custom-call(bf16[2,160,128]{2,1,0:T(8,128)(2,1)S(1)} %get-tuple-element.45.refs_0_.p0, ...), custom_call_target="tpu_custom_call" | custom-call | tf_op jit(solution)/shard_map/member_edges/pallas_call | solution.py:343
  18.3 0.4 %collective-permute-done.3.x_ref = bf16[2,144,128]{2,1,0:T(8,128)(2,1)S(1)} collective-permute-done((bf16[2,144,128]{2,1,0:T(8,128)(2,1)S(1)}, bf16[2,144,128]{2,1,0:T(8,128)(2,1)S(1)}, u32[]{:S(2)}, u32[]{:S(2)}) %collective-permute-start.3) | collective-permute-done | bytes 73760 | tf_op jit(solution)/shard_map/ppermute | solution.py:505
  18.7 0.5 %member_prefixes.1 = (bf16[2,144,128]{2,1,0:T(8,128)(2,1)S(1)}, bf16[2,144,128]{2,1,0:T(8,128)(2,1)S(1)}, bf16[2,144,128]{2,1,0:T(8,128)(2,1)S(1)}, bf16[2,144,128]{2,1,0:T(8,128)(2,1)S(1)}) custom-call(bf16[3,2,16,128]{3,2,1,0:T(8,128)(2,1)S(1)} %get-tuple-element.63.qf_ref, f32[3,2,16,128]{3,2,1,0:T(8,128)S(1)} %get-tuple-element.64.inner_ref, ...), custom_call_target="tpu_custom_call" | custom-call | tf_op jit(solution)/shard_map/member_prefixes/pallas_call | solution.py:387
  19.2 2.0 %collective-permute-start.6 = (bf16[2,144,128]{2,1,0:T(8,128)(2,1)S(1)}, bf16[2,144,128]{2,1,0:T(8,128)(2,1)S(1)}, u32[]{:S(2)}, u32[]{:S(2)}) collective-permute-start(bf16[2,144,128]{2,1,0:T(8,128)(2,1)S(1)} %get-tuple-element.74), channel_id=1, source_target_pairs={{0,3},{1,2},{2,1},{3,0},{4,7},{5,6},{6,5},{7,4},{8,11},{9,10},{10,... | collective-permute-start | bytes 221192 | tf_op jit(solution)/shard_map/ppermute | solution.py:505
  21.2 0.6 %collective-permute-start.4 = (bf16[2,144,128]{2,1,0:T(8,128)(2,1)S(1)}, bf16[2,144,128]{2,1,0:T(8,128)(2,1)S(1)}, u32[]{:S(2)}, u32[]{:S(2)}) collective-permute-start(bf16[2,144,128]{2,1,0:T(8,128)(2,1)S(1)} %get-tuple-element.69), channel_id=1, source_target_pairs={{0,2},{1,3},{2,0},{3,1},{4,6},{5,7},{6,4},{7,5},{8,10},{9,11},{10,... | collective-permute-start | bytes 221192 | tf_op jit(solution)/shard_map/ppermute | solution.py:505
  21.8 1.0 %collective-permute-start.5 = (bf16[2,144,128]{2,1,0:T(8,128)(2,1)S(1)}, bf16[2,144,128]{2,1,0:T(8,128)(2,1)S(1)}, u32[]{:S(2)}, u32[]{:S(2)}) collective-permute-start(bf16[2,144,128]{2,1,0:T(8,128)(2,1)S(1)} %get-tuple-element.70), channel_id=1, source_target_pairs={{0,1},{1,0},{2,3},{3,2},{4,5},{5,4},{6,7},{7,6},{8,9},{9,8},{10,11... | collective-permute-start | bytes 221192 | tf_op jit(solution)/shard_map/ppermute | solution.py:505
  22.8 1.9 %collective-permute-done.6.refs_1_ = bf16[2,144,128]{2,1,0:T(8,128)(2,1)S(1)} collective-permute-done((bf16[2,144,128]{2,1,0:T(8,128)(2,1)S(1)}, bf16[2,144,128]{2,1,0:T(8,128)(2,1)S(1)}, u32[]{:S(2)}, u32[]{:S(2)}) %collective-permute-start.6) | collective-permute-done | bytes 73760 | tf_op jit(solution)/shard_map/ppermute | solution.py:505
  24.6 0.0 copy-done
  24.6 1.6 %finish.2.refs_6_ = bf16[1024,1024]{1,0:T(8,128)(2,1)} custom-call(f32[1,1024]{1,0:T(1,128)S(1)} %bitcast.1, bf16[2,144,128]{2,1,0:T(8,128)(2,1)S(1)} %get-tuple-element.73.refs_0_, bf16[2,144,128]{2,1,0:T(8,128)(2,1)S(1)} %collective-permute-done.6.refs_1_, bf16[4,1024,128]{2,1,0:T(8,128)(2,1)S(1)} %get-tuple-element.75.refs_2_.refs_3_, ...), custom_call_target="tpu_custom_call" | custom-call | flops 134217728 | bytes 4194304 | tf_op jit(solution)/shard_map/finish/pallas_call | solution.py:483
  26.2 0.0 collective-permute-done.4.refs_0_
  26.2 0.0 collective-permute-done.5.refs_1_
  26.2 1.5 %finish.3 = bf16[1024,1024]{1,0:T(8,128)(2,1)} custom-call(f32[1,1024]{1,0:T(1,128)S(1)} %bitcast.2, bf16[2,144,128]{2,1,0:T(8,128)(2,1)S(1)} %collective-permute-done.4.refs_0_, bf16[2,144,128]{2,1,0:T(8,128)(2,1)S(1)} %collective-permute-done.5.refs_1_, ...), custom_call_target="tpu_custom_call", output_to_operand_aliasing={{}: (7, {})} | custom-call | flops 134217728 | bytes 4194304 | tf_op jit(solution)/shard_map/finish/pallas_call | solution.py:483
  (1 shorter events, 0.0 us)
Async XLA Ops:
  4.2 7.9 %collective-permute-start.2 = (bf16[2,160,128]{2,1,0:T(8,128)(2,1)S(1)}, bf16[2,160,128]{2,1,0:T(8,128)(2,1)S(1)}, u32[]{:S(2)}, u32[]{:S(2)}) collective-permute-start(bf16[2,160,128]{2,1,0:T(8,128)(2,1)S(1)} %get-tuple-element.77), channel_id=1, source_target_pairs={{0,3},{1,2},{2,1},{3,0},{4,7},{5,6},{6,5},{7,4},{8,11},{9,10},{10,... | collective-permute-start | bytes 245768 | tf_op jit(solution)/shard_map/ppermute | solution.py:505
  8.2 4.6 %collective-permute-start.1 = (bf16[2,160,128]{2,1,0:T(8,128)(2,1)S(1)}, bf16[2,160,128]{2,1,0:T(8,128)(2,1)S(1)}, u32[]{:S(2)}, u32[]{:S(2)}) collective-permute-start(bf16[2,160,128]{2,1,0:T(8,128)(2,1)S(1)} %get-tuple-element.78), channel_id=1, source_target_pairs={{0,2},{1,3},{2,0},{3,1},{4,6},{5,7},{6,4},{7,5},{8,10},{9,11},{10,... | collective-permute-start | bytes 245768 | tf_op jit(solution)/shard_map/ppermute | solution.py:505
  8.7 4.4 %collective-permute-start = (bf16[2,160,128]{2,1,0:T(8,128)(2,1)S(1)}, bf16[2,160,128]{2,1,0:T(8,128)(2,1)S(1)}, u32[]{:S(2)}, u32[]{:S(2)}) collective-permute-start(bf16[2,160,128]{2,1,0:T(8,128)(2,1)S(1)} %get-tuple-element.79), channel_id=1, source_target_pairs={{0,1},{1,0},{2,3},{3,2},{4,5},{5,4},{6,7},{7,6},{8,9},{9,8},{10,11... | collective-permute-start | bytes 245768 | tf_op jit(solution)/shard_map/ppermute | solution.py:505
  13.3 11.3 %copy-start = (f32[1024]{0:T(1024)S(1)}, f32[1024]{0:T(1024)}, u32[]{:S(2)}) copy-start(f32[1024]{0:T(1024)} %param.9) | copy-start | bytes 12292
  13.3 5.3 %collective-permute-start.3 = (bf16[2,144,128]{2,1,0:T(8,128)(2,1)S(1)}, bf16[2,144,128]{2,1,0:T(8,128)(2,1)S(1)}, u32[]{:S(2)}, u32[]{:S(2)}) collective-permute-start(bf16[2,144,128]{2,1,0:T(8,128)(2,1)S(1)} %group_total.1), channel_id=1, source_target_pairs={{0,4},{1,5},{2,6},{3,7},{4,0},{5,1},{6,2},{7,3},{8,12},{9,13},{10,... | collective-permute-start | bytes 221192 | tf_op jit(solution)/shard_map/ppermute | solution.py:505
  19.2 5.4 %collective-permute-start.6 = (bf16[2,144,128]{2,1,0:T(8,128)(2,1)S(1)}, bf16[2,144,128]{2,1,0:T(8,128)(2,1)S(1)}, u32[]{:S(2)}, u32[]{:S(2)}) collective-permute-start(bf16[2,144,128]{2,1,0:T(8,128)(2,1)S(1)} %get-tuple-element.74), channel_id=1, source_target_pairs={{0,3},{1,2},{2,1},{3,0},{4,7},{5,6},{6,5},{7,4},{8,11},{9,10},{10,... | collective-permute-start | bytes 221192 | tf_op jit(solution)/shard_map/ppermute | solution.py:505
  21.2 5.0 %collective-permute-start.4 = (bf16[2,144,128]{2,1,0:T(8,128)(2,1)S(1)}, bf16[2,144,128]{2,1,0:T(8,128)(2,1)S(1)}, u32[]{:S(2)}, u32[]{:S(2)}) collective-permute-start(bf16[2,144,128]{2,1,0:T(8,128)(2,1)S(1)} %get-tuple-element.69), channel_id=1, source_target_pairs={{0,2},{1,3},{2,0},{3,1},{4,6},{5,7},{6,4},{7,5},{8,10},{9,11},{10,... | collective-permute-start | bytes 221192 | tf_op jit(solution)/shard_map/ppermute | solution.py:505
  21.8 4.4 %collective-permute-start.5 = (bf16[2,144,128]{2,1,0:T(8,128)(2,1)S(1)}, bf16[2,144,128]{2,1,0:T(8,128)(2,1)S(1)}, u32[]{:S(2)}, u32[]{:S(2)}) collective-permute-start(bf16[2,144,128]{2,1,0:T(8,128)(2,1)S(1)} %get-tuple-element.70), channel_id=1, source_target_pairs={{0,1},{1,0},{2,3},{3,2},{4,5},{5,4},{6,7},{7,6},{8,9},{9,8},{10,11... | collective-permute-start | bytes 221192 | tf_op jit(solution)/shard_map/ppermute | solution.py:505
